TPU v7x, 32 devices: a whole 2x2x4 slice. The times are simulated.
32 devices in a mesh: clip: 4 (over z), seq: 8 (over y, x, core).
Axes of the slice: x: 2, y: 2, z: 4, core: 2. Of those that a mesh axis runs over, the one named last changes fastest.
Arguments:
- patches: bfloat16 [4, 1568, 1024], P('clip', 'seq'), may hold values from -6 to 12
- segment: int32 [4, 1568], P('clip', 'seq'), may hold values from 0 to 191, as said below
- dest_shard: int32 [4, 1536], P('clip', 'seq'), may hold values from -1 to 7, as said below
- dest_slot: int32 [4, 1536], P('clip', 'seq'), may hold values from -1 to 63, as said below
- w_qkv: bfloat16 [1024, 1536], replicated, may hold values from -1 to 4
- out_grad: bfloat16 [4, 512, 512], P('clip', 'seq'), may hold values from -6 to 6
Outputs:
- attended: bfloat16 [4, 512, 512], P('clip', 'seq')
- patch_grad: bfloat16 [4, 1568, 1024], P('clip', 'seq')
- weight_grad: float32 [1024, 1536], P('seq', 'clip')
Inputs may be any that keep to these rules, and one draw needn't show every extreme that they name: `segment`: within each block of 196 patches the ids start at 0, never fall and skip no value; every id names one or more patches. The number of tokens of a block is one more than its largest id. `dest_shard`: -1 exactly on the rows of a block past its number of tokens. A block of 192 rows sends at most 24 rows to each receiving block of its clip, and every receiving block gets exactly 64 rows. `dest_slot`: -1 exactly where dest_shard is -1; the rows sent to one receiving block take its rows 0 to 63 once each.
All inputs are finite; a program needn't handle non-finite values.
Results may differ from a plain program's by a relative error of at most 0.024.
Values may be sent and summed in bfloat16 or wider, within the bound.
No kernel may reach another device: no remote copies, remote signals or barrier semaphores. Data moves between devices by JAX's collectives and lax.ppermute only.
A program may use at most 64 MiB of HBM per device.

v0:
```python
import jax
import jax.numpy as jnp
from jax import lax
from jax.sharding import PartitionSpec as P

HEADS = 8
HEAD_DIM = 64


neg_large = -1e30


def split_heads(rows_in):
    return rows_in.reshape(rows_in.shape[0], HEADS, HEAD_DIM)


def forward_fold(query_heads, running, pieces):
    scaling = HEAD_DIM ** (-0.5)
    row_max, row_total, weighted = running
    key_heads = split_heads(pieces[0])
    value_heads = split_heads(pieces[1])
    scores = (
        jnp.einsum("rhd,khd->hrk", query_heads, key_heads, preferred_element_type=jnp.float32)
        * scaling
    )
    new_max = jnp.maximum(row_max, jnp.max(scores, axis=2))
    weights = jnp.exp(scores - new_max[:, :, None])
    row_total = jnp.sum(weights, axis=2)
    weighted = jnp.einsum(
        "hrk,khd->hrd",
        weights.astype(jnp.bfloat16),
        value_heads,
        preferred_element_type=jnp.float32,
    )
    return (new_max, row_total, weighted)


def query_fold(query_heads, grad_heads, log_total, grad_dot):
    scaling = HEAD_DIM ** (-0.5)

    def combine_piece(running, pieces, offset):
        key_heads = split_heads(pieces[0])
        value_heads = split_heads(pieces[1])
        scores = (
            jnp.einsum("rhd,khd->hrk", query_heads, key_heads, preferred_element_type=jnp.float32)
            * scaling
        )
        probability = jnp.exp(scores - log_total[:, :, None])
        prob_grad = jnp.einsum(
            "rhd,khd->hrk", grad_heads, value_heads, preferred_element_type=jnp.float32
        )
        score_grad = (probability * (prob_grad - grad_dot[:, :, None])).astype(jnp.bfloat16)
        return (
            jnp.einsum("hrk,khd->hrd", score_grad, key_heads, preferred_element_type=jnp.float32)
            * scaling
        )

    return combine_piece


def key_fold(key_heads, value_heads, all_log, all_dot, pieces):
    scaling = HEAD_DIM ** (-0.5)
    piece_query = split_heads(pieces[0])
    piece_grad = split_heads(pieces[1])
    piece_log = all_log.T
    piece_dot = all_dot.T
    scores = (
        jnp.einsum("qhd,khd->hqk", piece_query, key_heads, preferred_element_type=jnp.float32)
        * scaling
    )
    probability = jnp.exp(scores - piece_log[:, :, None])
    value_grad = jnp.einsum(
        "hqk,qhd->hkd",
        probability.astype(jnp.bfloat16),
        piece_grad,
        preferred_element_type=jnp.float32,
    )
    prob_grad = jnp.einsum(
        "qhd,khd->hqk", piece_grad, value_heads, preferred_element_type=jnp.float32
    )
    score_grad = (probability * (prob_grad - piece_dot[:, :, None])).astype(jnp.bfloat16)
    key_grad = (
        jnp.einsum("hqk,qhd->hkd", score_grad, piece_query, preferred_element_type=jnp.float32)
        * scaling
    )
    return (key_grad, value_grad)


def head_rows(matrix):
    return matrix.transpose(1, 0, 2).reshape(matrix.shape[1], HEADS * HEAD_DIM)


def local(patches, segment, dest_shard, dest_slot, w_qkv, out_grad):
    shard_count = lax.axis_size("seq")
    patch_rows = patches[0]
    patch_token = segment[0]
    targets = dest_shard[0]
    slot_ids = dest_slot[0]
    token_cap = targets.shape[0]
    pair_cap = token_cap // shard_count
    local_rows = out_grad.shape[1]
    inner_width = HEADS * HEAD_DIM
    member = (
        lax.broadcasted_iota(jnp.int32, (token_cap, patch_token.shape[0]), 0)
        == patch_token[None, :]
    )
    member_half = member.astype(jnp.bfloat16)
    counts = jnp.sum(member.astype(jnp.float32), axis=1)
    token_sums = jnp.dot(member_half, patch_rows, preferred_element_type=jnp.float32)
    tokens = (token_sums / jnp.maximum(counts, 1.0)[:, None]).astype(jnp.bfloat16)
    to_shard = (
        targets[:, None] == lax.broadcasted_iota(jnp.int32, (token_cap, shard_count), 1)
    ).astype(jnp.int32)
    ranking = jnp.sum((jnp.cumsum(to_shard, axis=0) - 1) * to_shard, axis=1)
    position = jnp.where(targets >= 0, targets * pair_cap + ranking, -1)
    chooser = position[None, :] == lax.broadcasted_iota(
        jnp.int32, (shard_count * pair_cap, token_cap), 0
    )
    chooser_half = chooser.astype(jnp.bfloat16)
    send_rows = jnp.dot(chooser_half, tokens, preferred_element_type=jnp.float32).astype(
        jnp.bfloat16
    )
    send_slot = jnp.sum(chooser.astype(jnp.int32) * (slot_ids + 1)[None, :], axis=1) - 1
    came_rows, came_slot = (
        lax.all_to_all(
            send_rows.reshape(shard_count, pair_cap, -1),
            "seq",
            split_axis=0,
            concat_axis=0,
            tiled=True,
        ),
        lax.all_to_all(
            send_slot.reshape(shard_count, pair_cap), "seq", split_axis=0, concat_axis=0, tiled=True
        ),
    )
    came_slot = came_slot.reshape(-1)
    placer = (
        came_slot[None, :]
        == lax.broadcasted_iota(jnp.int32, (local_rows, shard_count * pair_cap), 0)
    ).astype(jnp.bfloat16)
    placed = jnp.dot(
        placer, came_rows.reshape(shard_count * pair_cap, -1), preferred_element_type=jnp.float32
    ).astype(jnp.bfloat16)
    projected = jnp.dot(placed, w_qkv, preferred_element_type=jnp.float32).astype(jnp.bfloat16)
    query_rows = projected[:, :inner_width]
    key_rows = projected[:, inner_width : 2 * inner_width]
    value_rows = projected[:, 2 * inner_width :]
    query_heads = split_heads(query_rows)
    initial = (
        jnp.full((HEADS, local_rows), neg_large, jnp.float32),
        jnp.zeros((HEADS, local_rows), jnp.float32),
        jnp.zeros((HEADS, local_rows, HEAD_DIM), jnp.float32),
    )
    row_max, row_total, weighted = forward_fold(
        query_heads,
        initial,
        (
            lax.all_gather(key_rows, "seq", axis=0, tiled=True),
            lax.all_gather(value_rows, "seq", axis=0, tiled=True),
        ),
    )
    attended_rows = head_rows((weighted / row_total[:, :, None]).astype(jnp.bfloat16))
    grad_rows = out_grad[0]
    grad_heads = split_heads(grad_rows)
    log_total = row_max + jnp.log(row_total)
    grad_dot = jnp.sum(
        grad_heads.astype(jnp.float32) * split_heads(attended_rows).astype(jnp.float32), axis=2
    )
    blank = jnp.zeros((HEADS, local_rows, HEAD_DIM), jnp.float32)
    query_step = query_fold(query_heads, grad_heads, log_total, grad_dot.T)
    query_grad = query_step(
        blank,
        (
            lax.all_gather(key_rows, "seq", axis=0, tiled=True),
            lax.all_gather(value_rows, "seq", axis=0, tiled=True),
        ),
        jnp.int32(0),
    )
    all_log, all_dot = (
        lax.all_gather(log_total.T, "seq", axis=0, tiled=True),
        lax.all_gather(grad_dot, "seq", axis=0, tiled=True),
    )
    key_grad, value_grad = key_fold(
        split_heads(key_rows),
        split_heads(value_rows),
        all_log,
        all_dot,
        (
            lax.all_gather(query_rows, "seq", axis=0, tiled=True),
            lax.all_gather(grad_rows, "seq", axis=0, tiled=True),
        ),
    )
    proj_grad = jnp.concatenate(
        [head_rows(query_grad), head_rows(key_grad), head_rows(value_grad)], axis=1
    ).astype(jnp.bfloat16)
    placed_grad = jnp.einsum(
        "rc,dc->rd", proj_grad, w_qkv, preferred_element_type=jnp.float32
    ).astype(jnp.bfloat16)
    partial_value = jnp.einsum(
        "rd,rc->dc", placed, proj_grad, preferred_element_type=jnp.float32
    ).astype(jnp.bfloat16)
    across = lax.psum_scatter(partial_value, "seq", scatter_dimension=0, tiled=True).astype(
        jnp.float32
    )
    weight_grad = lax.psum_scatter(
        across.astype(jnp.bfloat16), "clip", scatter_dimension=1, tiled=True
    ).astype(jnp.float32)
    back_rows = jnp.einsum(
        "rj,rd->jd", placer, placed_grad, preferred_element_type=jnp.float32
    ).astype(jnp.bfloat16)
    returned = lax.all_to_all(
        back_rows.reshape(shard_count, pair_cap, -1), "seq", split_axis=0, concat_axis=0, tiled=True
    )
    token_grad = jnp.einsum(
        "jt,jd->td",
        chooser_half,
        returned.reshape(shard_count * pair_cap, -1),
        preferred_element_type=jnp.float32,
    ).astype(jnp.bfloat16)
    patch_sums = jnp.einsum(
        "tp,td->pd", member_half, token_grad, preferred_element_type=jnp.float32
    )
    patch_count = jnp.sum(member.astype(jnp.float32) * counts[:, None], axis=0)
    patch_grad = (patch_sums / patch_count[:, None]).astype(jnp.bfloat16)
    return (attended_rows[None], patch_grad[None], weight_grad)


def solution(mesh):
    return jax.shard_map(
        local,
        mesh=mesh,
        in_specs=(
            P("clip", "seq", None),
            P("clip", "seq"),
            P("clip", "seq"),
            P("clip", "seq"),
            P(),
            P("clip", "seq", None),
        ),
        out_specs=(P("clip", "seq", None), P("clip", "seq", None), P("seq", "clip")),
        check_vma=False,
    )
```

profile of v0, /device:TPU:0, one launch (start us, length us, event | category | flops | bytes accessed | tf_op | source)
XLA Modules:
  0.0 202.9 jit_solution(1302589991160825272)
XLA Ops:
  11.9 5.2 %all-to-all-start = ((s32[8,1,24]{2,1,0:T(1,128)}), s32[8,1,24]{2,1,0:T(1,128)S(1)}, u32[]{:S(2)}, u32[]{:S(2)}) async-start(s32[8,1,24]{2,1,0:T(1,128)} %sub.57), calls=%async_computation | async-start | bytes 8192 | tf_op jit(solution)/shard_map/all_to_all | solution.py:132
  18.5 2.2 %convolution_convert_fusion.4 = bf16[192,1024]{1,0:T(8,128)(2,1)} fusion(bf16[1,196,1024]{2,1,0:T(8,128)(2,1)} %param.6, f32[192]{0:T(256)S(1)} %broadcast_maximum_fusion.1, s32[196]{0:T(256)} %bitcast.130, s32[192]{0:T(256)S(1)} %bitcast.126), kind=kOutput, calls=%fused_computation.20 | convolution fusion | flops 153232128 | bytes 796944 | tf_op jit(solution)/shard_map/dot_general | solution.py:120
  21.7 3.5 %all-to-all-start.1 = ((bf16[8,24,1024]{2,1,0:T(8,128)(2,1)}), bf16[8,24,1024]{2,1,0:T(8,128)(2,1)S(1)}, u32[]{:S(2)}, u32[]{:S(2)}) async-start(bf16[8,24,1024]{2,1,0:T(8,128)(2,1)} %bitcast.112), calls=%async_computation.1 | async-start | bytes 786432 | tf_op jit(solution)/shard_map/all_to_all | solution.py:125
  25.2 1.6 copy.48
  26.8 12.1 %all-gather = bf16[1,512,512]{2,1,0:T(8,128)(2,1)} all-gather(bf16[1,64,512]{2,1,0:T(8,128)(2,1)} %param.11), channel_id=2, replica_groups=mesh['clip'=4,'seq'=8] {'seq'}, dimensions={1}, use_global_device_ids=true | all-gather | bytes 589824 | tf_op jit(solution)/shard_map/all_gather | solution.py:190
  38.9 2.1 %copy.54 = bf16[1,512,512]{1,2,0:T(8,128)(2,1)} copy(bf16[1,512,512]{2,1,0:T(8,128)(2,1)} %all-gather) | data formatting | bytes 1048576 | tf_op jit(solution)/shard_map/all_gather | solution.py:190
  44.5 10.3 %all_gather.20 = bf16[512,512]{1,0:T(8,128)(2,1)} all-gather(bf16[64,512]{1,0:T(8,128)(2,1)S(1)} %get-tuple-element.17), channel_id=1, replica_groups=mesh['clip'=4,'seq'=8] {'seq'}, dimensions={0}, use_global_device_ids=true | all-gather | bytes 589824 | tf_op jit(solution)/shard_map/all_gather | solution.py:158
  55.7 10.3 %all_gather.21 = bf16[512,512]{1,0:T(8,128)(2,1)} all-gather(bf16[64,512]{1,0:T(8,128)(2,1)S(1)} %get-tuple-element.16), channel_id=1, replica_groups=mesh['clip'=4,'seq'=8] {'seq'}, dimensions={0}, use_global_device_ids=true | all-gather | bytes 589824 | tf_op jit(solution)/shard_map/all_gather | solution.py:159
  66.1 10.4 %all_gather.22 = bf16[512,512]{1,0:T(8,128)(2,1)} all-gather(bf16[64,512]{1,0:T(8,128)(2,1)S(1)} %get-tuple-element.15), channel_id=1, replica_groups=mesh['clip'=4,'seq'=8] {'seq'}, dimensions={0}, use_global_device_ids=true | all-gather | bytes 589824 | tf_op jit(solution)/shard_map/all_gather | solution.py:189
  76.5 2.1 %copy.45 = bf16[512,512]{0,1:T(8,128)(2,1)} copy(bf16[512,512]{1,0:T(8,128)(2,1)} %all_gather.20) | data formatting | bytes 1048576 | tf_op jit(solution)/shard_map/all_gather | solution.py:158
  78.5 1.4 fusion.51
  81.3 2.0 %copy.47 = bf16[512,512]{0,1:T(8,128)(2,1)} copy(bf16[512,512]{1,0:T(8,128)(2,1)} %all_gather.21) | data formatting | bytes 1048576 | tf_op jit(solution)/shard_map/all_gather | solution.py:159
  83.4 2.1 %copy.51 = bf16[512,512]{0,1:T(8,128)(2,1)} copy(bf16[512,512]{1,0:T(8,128)(2,1)} %all_gather.22) | data formatting | bytes 1048576 | tf_op jit(solution)/shard_map/all_gather | solution.py:189
  85.4 8.5 %all-gather.1 = f32[8,64,8]{1,2,0:T(8,128)S(1)} all-gather(f32[1,64,8]{1,2,0:T(8,128)S(1)} %fusion.49), channel_id=1, replica_groups=mesh['clip'=4,'seq'=8] {'seq'}, dimensions={0}, use_global_device_ids=true | all-gather | bytes 18432 | tf_op jit(solution)/shard_map/all_gather | solution.py:180
  94.1 2.4 %multiply_reduce_fusion = (f32[64,8]{0,1:T(8,128)S(1)}, bf16[64,8,64]{0,2,1:T(8,128)(2,1)}) fusion(bf16[64,8,64]{0,2,1:T(8,128)(2,1)S(1)} %bitcast.115, f32[64,8]{0,1:T(8,128)S(1)} %bitcast.120, bf16[512,8,64]{0,2,1:T(8,128)(2,1)} %bitcast.110, f32[8,64,512]{2,1,0:T(8,128)} %copy-done.2, f32[8,64]{1,0:T(8,128)S(1)} %broadcast_maximum_fusion), kind=kOutput, calls=%fused_computation.49 | convolution fusion | flops 34274816 | bytes 1710080 | tf_op jit(solution)/shard_map/hrk,khd->hrd/dot_general | solution.py:29
  96.4 2.7 %fusion.20 = bf16[64,8,64]{2,0,1:T(8,128)(2,1)} fusion(bf16[512,8,64]{0,2,1:T(8,128)(2,1)} %bitcast.107, bf16[512,8,64]{0,2,1:T(8,128)(2,1)} %bitcast.111, bf16[64,8,64]{0,2,1:T(8,128)(2,1)S(1)} %bitcast.116, f32[8,64,512]{2,1,0:T(8,128)} %copy-done.2, f32[8,64]{1,0:T(8,128)S(1)} %bitcast.123, f32[8,64]{1,0:T(8,128)S(1)} %log_add_fusion), kind=kOutput, calls=%fused_computation.35 | convolution fusion | flops 68222976 | bytes 2232320 | tf_op jit(solution)/shard_map/hrk,khd->hrd/dot_general | solution.py:54
  100.3 8.6 %all-gather.2 = f32[8,64,8]{1,2,0:T(8,128)S(1)} all-gather(f32[1,64,8]{1,2,0:T(8,128)S(1)} %bitcast.124), channel_id=1, replica_groups=mesh['clip'=4,'seq'=8] {'seq'}, dimensions={0}, use_global_device_ids=true | all-gather | bytes 18432 | tf_op jit(solution)/shard_map/all_gather | solution.py:181
  109.6 1.4 fusion.1
  112.0 1.3 fusion.19
  114.1 1.1 reshape.115
  115.2 2.6 %fusion.21 = bf16[64,8,64]{2,0,1:T(8,128)(2,1)} fusion(bf16[512,8,64]{0,2,1:T(8,128)(2,1)} %bitcast.105, f32[8,512,64]{1,2,0:T(8,128)} %copy-done.1, bf16[512,8,64]{0,2,1:T(8,128)(2,1)} %bitcast.103, f32[8,512]{1,0:T(8,128)} %bitcast.119, bf16[64,8,64]{2,1,0:T(8,128)(2,1)} %reshape.112), kind=kOutput, calls=%fused_computation.36 | convolution fusion | flops 67960832 | bytes 2244608 | tf_op jit(solution)/shard_map/hqk,qhd->hkd/dot_general | solution.py:83
  117.8 1.6 copy.57
  119.5 1.7 reshape.114
  122.0 2.7 %convolution_convert_fusion = bf16[1024,1536]{1,0:T(8,128)(2,1)} fusion(bf16[64,1024]{1,0:T(8,128)(2,1)S(1)} %copy-done.4, bf16[64,1536]{1,0:T(8,128)(2,1)S(1)} %constant_dynamic-update-slice_fusion), kind=kOutput, calls=%fused_computation | convolution fusion | flops 202899456 | bytes 3473408 | tf_op jit(solution)/shard_map/rd,rc->dc/dot_general | solution.py:199
  124.8 46.6 %reduce-scatter.5.cloned.1.call-done = bf16[128,1536]{1,0:T(8,128)(2,1)} async-done(((bf16[1024,1536]{1,0:T(8,128)(2,1)}), bf16[128,1536]{1,0:T(8,128)(2,1)}) %reduce-scatter.5.cloned.1.call-update) | async-done | bytes 393232 | tf_op jit(solution)/shard_map/reduce_scatter | solution.py:202
  171.3 1.9 copy.61
  173.3 2.0 convolution_convert_fusion.3
  175.3 3.5 %all-to-all-start.2 = ((bf16[8,24,1024]{2,1,0:T(8,128)(2,1)}), bf16[8,24,1024]{2,1,0:T(8,128)(2,1)S(1)}, u32[]{:S(2)}, u32[]{:S(2)}) async-start(bf16[8,24,1024]{2,1,0:T(8,128)(2,1)} %bitcast.30), calls=%async_computation.2 | async-start | bytes 786432 | tf_op jit(solution)/shard_map/all_to_all | solution.py:211
  178.9 1.6 copy.59
  180.5 6.5 %all-to-all-done.2 = bf16[8,24,1024]{2,1,0:T(8,128)(2,1)S(1)} async-done(((bf16[8,24,1024]{2,1,0:T(8,128)(2,1)}), bf16[8,24,1024]{2,1,0:T(8,128)(2,1)S(1)}, u32[]{:S(2)}, u32[]{:S(2)}) %all-to-all-start.2) | async-done | bytes 393248 | tf_op jit(solution)/shard_map/all_to_all | solution.py:211
  187.0 1.3 fusion.12
  188.3 6.1 %reduce-scatter.7.cloned.1.call-done = bf16[384,128]{1,0:T(8,128)(2,1)} async-done(((bf16[1536,128]{1,0:T(8,128)(2,1)}), bf16[384,128]{1,0:T(8,128)(2,1)}) %reduce-scatter.7.cloned.1.call-update) | async-done | bytes 98320
  (73 shorter events, 19.3 us)
Async XLA Ops:
  7.2 35.9 %copy-start = (bf16[1024,1536]{1,0:T(8,128)(2,1)S(1)}, bf16[1024,1536]{1,0:T(8,128)(2,1)}, u32[]{:S(2)}) copy-start(bf16[1024,1536]{1,0:T(8,128)(2,1)} %param.10) | copy-start | bytes 9437188
  11.1 10.6 %copy-start.10 = (s32[1,192]{1,0:T(1,128)}, s32[1,192]{1,0:T(1,128)S(1)}, u32[]{:S(2)}) copy-start(s32[1,192]{1,0:T(1,128)S(1)} %compare_select_fusion) | copy-start | bytes 2308
  11.9 9.8 %all-to-all-start = ((s32[8,1,24]{2,1,0:T(1,128)}), s32[8,1,24]{2,1,0:T(1,128)S(1)}, u32[]{:S(2)}, u32[]{:S(2)}) async-start(s32[8,1,24]{2,1,0:T(1,128)} %sub.57), calls=%async_computation | async-start | bytes 8192 | tf_op jit(solution)/shard_map/all_to_all | solution.py:132
  17.9 0.6 copy-start.6
  21.7 20.5 %all-to-all-start.1 = ((bf16[8,24,1024]{2,1,0:T(8,128)(2,1)}), bf16[8,24,1024]{2,1,0:T(8,128)(2,1)S(1)}, u32[]{:S(2)}, u32[]{:S(2)}) async-start(bf16[8,24,1024]{2,1,0:T(8,128)(2,1)} %bitcast.112), calls=%async_computation.1 | async-start | bytes 786432 | tf_op jit(solution)/shard_map/all_to_all | solution.py:125
  25.2 146.2 %reduce-scatter.5.cloned.1.call-start = ((), (), s32[]{:S(2)}) async-start(), calls=%async_computation.5 | async-start | bytes 3538944 | tf_op jit(solution)/shard_map/reduce_scatter | solution.py:202
  42.2 34.2 %copy-start.8 = (s32[192]{0:T(256)}, s32[192]{0:T(256)S(1)}, u32[]{:S(2)}) copy-start(s32[192]{0:T(256)S(1)} %eq.53) | copy-start | bytes 2308
  42.4 0.6 copy-start.3
  76.5 17.6 %copy-start.5 = (bf16[1,64,512]{1,2,0:T(8,128)(2,1)S(1)}, bf16[1,64,512]{1,2,0:T(8,128)(2,1)}, u32[]{:S(2)}) copy-start(bf16[1,64,512]{1,2,0:T(8,128)(2,1)} %copy.48) | copy-start | bytes 196612
  79.9 1.0 copy-start.2
  109.6 12.4 %copy-start.4 = (bf16[64,1024]{1,0:T(8,128)(2,1)S(1)}, bf16[64,1024]{1,0:T(8,128)(2,1)}, u32[]{:S(2)}) copy-start(bf16[64,1024]{1,0:T(8,128)(2,1)} %copy-done.3) | copy-start | bytes 393220
  111.1 1.0 copy-start.1
  122.0 51.3 %copy-start.9 = (s32[192]{0:T(256)S(1)}, s32[192]{0:T(256)}, u32[]{:S(2)}) copy-start(s32[192]{0:T(256)} %copy-done.8) | copy-start | bytes 2308
  124.7 54.0 %copy-start.7 = (f32[192]{0:T(256)S(1)}, f32[192]{0:T(256)}, u32[]{:S(2)}) copy-start(f32[192]{0:T(256)} %copy-done.6) | copy-start | bytes 2308
  124.7 54.0 %copy-start.12 = (s32[1,196]{1,0:T(1,128)S(1)}, s32[1,196]{1,0:T(1,128)}, u32[]{:S(2)}) copy-start(s32[1,196]{1,0:T(1,128)} %param.7) | copy-start | bytes 2356
  124.7 62.3 %copy-start.11 = (s32[1,192]{1,0:T(1,128)S(1)}, s32[1,192]{1,0:T(1,128)}, u32[]{:S(2)}) copy-start(s32[1,192]{1,0:T(1,128)} %copy-done.10) | copy-start | bytes 2308
  124.7 69.6 %reduce-scatter.7.cloned.1.call-start = ((), (), s32[]{:S(2)}) async-start(), calls=%async_computation.6 | async-start | bytes 491520
  175.3 11.7 %all-to-all-start.2 = ((bf16[8,24,1024]{2,1,0:T(8,128)(2,1)}), bf16[8,24,1024]{2,1,0:T(8,128)(2,1)S(1)}, u32[]{:S(2)}, u32[]{:S(2)}) async-start(bf16[8,24,1024]{2,1,0:T(8,128)(2,1)} %bitcast.30), calls=%async_computation.2 | async-start | bytes 786432 | tf_op jit(solution)/shard_map/all_to_all | solution.py:211
Sparse Core Ops, SparseCore 0:
  124.8 46.4 reduce-scatter.4
  173.7 20.5 reduce-scatter.6
where the time goes:
time: 204 us; the launch traced here: 203 us
  waiting for transfers between devices  60.2 us (30%)
  blocking collectives  60.2 us (30%)
  local copies, waits for them, and re-layouts  28.7 us (14%)
  matrix products  20.9 us (10%)
  between operations  14.3 us (7%)
  starting transfers between devices  12.2 us (6%)
  other arithmetic  6.48 us (3%)
    reduce_scatter x1, waiting for transfers between devices, local(): lax.psum_scatter(partial_value, 'seq', scatter_dimension=0, tiled=True)  46.6 us
    all_gather x1, blocking collectives, local(): lax.all_gather(grad_rows, 'seq', axis=0, tiled=True)  12.1 us
    unnamed x34, local copies, waits for them, and re-layouts  11 us
    all_gather x1, blocking collectives, local(): lax.all_gather(query_rows, 'seq', axis=0, tiled=True)  10.4 us
    all_gather x1, blocking collectives, local(): lax.all_gather(key_rows, 'seq', axis=0, tiled=True)  10.3 us
    all_gather x1, blocking collectives, local(): lax.all_gather(value_rows, 'seq', axis=0, tiled=True)  10.3 us
    all_gather x1, blocking collectives, local(): lax.all_gather(grad_dot, 'seq', axis=0, tiled=True)  8.6 us
    all_gather x1, blocking collectives, local(): lax.all_gather(log_total.T, 'seq', axis=0, tiled=True)  8.54 us
  transfers between devices with their start and end apart: 5, of which 4 were waited for; matrix products, arithmetic and copies ran while one was open for 6% of the time, Pallas kernels for 0%

commit v1 on v0

--- a/solution.py
+++ b/solution.py
@@ -1,6 +1,8 @@
 import jax
 import jax.numpy as jnp
 from jax import lax
+from jax.experimental import pallas as pl
+from jax.experimental.pallas import tpu as pltpu
 from jax.sharding import PartitionSpec as P
 
 HEADS = 8
@@ -90,7 +92,7 @@
     return matrix.transpose(1, 0, 2).reshape(matrix.shape[1], HEADS * HEAD_DIM)
 
 
-def local(patches, segment, dest_shard, dest_slot, w_qkv, out_grad):
+def rows_plan(patches, segment, dest_shard, dest_slot, w_qkv, out_grad):
     shard_count = lax.axis_size("seq")
     patch_rows = patches[0]
     patch_token = segment[0]
@@ -225,9 +227,288 @@
     return (attended_rows[None], patch_grad[None], weight_grad)
 
 
+VMEM_LIMIT = 40 * 1024 * 1024
+NN = (((1,), (0,)), ((), ()))
+NT = (((1,), (1,)), ((), ()))
+TN = (((0,), (0,)), ((), ()))
+
+
+def dot(left, right, dims=NN):
+    return lax.dot_general(left, right, dims, preferred_element_type=jnp.float32)
+
+
+def call(body, outs, *args, scratch=()):
+    return pl.pallas_call(
+        body,
+        out_shape=outs,
+        scratch_shapes=scratch,
+        compiler_params=pltpu.CompilerParams(vmem_limit_bytes=VMEM_LIMIT),
+    )(*args)
+
+
+def one_hot(condition):
+    return jnp.where(condition, 1.0, 0.0).astype(jnp.bfloat16)
+
+
+def fold_half(rows):
+    half = rows.shape[0] // 2
+    return jnp.concatenate([rows[:half], rows[half:]], axis=1)
+
+
+def unfold_half(rows):
+    width = rows.shape[1] // 2
+    return jnp.concatenate([rows[:, :width], rows[:, width:]], axis=0)
+
+
+def wide_row(row):
+    short = 256 - row.shape[1]
+    wide = row.astype(jnp.float32)
+    wide = jnp.concatenate([wide, jnp.full((1, short), -1.0, jnp.float32)], axis=1)
+    return wide[:, :128], wide[:, 128:]
+
+
+def token_kernel(patch_ref, segment_ref, shard_ref, slot_ref, w_ref, grad_ref, send_ref, block_ref):
+    token_cap = shard_ref.shape[1]
+    local_rows, inner = grad_ref.shape
+    devices = send_ref.shape[0]
+    width = block_ref.shape[2]
+    member = (
+        lax.broadcasted_iota(jnp.int32, (token_cap, segment_ref.shape[1]), 0) == segment_ref[...]
+    )
+    counts = jnp.sum(jnp.where(member, 1.0, 0.0), axis=1, keepdims=True)
+    token_sums = dot(one_hot(member), patch_ref[...])
+    tokens = (token_sums / jnp.maximum(counts, 1.0)).astype(jnp.bfloat16)
+    for place in range(devices):
+        block_ref[place] = tokens[:, place * width : (place + 1) * width]
+    projected = dot(tokens, w_ref[...]).astype(jnp.bfloat16)
+    shard_low, shard_high = wide_row(shard_ref[...])
+    slot_low, slot_high = wide_row(slot_ref[...])
+    line = lax.broadcasted_iota(jnp.int32, (16, 128), 0)
+    where_to = jnp.where(
+        line == 0,
+        shard_low,
+        jnp.where(line == 1, shard_high, jnp.where(line == 2, slot_low, slot_high)),
+    ).astype(jnp.bfloat16)
+    grads = grad_ref[...]
+    for head in range(devices):
+        first = head * HEAD_DIM
+        query, key, value = (
+            projected[:, part * inner + first : part * inner + first + HEAD_DIM]
+            for part in range(3)
+        )
+        start = 0
+        for piece in (
+            jnp.concatenate([query, key], axis=1),
+            fold_half(value),
+            where_to,
+            fold_half(grads[:, first : first + HEAD_DIM]),
+        ):
+            send_ref[head, start : start + piece.shape[0]] = piece
+            start += piece.shape[0]
+
+
+def target_row(lines, token_cap, local_rows):
+    lines = lines.astype(jnp.float32)
+    shard = jnp.concatenate([lines[0:1], lines[1:2]], axis=1)[:, :token_cap]
+    slot = jnp.concatenate([lines[2:3], lines[3:4]], axis=1)[:, :token_cap]
+    return (shard * local_rows + slot).astype(jnp.int32)
+
+
+def head_kernel(token_cap, came_ref, attended_ref, proj_ref, target_ref):
+    devices, local_rows = came_ref.shape[0], 2 * attended_ref.shape[1]
+    rows = devices * local_rows
+    scaling = HEAD_DIM ** (-0.5)
+    half_cap = token_cap // 2
+    lines_at = token_cap + half_cap
+    row_id = lax.broadcasted_iota(jnp.int32, (rows, token_cap), 0)
+    total = jnp.zeros((rows, 3 * HEAD_DIM), jnp.float32)
+    grads = []
+    for sender in range(devices):
+        target = target_row(came_ref[sender, lines_at : lines_at + 16], token_cap, local_rows)
+        target_ref[sender : sender + 1, :] = target
+        placer = one_hot(row_id == target)
+        rows_in = jnp.concatenate(
+            [
+                came_ref[sender, :token_cap],
+                unfold_half(came_ref[sender, token_cap:lines_at]),
+            ],
+            axis=1,
+        )
+        total = total + dot(placer, rows_in)
+        grads.append(unfold_half(came_ref[sender, lines_at + 16 :]))
+    projected = total.astype(jnp.bfloat16)
+    query = projected[:, :HEAD_DIM]
+    key = projected[:, HEAD_DIM : 2 * HEAD_DIM]
+    value = projected[:, 2 * HEAD_DIM :]
+    grad = jnp.concatenate(grads, axis=0)
+    scores = dot(key, query, NT) * scaling
+    weights = jnp.exp(scores - jnp.max(scores, axis=0, keepdims=True))
+    row_total = jnp.sum(weights, axis=0, keepdims=True)
+    attended = (dot(value, weights.astype(jnp.bfloat16), TN) / row_total).astype(jnp.bfloat16)
+    attended = attended.astype(jnp.float32)
+    grad_dot = jnp.sum(grad.astype(jnp.float32).T * attended, axis=0, keepdims=True)
+    probability = weights * (1.0 / row_total)
+    score_grad = (probability * (dot(value, grad, NT) - grad_dot)).astype(jnp.bfloat16)
+    value_grad = dot(probability.astype(jnp.bfloat16), grad)
+    key_grad = dot(score_grad, query) * scaling
+    query_grad = (dot(key, score_grad, TN) * scaling).T
+    attended = attended.T.astype(jnp.bfloat16)
+    for place in range(devices):
+        attended_ref[place] = fold_half(attended[place * local_rows : (place + 1) * local_rows])
+    proj_ref[:rows] = jnp.concatenate([query_grad, key_grad], axis=1).astype(jnp.bfloat16)
+    proj_ref[rows:] = fold_half(value_grad.astype(jnp.bfloat16))
+
+
+def block_kernel(came_ref, target_ref, placed_ref):
+    devices, token_cap, width = came_ref.shape
+    rows = placed_ref.shape[1]
+    row_id = lax.broadcasted_iota(jnp.int32, (rows, token_cap), 0)
+    total = jnp.zeros((rows, width), jnp.float32)
+    for sender in range(devices):
+        total = total + dot(one_hot(row_id == target_ref[sender : sender + 1, :]), came_ref[sender])
+    placed_ref[...] = total.T.astype(jnp.bfloat16)
+
+
+def by_column(left, pieces, held_ref):
+    rows = left.shape[1]
+    half = rows // 2
+    me = lax.axis_index("seq")
+    for flip, piece in enumerate(pieces):
+        both = dot(left, piece[:rows])
+        low = dot(left[:, :half], piece[rows:])
+        high = dot(left[:, half:], piece[rows:])
+        value = low[:, :HEAD_DIM] + high[:, HEAD_DIM:]
+        held_ref[jnp.bitwise_xor(me, flip)] = jnp.concatenate([both, value], axis=1)
+    return jnp.concatenate(
+        [
+            held_ref[head, :, part * HEAD_DIM : (part + 1) * HEAD_DIM]
+            for part in range(3)
+            for head in range(len(pieces))
+        ],
+        axis=1,
+    )
+
+
+def weight_kernel(placed_ref, *refs):
+    pieces, outs, (held_ref, block_ref) = refs[:HEADS], refs[HEADS:-2], refs[-2:]
+    columns = by_column(placed_ref[...], pieces, held_ref).astype(jnp.bfloat16)
+    width = columns.shape[1] // len(outs)
+    me = lax.axis_index("clip")
+    for index in range(len(outs)):
+        block_ref[index] = columns[:, index * width : (index + 1) * width]
+    for flip, out in enumerate(outs):
+        out[...] = block_ref[jnp.bitwise_xor(me, flip)]
+
+
+def patch_kernel(segment_ref, shard_ref, slot_ref, w_ref, came_ref, *refs):
+    pieces, (patch_ref, attended_ref, held_ref) = refs[:HEADS], refs[HEADS:]
+    token_cap = shard_ref.shape[1]
+    local_rows = attended_ref.shape[0]
+    rows = came_ref.shape[0] * local_rows
+    shard = shard_ref[...]
+    target = jnp.where(shard >= 0, shard * local_rows + slot_ref[...], -1)
+    row_id = lax.broadcasted_iota(jnp.int32, (rows, token_cap), 0)
+    chooser = jnp.where(row_id == target, 1.0, 0.0).T.astype(jnp.bfloat16)
+    proj_grad = by_column(chooser, pieces, held_ref).astype(jnp.bfloat16)
+    token_grad = dot(proj_grad, w_ref[...], NT).astype(jnp.bfloat16).astype(jnp.float32)
+    member = (
+        lax.broadcasted_iota(jnp.int32, (token_cap, segment_ref.shape[1]), 0) == segment_ref[...]
+    )
+    counts = jnp.sum(jnp.where(member, 1.0, 0.0), axis=1, keepdims=True)
+    shared = (token_grad / jnp.maximum(counts, 1.0)).astype(jnp.bfloat16)
+    patch_ref[...] = dot(one_hot(member), shared, TN).astype(jnp.bfloat16)
+    attended_ref[...] = jnp.concatenate(
+        [unfold_half(came_ref[head]) for head in range(came_ref.shape[0])], axis=1
+    )
+
+
+def sum_kernel(*refs):
+    total = refs[0][...].astype(jnp.float32)
+    for ref in refs[1:-1]:
+        total = total + ref[...].astype(jnp.float32)
+    refs[-1][...] = total
+
+
+def exchange(rows, axis, flip):
+    count = lax.axis_size(axis)
+    return lax.ppermute(rows, axis, [(index, index ^ flip) for index in range(count)])
+
+
+def all_to_all(rows):
+    return lax.all_to_all(rows, "seq", split_axis=0, concat_axis=0, tiled=True)
+
+
+def shape(*sizes, dtype=jnp.bfloat16):
+    return jax.ShapeDtypeStruct(sizes, dtype)
+
+
+def heads_plan(patches, segment, dest_shard, dest_slot, w_qkv, out_grad):
+    devices = lax.axis_size("seq")
+    clips = lax.axis_size("clip")
+    token_cap = dest_shard.shape[1]
+    local_rows, inner = out_grad.shape[1:]
+    rows = devices * local_rows
+    model = patches.shape[2]
+    width = model // devices
+    sent = token_cap + token_cap // 2 + 16 + local_rows // 2
+    send, blocks = call(
+        token_kernel,
+        [shape(devices, sent, 2 * HEAD_DIM), shape(devices, token_cap, width)],
+        patches[0],
+        segment,
+        dest_shard,
+        dest_slot,
+        w_qkv,
+        out_grad[0],
+    )
+    came = all_to_all(send)
+    came_blocks = all_to_all(blocks)
+    attended_send, proj, target = call(
+        lambda *refs: head_kernel(token_cap, *refs),
+        [
+            shape(devices, local_rows // 2, 2 * HEAD_DIM),
+            shape(rows + rows // 2, 2 * HEAD_DIM),
+            shape(devices, token_cap, dtype=jnp.int32),
+        ],
+        came,
+    )
+    placed = call(block_kernel, shape(width, rows), came_blocks, target)
+    even = [proj] + [exchange(proj, "seq", flip) for flip in range(2, devices, 2)]
+    odd = [exchange(piece, "seq", 1) for piece in even]
+    pieces = [piece for pair in zip(even, odd) for piece in pair]
+    weights = call(
+        weight_kernel,
+        [shape(width, 3 * inner // clips)] * clips,
+        placed,
+        *pieces,
+        scratch=[
+            pltpu.VMEM((devices, width, 3 * HEAD_DIM), jnp.float32),
+            pltpu.VMEM((clips, width, 3 * inner // clips), jnp.bfloat16),
+        ],
+    )
+    weights = [weights[0]] + [exchange(weights[flip], "clip", flip) for flip in range(1, clips)]
+    patch_grad, attended = call(
+        patch_kernel,
+        [shape(patches.shape[1], model), shape(local_rows, inner)],
+        segment,
+        dest_shard,
+        dest_slot,
+        w_qkv,
+        all_to_all(attended_send),
+        *pieces,
+        scratch=[pltpu.VMEM((devices, token_cap, 3 * HEAD_DIM), jnp.float32)],
+    )
+    weight_grad = call(
+        sum_kernel, shape(width, 3 * inner // clips, dtype=jnp.float32), *weights
+    )
+    return attended[None], patch_grad[None], weight_grad
+
+
 def solution(mesh):
+    devices, clips = mesh.shape["seq"], mesh.shape["clip"]
+    one_head_each = devices == HEADS and clips in (1, 2, 4, 8)
     return jax.shard_map(
-        local,
+        heads_plan if one_head_each else rows_plan,
         mesh=mesh,
         in_specs=(
             P("clip", "seq", None),

time: 204 us -> 67.3 us (0.33)
  waiting for transfers between devices: 60.2 us -> 7.8 us
  blocking collectives: 60.2 us -> 25 us
  matrix products: 20.9 us -> 0 us
  local copies, waits for them, and re-layouts: 28.7 us -> 7.81 us
  between operations: 14.3 us -> 0.74 us
  Pallas kernels: 0 us -> 13.1 us
  other arithmetic: 6.48 us -> 0 us
    all_gather x6 -> x0, blocking collectives: 60.2 us -> none  [the longest x1 12.1 us: local(): lax.all_gather(grad_rows, 'seq', axis=0, tiled=True)]
    reduce_scatter x1 -> x0, waiting for transfers between devices: 46.6 us -> none  [local(): lax.psum_scatter(partial_value, 'seq', scatter_dimension=0, tiled=True)]
    all_to_all x0 -> x2, blocking collectives: none -> 25 us  [all_to_all(): return lax.all_to_all(rows, 'seq', split_axis=0, concat_axis=0, tiled=True)]
    dot_general x12 -> x0, matrix products: 20.9 us -> none  [the longest x1 2.74 us: combine_piece(): jnp.einsum('hrk,khd->hrd', score_grad, key_heads, preferred_element_type=...]
    pallas_call x0 -> x6, Pallas kernels: none -> 13.1 us  [call(): pl.pallas_call(body, out_shape=outs, scratch_shapes=scratch, compiler_par...]
    ppermute x0 -> x10, starting transfers between devices: none -> 8.86 us  [exchange(): lax.ppermute(rows, axis, [(index, index ^ flip) for index in range(count)])]
    all_to_all x3 -> x1, starting transfers between devices: 12.1 us -> 3.45 us  [all_to_all(): return lax.all_to_all(rows, 'seq', split_axis=0, concat_axis=0, tiled=True)]
    all_gather x6 -> x0, local copies, waits for them, and re-layouts: 8.28 us -> none  [the longest x1 2.09 us: local(): lax.all_gather(key_rows, 'seq', axis=0, tiled=True)]
  transfers between devices with their start and end apart: 5 -> 11, of which waited for: 4 -> 3; matrix products, arithmetic and copies ran while one was open for 6% -> 0% of each run, Pallas kernels for 0% -> 8%
where the time goes in v1:
time: 67.3 us; the launch traced here: 66.8 us
  blocking collectives  25 us (37%)
  Pallas kernels  13.1 us (19%)
  starting transfers between devices  12.3 us (18%)
  local copies, waits for them, and re-layouts  7.81 us (12%)
  waiting for transfers between devices  7.8 us (12%)
  between operations  0.74 us (1%)
    all_to_all x2, blocking collectives, all_to_all(): return lax.all_to_all(rows, 'seq', split_axis=0, concat_axis=0, tiled=True)  25 us
    pallas_call x6, Pallas kernels, call(): pl.pallas_call(body, out_shape=outs, scratch_shapes=scratch, compiler_par...  13.1 us
    ppermute x10, starting transfers between devices, exchange(): lax.ppermute(rows, axis, [(index, index ^ flip) for index in range(count)])  8.86 us
    unnamed x24, local copies, waits for them, and re-layouts  7.81 us
    ppermute x10, waiting for transfers between devices, exchange(): lax.ppermute(rows, axis, [(index, index ^ flip) for index in range(count)])  4.86 us
    all_to_all x1, starting transfers between devices, all_to_all(): return lax.all_to_all(rows, 'seq', split_axis=0, concat_axis=0, tiled=True)  3.45 us
    all_to_all x1, waiting for transfers between devices, all_to_all(): return lax.all_to_all(rows, 'seq', split_axis=0, concat_axis=0, tiled=True)  2.93 us
  transfers between devices with their start and end apart: 11, of which 3 were waited for; matrix products, arithmetic and copies ran while one was open for 0% of the time, Pallas kernels for 8%

profile of v1, /device:TPU:0, one launch (start us, length us, event | category | flops | bytes accessed | tf_op | source)
XLA Modules:
  0.0 66.8 jit_solution(11635791011603826070)
XLA Ops:
  0.6 0.0 copy-start
  0.6 1.9 %copy-done = bf16[1024,1536]{1,0:T(8,128)(2,1)S(1)} copy-done((bf16[1024,1536]{1,0:T(8,128)(2,1)S(1)}, bf16[1024,1536]{1,0:T(8,128)(2,1)}, u32[]{:S(2)}) %copy-start) | copy-done | bytes 3145752
  2.5 1.0 %copy-done.2 = bf16[1,196,1024]{2,1,0:T(8,128)(2,1)S(1)} copy-done((bf16[1,196,1024]{2,1,0:T(8,128)(2,1)S(1)}, bf16[1,196,1024]{2,1,0:T(8,128)(2,1)}, u32[]{:S(2)}) %copy-start.2) | copy-done | bytes 401432
  3.5 0.8 %copy-done.5 = bf16[1,64,512]{2,1,0:T(8,128)(2,1)S(1)} copy-done((bf16[1,64,512]{2,1,0:T(8,128)(2,1)S(1)}, bf16[1,64,512]{2,1,0:T(8,128)(2,1)}, u32[]{:S(2)}) %copy-start.5) | copy-done | bytes 65560
  4.4 0.7 %copy-done.6 = s32[1,196]{1,0:T(1,128)S(1)} copy-done((s32[1,196]{1,0:T(1,128)S(1)}, s32[1,196]{1,0:T(1,128)}, u32[]{:S(2)}) %copy-start.6) | copy-done | bytes 808
  5.0 0.7 %copy-done.8 = s32[1,192]{1,0:T(1,128)S(1)} copy-done((s32[1,192]{1,0:T(1,128)S(1)}, s32[1,192]{1,0:T(1,128)}, u32[]{:S(2)}) %copy-start.8) | copy-done | bytes 792
  5.7 0.7 %copy-done.10 = s32[1,192]{1,0:T(1,128)S(1)} copy-done((s32[1,192]{1,0:T(1,128)S(1)}, s32[1,192]{1,0:T(1,128)}, u32[]{:S(2)}) %copy-start.10) | copy-done | bytes 792
  6.4 1.0 %shard_map.85 = (bf16[8,336,128]{2,1,0:T(8,128)(2,1)S(1)}, bf16[8,192,128]{2,1,0:T(8,128)(2,1)S(1)}) custom-call(bf16[196,1024]{1,0:T(8,128)(2,1)S(1)} %bitcast.4, s32[1,196]{1,0:T(1,128)S(1)} %copy-done.6, s32[1,192]{1,0:T(1,128)S(1)} %copy-done.8, s32[1,192]{1,0:T(1,128)S(1)} %copy-done.10, bf16[1024,1536]{1,0:T(8,128)(2,1)S(1)} %copy-done, ...), custom_call_target="tpu_custom_call" | custom-call | tf_op jit(solution)/shard_map/pallas_call | solution.py:241
  7.4 0.0 copy-start.3
  7.4 0.7 %copy-done.3 = bf16[8,192,128]{2,1,0:T(8,128)(2,1)} copy-done((bf16[8,192,128]{2,1,0:T(8,128)(2,1)}, bf16[8,192,128]{2,1,0:T(8,128)(2,1)S(1)}, u32[]{:S(2)}) %copy-start.3) | copy-done | bytes 393240
  8.1 16.7 %all_to_all.15.refs_0_ = bf16[8,336,128]{2,1,0:T(8,128)(2,1)S(1)} all-to-all(bf16[8,336,128]{2,1,0:T(8,128)(2,1)S(1)} %get-tuple-element.14), channel_id=1, replica_groups=mesh['clip'=4,'seq'=8] {'seq'}, dimensions={0} | all-to-all | bytes 1376256 | tf_op jit(solution)/shard_map/all_to_all | solution.py:438
  24.9 3.5 %shard_map.86 = (bf16[8,32,128]{2,1,0:T(8,128)(2,1)S(1)}, bf16[768,128]{1,0:T(8,128)(2,1)}, s32[8,192]{1,0:T(8,128)S(1)}) custom-call(bf16[8,336,128]{2,1,0:T(8,128)(2,1)S(1)} %all_to_all.15.refs_0_), custom_call_target="tpu_custom_call" | custom-call | tf_op jit(solution)/shard_map/pallas_call | solution.py:241
  28.3 0.6 copy-done.4
  29.0 0.6 collective-permute-start.1
  29.5 0.6 collective-permute-start.3
  30.1 2.4 %collective-permute-start.5 = (bf16[768,128]{1,0:T(8,128)(2,1)}, bf16[768,128]{1,0:T(8,128)(2,1)}, u32[]{:S(2)}, u32[]{:S(2)}) collective-permute-start(bf16[768,128]{1,0:T(8,128)(2,1)} %get-tuple-element.16.refs_0_), channel_id=1, source_target_pairs={{0,6},{1,7},{2,4},{3,5},{4,2},{5,3},{6,0},{7,1},{8,14},{9,15},{10,... | collective-permute-start | bytes 589832 | tf_op jit(solution)/shard_map/ppermute | solution.py:434
  32.5 3.5 %all-to-all-start.2 = ((bf16[8,192,128]{2,1,0:T(8,128)(2,1)}), bf16[8,192,128]{2,1,0:T(8,128)(2,1)S(1)}, u32[]{:S(2)}, u32[]{:S(2)}) async-start(bf16[8,192,128]{2,1,0:T(8,128)(2,1)} %copy-done.3), calls=%async_computation.2 | async-start | bytes 786432 | tf_op jit(solution)/shard_map/all_to_all | solution.py:438
  35.9 0.4 collective-permute-start
  36.3 0.8 %collective-permute-done.1.refs_2_ = bf16[768,128]{1,0:T(8,128)(2,1)} collective-permute-done((bf16[768,128]{1,0:T(8,128)(2,1)}, bf16[768,128]{1,0:T(8,128)(2,1)}, u32[]{:S(2)}, u32[]{:S(2)}) %collective-permute-start.1) | collective-permute-done | bytes 196640 | tf_op jit(solution)/shard_map/ppermute | solution.py:434
  37.1 4.1 %collective-permute-done.3.refs_4_ = bf16[768,128]{1,0:T(8,128)(2,1)} collective-permute-done((bf16[768,128]{1,0:T(8,128)(2,1)}, bf16[768,128]{1,0:T(8,128)(2,1)}, u32[]{:S(2)}, u32[]{:S(2)}) %collective-permute-start.3) | collective-permute-done | bytes 196640 | tf_op jit(solution)/shard_map/ppermute | solution.py:434
  41.2 0.5 collective-permute-start.6
  41.7 2.9 %all-to-all-done.2.came_ref = bf16[8,192,128]{2,1,0:T(8,128)(2,1)S(1)} async-done(((bf16[8,192,128]{2,1,0:T(8,128)(2,1)}), bf16[8,192,128]{2,1,0:T(8,128)(2,1)S(1)}, u32[]{:S(2)}, u32[]{:S(2)}) %all-to-all-start.2) | async-done | bytes 393248 | tf_op jit(solution)/shard_map/all_to_all | solution.py:438
  44.6 0.8 %shard_map.88.placed_ref = bf16[128,512]{1,0:T(8,128)(2,1)S(1)} custom-call(bf16[8,192,128]{2,1,0:T(8,128)(2,1)S(1)} %all-to-all-done.2.came_ref, s32[8,192]{1,0:T(8,128)S(1)} %get-tuple-element.20.target_ref), custom_call_target="tpu_custom_call" | custom-call | tf_op jit(solution)/shard_map/pallas_call | solution.py:241
  45.4 2.4 %shard_map.89 = (bf16[128,384]{1,0:T(8,128)(2,1)S(1)}, bf16[128,384]{1,0:T(8,128)(2,1)S(1)}, bf16[128,384]{1,0:T(8,128)(2,1)S(1)}, bf16[128,384]{1,0:T(8,128)(2,1)S(1)}) custom-call(bf16[128,512]{1,0:T(8,128)(2,1)S(1)} %shard_map.88.placed_ref, bf16[768,128]{1,0:T(8,128)(2,1)} %get-tuple-element.16.refs_0_, bf16[768,128]{1,0:T(8,128)(2,1)} %collective-permute-done.refs_1_, ...), custom_call_target="tpu_custom_call" | custom-call | tf_op jit(solution)/shard_map/pallas_call | solution.py:241
  47.9 1.6 %collective-permute-start.7 = (bf16[128,384]{1,0:T(8,128)(2,1)S(1)}, bf16[128,384]{1,0:T(8,128)(2,1)S(1)}, u32[]{:S(2)}, u32[]{:S(2)}) collective-permute-start(bf16[128,384]{1,0:T(8,128)(2,1)S(1)} %get-tuple-element.22), channel_id=1, source_target_pairs={{0,8},{8,0},{16,24},{24,16},{1,9},{9,1},{17,25},{25,17},{2,10},{10... | collective-permute-start | bytes 294920 | tf_op jit(solution)/shard_map/ppermute | solution.py:434
  49.5 2.6 %collective-permute-start.8 = (bf16[128,384]{1,0:T(8,128)(2,1)S(1)}, bf16[128,384]{1,0:T(8,128)(2,1)S(1)}, u32[]{:S(2)}, u32[]{:S(2)}) collective-permute-start(bf16[128,384]{1,0:T(8,128)(2,1)S(1)} %get-tuple-element.23), channel_id=1, source_target_pairs={{0,16},{8,24},{16,0},{24,8},{1,17},{9,25},{17,1},{25,9},{2,18},{10... | collective-permute-start | bytes 294920 | tf_op jit(solution)/shard_map/ppermute | solution.py:434
  52.1 0.2 collective-permute-start.9
  52.3 8.3 %all_to_all.16.came_ref = bf16[8,32,128]{2,1,0:T(8,128)(2,1)S(1)} all-to-all(bf16[8,32,128]{2,1,0:T(8,128)(2,1)} %copy-done.4), channel_id=1, replica_groups=mesh['clip'=4,'seq'=8] {'seq'}, dimensions={0} | all-to-all | bytes 131072 | tf_op jit(solution)/shard_map/all_to_all | solution.py:438
  60.6 0.0 copy-start.11
  60.6 0.7 %copy-done.11 = s32[1,192]{1,0:T(1,128)S(1)} copy-done((s32[1,192]{1,0:T(1,128)S(1)}, s32[1,192]{1,0:T(1,128)}, u32[]{:S(2)}) %copy-start.11) | copy-done | bytes 792
  61.3 4.7 %shard_map.87 = (bf16[196,1024]{1,0:T(8,128)(2,1)}, bf16[64,512]{1,0:T(8,128)(2,1)}) custom-call(s32[1,196]{1,0:T(1,128)S(1)} %copy-done.7, s32[1,192]{1,0:T(1,128)S(1)} %copy-done.9, s32[1,192]{1,0:T(1,128)S(1)} %copy-done.11, bf16[1024,1536]{1,0:T(8,128)(2,1)S(1)} %copy-done.1, bf16[8,32,128]{2,1,0:T(8,128)(2,1)S(1)} %all_to_all.16.came_ref, ...), custom_call_target="tpu_custom_call" | custom-call | tf_op jit(solution)/shard_map/pallas_call | solution.py:241
  66.0 0.7 %shard_map.90 = f32[128,384]{1,0:T(8,128)} custom-call(bf16[128,384]{1,0:T(8,128)(2,1)S(1)} %get-tuple-element.21.refs_0_, bf16[128,384]{1,0:T(8,128)(2,1)S(1)} %collective-permute-done.7.refs_1_, bf16[128,384]{1,0:T(8,128)(2,1)S(1)} %collective-permute-done.8.refs_2_, bf16[128,384]{1,0:T(8,128)(2,1)S(1)} %collective-permute-done.9.refs_3_), custom_call_target="tpu_custom_call" | custom-call | tf_op jit(solution)/shard_map/pallas_call | solution.py:241
  (22 shorter events, 0.0 us)
Async XLA Ops:
  0.6 1.9 %copy-start = (bf16[1024,1536]{1,0:T(8,128)(2,1)S(1)}, bf16[1024,1536]{1,0:T(8,128)(2,1)}, u32[]{:S(2)}) copy-start(bf16[1024,1536]{1,0:T(8,128)(2,1)} %w_ref.3) | copy-start | bytes 9437188
  2.5 1.0 %copy-start.2 = (bf16[1,196,1024]{2,1,0:T(8,128)(2,1)S(1)}, bf16[1,196,1024]{2,1,0:T(8,128)(2,1)}, u32[]{:S(2)}) copy-start(bf16[1,196,1024]{2,1,0:T(8,128)(2,1)} %param.6) | copy-start | bytes 1204228
  3.5 0.8 %copy-start.5 = (bf16[1,64,512]{2,1,0:T(8,128)(2,1)S(1)}, bf16[1,64,512]{2,1,0:T(8,128)(2,1)}, u32[]{:S(2)}) copy-start(bf16[1,64,512]{2,1,0:T(8,128)(2,1)} %param.11) | copy-start | bytes 196612
  4.4 0.7 %copy-start.6 = (s32[1,196]{1,0:T(1,128)S(1)}, s32[1,196]{1,0:T(1,128)}, u32[]{:S(2)}) copy-start(s32[1,196]{1,0:T(1,128)} %segment_ref.3) | copy-start | bytes 2356
  5.0 0.7 %copy-start.8 = (s32[1,192]{1,0:T(1,128)S(1)}, s32[1,192]{1,0:T(1,128)}, u32[]{:S(2)}) copy-start(s32[1,192]{1,0:T(1,128)} %shard_ref.3) | copy-start | bytes 2308
  5.7 0.7 %copy-start.10 = (s32[1,192]{1,0:T(1,128)S(1)}, s32[1,192]{1,0:T(1,128)}, u32[]{:S(2)}) copy-start(s32[1,192]{1,0:T(1,128)} %slot_ref.3) | copy-start | bytes 2308
  7.4 0.7 %copy-start.3 = (bf16[8,192,128]{2,1,0:T(8,128)(2,1)}, bf16[8,192,128]{2,1,0:T(8,128)(2,1)S(1)}, u32[]{:S(2)}) copy-start(bf16[8,192,128]{2,1,0:T(8,128)(2,1)S(1)} %get-tuple-element.19) | copy-start | bytes 1179652
  8.1 52.5 %copy-start.1 = (bf16[1024,1536]{1,0:T(8,128)(2,1)S(1)}, bf16[1024,1536]{1,0:T(8,128)(2,1)}, u32[]{:S(2)}) copy-start(bf16[1024,1536]{1,0:T(8,128)(2,1)} %w_ref.3) | copy-start | bytes 9437188
  8.1 52.5 %copy-start.7 = (s32[1,196]{1,0:T(1,128)S(1)}, s32[1,196]{1,0:T(1,128)}, u32[]{:S(2)}) copy-start(s32[1,196]{1,0:T(1,128)} %segment_ref.3) | copy-start | bytes 2356
  8.1 52.5 %copy-start.9 = (s32[1,192]{1,0:T(1,128)S(1)}, s32[1,192]{1,0:T(1,128)}, u32[]{:S(2)}) copy-start(s32[1,192]{1,0:T(1,128)} %shard_ref.3) | copy-start | bytes 2308
  28.3 0.6 copy-start.4
  29.0 8.1 %collective-permute-start.1 = (bf16[768,128]{1,0:T(8,128)(2,1)}, bf16[768,128]{1,0:T(8,128)(2,1)}, u32[]{:S(2)}, u32[]{:S(2)}) collective-permute-start(bf16[768,128]{1,0:T(8,128)(2,1)} %get-tuple-element.16.refs_0_), channel_id=1, source_target_pairs={{0,2},{1,3},{2,0},{3,1},{4,6},{5,7},{6,4},{7,5},{8,10},{9,11},{10,... | collective-permute-start | bytes 589832 | tf_op jit(solution)/shard_map/ppermute | solution.py:434
  29.5 11.6 %collective-permute-start.3 = (bf16[768,128]{1,0:T(8,128)(2,1)}, bf16[768,128]{1,0:T(8,128)(2,1)}, u32[]{:S(2)}, u32[]{:S(2)}) collective-permute-start(bf16[768,128]{1,0:T(8,128)(2,1)} %get-tuple-element.16.refs_0_), channel_id=1, source_target_pairs={{0,4},{1,5},{2,6},{3,7},{4,0},{5,1},{6,2},{7,3},{8,12},{9,13},{10,... | collective-permute-start | bytes 589832 | tf_op jit(solution)/shard_map/ppermute | solution.py:434
  30.1 11.1 %collective-permute-start.5 = (bf16[768,128]{1,0:T(8,128)(2,1)}, bf16[768,128]{1,0:T(8,128)(2,1)}, u32[]{:S(2)}, u32[]{:S(2)}) collective-permute-start(bf16[768,128]{1,0:T(8,128)(2,1)} %get-tuple-element.16.refs_0_), channel_id=1, source_target_pairs={{0,6},{1,7},{2,4},{3,5},{4,2},{5,3},{6,0},{7,1},{8,14},{9,15},{10,... | collective-permute-start | bytes 589832 | tf_op jit(solution)/shard_map/ppermute | solution.py:434
  32.5 12.2 %all-to-all-start.2 = ((bf16[8,192,128]{2,1,0:T(8,128)(2,1)}), bf16[8,192,128]{2,1,0:T(8,128)(2,1)S(1)}, u32[]{:S(2)}, u32[]{:S(2)}) async-start(bf16[8,192,128]{2,1,0:T(8,128)(2,1)} %copy-done.3), calls=%async_computation.2 | async-start | bytes 786432 | tf_op jit(solution)/shard_map/all_to_all | solution.py:438
  35.9 9.5 %collective-permute-start = (bf16[768,128]{1,0:T(8,128)(2,1)}, bf16[768,128]{1,0:T(8,128)(2,1)}, u32[]{:S(2)}, u32[]{:S(2)}) collective-permute-start(bf16[768,128]{1,0:T(8,128)(2,1)} %get-tuple-element.16.refs_0_), channel_id=1, source_target_pairs={{0,1},{1,0},{2,3},{3,2},{4,5},{5,4},{6,7},{7,6},{8,9},{9,8},{10,11... | collective-permute-start | bytes 589832 | tf_op jit(solution)/shard_map/ppermute | solution.py:434
  37.1 8.3 %collective-permute-start.2 = (bf16[768,128]{1,0:T(8,128)(2,1)}, bf16[768,128]{1,0:T(8,128)(2,1)}, u32[]{:S(2)}, u32[]{:S(2)}) collective-permute-start(bf16[768,128]{1,0:T(8,128)(2,1)} %collective-permute-done.1.refs_2_), channel_id=1, source_target_pairs={{0,1},{1,0},{2,3},{3,2},{4,5},{5,4},{6,7},{7,6},{8,9},{9,8},{10,11... | collective-permute-start | bytes 589832 | tf_op jit(solution)/shard_map/ppermute | solution.py:434
  41.2 4.2 %collective-permute-start.4 = (bf16[768,128]{1,0:T(8,128)(2,1)}, bf16[768,128]{1,0:T(8,128)(2,1)}, u32[]{:S(2)}, u32[]{:S(2)}) collective-permute-start(bf16[768,128]{1,0:T(8,128)(2,1)} %collective-permute-done.3.refs_4_), channel_id=1, source_target_pairs={{0,1},{1,0},{2,3},{3,2},{4,5},{5,4},{6,7},{7,6},{8,9},{9,8},{10,11... | collective-permute-start | bytes 589832 | tf_op jit(solution)/shard_map/ppermute | solution.py:434
  41.2 4.2 %collective-permute-start.6 = (bf16[768,128]{1,0:T(8,128)(2,1)}, bf16[768,128]{1,0:T(8,128)(2,1)}, u32[]{:S(2)}, u32[]{:S(2)}) collective-permute-start(bf16[768,128]{1,0:T(8,128)(2,1)} %collective-permute-done.5.refs_6_), channel_id=1, source_target_pairs={{0,1},{1,0},{2,3},{3,2},{4,5},{5,4},{6,7},{7,6},{8,9},{9,8},{10,11... | collective-permute-start | bytes 589832 | tf_op jit(solution)/shard_map/ppermute | solution.py:434
  47.9 18.1 %collective-permute-start.7 = (bf16[128,384]{1,0:T(8,128)(2,1)S(1)}, bf16[128,384]{1,0:T(8,128)(2,1)S(1)}, u32[]{:S(2)}, u32[]{:S(2)}) collective-permute-start(bf16[128,384]{1,0:T(8,128)(2,1)S(1)} %get-tuple-element.22), channel_id=1, source_target_pairs={{0,8},{8,0},{16,24},{24,16},{1,9},{9,1},{17,25},{25,17},{2,10},{10... | collective-permute-start | bytes 294920 | tf_op jit(solution)/shard_map/ppermute | solution.py:434
  49.5 16.5 %collective-permute-start.8 = (bf16[128,384]{1,0:T(8,128)(2,1)S(1)}, bf16[128,384]{1,0:T(8,128)(2,1)S(1)}, u32[]{:S(2)}, u32[]{:S(2)}) collective-permute-start(bf16[128,384]{1,0:T(8,128)(2,1)S(1)} %get-tuple-element.23), channel_id=1, source_target_pairs={{0,16},{8,24},{16,0},{24,8},{1,17},{9,25},{17,1},{25,9},{2,18},{10... | collective-permute-start | bytes 294920 | tf_op jit(solution)/shard_map/ppermute | solution.py:434
  52.1 13.9 %collective-permute-start.9 = (bf16[128,384]{1,0:T(8,128)(2,1)S(1)}, bf16[128,384]{1,0:T(8,128)(2,1)S(1)}, u32[]{:S(2)}, u32[]{:S(2)}) collective-permute-start(bf16[128,384]{1,0:T(8,128)(2,1)S(1)} %get-tuple-element.24), channel_id=1, source_target_pairs={{0,24},{8,16},{16,8},{24,0},{1,25},{9,17},{17,9},{25,1},{2,26},{10... | collective-permute-start | bytes 294920 | tf_op jit(solution)/shard_map/ppermute | solution.py:434
  60.6 0.7 %copy-start.11 = (s32[1,192]{1,0:T(1,128)S(1)}, s32[1,192]{1,0:T(1,128)}, u32[]{:S(2)}) copy-start(s32[1,192]{1,0:T(1,128)} %slot_ref.3) | copy-start | bytes 2308

commit v2 on v1

--- a/solution.py
+++ b/solution.py
@@ -237,12 +237,13 @@
     return lax.dot_general(left, right, dims, preferred_element_type=jnp.float32)
 
 
-def call(body, outs, *args, scratch=()):
+def call(body, outs, *args, scratch=(), space=pltpu.VMEM, limit=VMEM_LIMIT):
     return pl.pallas_call(
         body,
         out_shape=outs,
+        in_specs=[pl.BlockSpec(memory_space=space)] * len(args),
         scratch_shapes=scratch,
-        compiler_params=pltpu.CompilerParams(vmem_limit_bytes=VMEM_LIMIT),
+        compiler_params=pltpu.CompilerParams(vmem_limit_bytes=limit),
     )(*args)
 
 
@@ -267,22 +268,35 @@
     return wide[:, :128], wide[:, 128:]
 
 
-def token_kernel(patch_ref, segment_ref, shard_ref, slot_ref, w_ref, grad_ref, send_ref, block_ref):
+def token_kernel(*refs):
+    sources, refs = refs[:6], refs[6:]
+    sends, refs = refs[:HEADS], refs[HEADS:]
+    (target_ref, segment_out, held_ref), refs = refs[:3], refs[3:]
+    copies = [
+        pltpu.make_async_copy(source, held, refs[6].at[index])
+        for index, (source, held) in enumerate(zip(sources, refs))
+    ]
+    for copy in copies:
+        copy.start()
+    segment_ref, patch_ref, shard_ref, slot_ref, grad_ref, w_ref = refs[:6]
     token_cap = shard_ref.shape[1]
     local_rows, inner = grad_ref.shape
-    devices = send_ref.shape[0]
-    width = block_ref.shape[2]
-    member = (
-        lax.broadcasted_iota(jnp.int32, (token_cap, segment_ref.shape[1]), 0) == segment_ref[...]
-    )
+    devices = len(sends)
+    width = patch_ref.shape[1] // devices
+    copies[0].wait()
+    segment = segment_ref[...]
+    segment_out[...] = segment
+    member = lax.broadcasted_iota(jnp.int32, (token_cap, segment.shape[1]), 0) == segment
     counts = jnp.sum(jnp.where(member, 1.0, 0.0), axis=1, keepdims=True)
+    copies[1].wait()
     token_sums = dot(one_hot(member), patch_ref[...])
     tokens = (token_sums / jnp.maximum(counts, 1.0)).astype(jnp.bfloat16)
-    for place in range(devices):
-        block_ref[place] = tokens[:, place * width : (place + 1) * width]
-    projected = dot(tokens, w_ref[...]).astype(jnp.bfloat16)
-    shard_low, shard_high = wide_row(shard_ref[...])
-    slot_low, slot_high = wide_row(slot_ref[...])
+    for copy in copies[2:5]:
+        copy.wait()
+    shard, slot = shard_ref[...], slot_ref[...]
+    target_ref[...] = jnp.where(shard >= 0, shard * local_rows + slot, -1)
+    shard_low, shard_high = wide_row(shard)
+    slot_low, slot_high = wide_row(slot)
     line = lax.broadcasted_iota(jnp.int32, (16, 128), 0)
     where_to = jnp.where(
         line == 0,
@@ -290,6 +304,8 @@
         jnp.where(line == 1, shard_high, jnp.where(line == 2, slot_low, slot_high)),
     ).astype(jnp.bfloat16)
     grads = grad_ref[...]
+    copies[5].wait()
+    projected = dot(tokens, w_ref[...]).astype(jnp.bfloat16)
     for head in range(devices):
         first = head * HEAD_DIM
         query, key, value = (
@@ -302,9 +318,13 @@
             fold_half(value),
             where_to,
             fold_half(grads[:, first : first + HEAD_DIM]),
+            tokens[:, head * width : (head + 1) * width],
         ):
-            send_ref[head, start : start + piece.shape[0]] = piece
+            held_ref[head, start : start + piece.shape[0]] = piece
             start += piece.shape[0]
+    me = lax.axis_index("seq")
+    for flip, send in enumerate(sends):
+        send[...] = held_ref[jnp.bitwise_xor(me, flip)]
 
 
 def target_row(lines, token_cap, local_rows):
@@ -314,33 +334,31 @@
     return (shard * local_rows + slot).astype(jnp.int32)
 
 
-def head_kernel(token_cap, came_ref, attended_ref, proj_ref, target_ref):
-    devices, local_rows = came_ref.shape[0], 2 * attended_ref.shape[1]
+def head_kernel(token_cap, *refs):
+    pieces, refs = refs[:HEADS], refs[HEADS:]
+    outs, (target_ref, grad_ref, attended_ref) = refs[: HEADS // 2], refs[HEADS // 2 :]
+    devices, local_rows = len(pieces), grad_ref.shape[1]
     rows = devices * local_rows
     scaling = HEAD_DIM ** (-0.5)
     half_cap = token_cap // 2
     lines_at = token_cap + half_cap
     row_id = lax.broadcasted_iota(jnp.int32, (rows, token_cap), 0)
     total = jnp.zeros((rows, 3 * HEAD_DIM), jnp.float32)
-    grads = []
-    for sender in range(devices):
-        target = target_row(came_ref[sender, lines_at : lines_at + 16], token_cap, local_rows)
-        target_ref[sender : sender + 1, :] = target
-        placer = one_hot(row_id == target)
+    me = lax.axis_index("seq")
+    for flip, piece in enumerate(pieces):
+        sender = jnp.bitwise_xor(me, flip)
+        target = target_row(piece[lines_at : lines_at + 16], token_cap, local_rows)
+        target_ref[sender] = target
         rows_in = jnp.concatenate(
-            [
-                came_ref[sender, :token_cap],
-                unfold_half(came_ref[sender, token_cap:lines_at]),
-            ],
-            axis=1,
+            [piece[:token_cap], unfold_half(piece[token_cap:lines_at])], axis=1
         )
-        total = total + dot(placer, rows_in)
-        grads.append(unfold_half(came_ref[sender, lines_at + 16 :]))
+        total = total + dot(one_hot(row_id == target), rows_in)
+        grad_ref[sender] = unfold_half(piece[lines_at + 16 : lines_at + 16 + local_rows // 2])
     projected = total.astype(jnp.bfloat16)
     query = projected[:, :HEAD_DIM]
     key = projected[:, HEAD_DIM : 2 * HEAD_DIM]
     value = projected[:, 2 * HEAD_DIM :]
-    grad = jnp.concatenate(grads, axis=0)
+    grad = jnp.concatenate([grad_ref[place] for place in range(devices)], axis=0)
     scores = dot(key, query, NT) * scaling
     weights = jnp.exp(scores - jnp.max(scores, axis=0, keepdims=True))
     row_total = jnp.sum(weights, axis=0, keepdims=True)
@@ -355,28 +373,39 @@
     attended = attended.T.astype(jnp.bfloat16)
     for place in range(devices):
         attended_ref[place] = fold_half(attended[place * local_rows : (place + 1) * local_rows])
-    proj_ref[:rows] = jnp.concatenate([query_grad, key_grad], axis=1).astype(jnp.bfloat16)
-    proj_ref[rows:] = fold_half(value_grad.astype(jnp.bfloat16))
-
-
-def block_kernel(came_ref, target_ref, placed_ref):
-    devices, token_cap, width = came_ref.shape
-    rows = placed_ref.shape[1]
+    proj_grad = jnp.concatenate([query_grad, key_grad], axis=1).astype(jnp.bfloat16)
+    value_grad = fold_half(value_grad.astype(jnp.bfloat16))
+    end = rows + rows // 2
+    for chip, out in enumerate(outs):
+        out[:rows] = proj_grad
+        out[rows:end] = value_grad
+        for core in range(2):
+            first = end + core * local_rows // 2
+            place = jnp.bitwise_xor(me, 2 * chip + core)
+            out[first : first + local_rows // 2] = attended_ref[place]
+
+
+def block_kernel(target_ref, *refs):
+    pieces, placed_ref = refs[:-1], refs[-1]
+    token_cap = target_ref.shape[2]
+    width, rows = placed_ref.shape
     row_id = lax.broadcasted_iota(jnp.int32, (rows, token_cap), 0)
     total = jnp.zeros((rows, width), jnp.float32)
-    for sender in range(devices):
-        total = total + dot(one_hot(row_id == target_ref[sender : sender + 1, :]), came_ref[sender])
+    me = lax.axis_index("seq")
+    for flip, piece in enumerate(pieces):
+        target = target_ref[jnp.bitwise_xor(me, flip)]
+        total = total + dot(one_hot(row_id == target), piece[piece.shape[0] - token_cap :])
     placed_ref[...] = total.T.astype(jnp.bfloat16)
 
 
 def by_column(left, pieces, held_ref):
     rows = left.shape[1]
-    half = rows // 2
+    half, end = rows // 2, rows + rows // 2
     me = lax.axis_index("seq")
     for flip, piece in enumerate(pieces):
         both = dot(left, piece[:rows])
-        low = dot(left[:, :half], piece[rows:])
-        high = dot(left[:, half:], piece[rows:])
+        low = dot(left[:, :half], piece[rows:end])
+        high = dot(left[:, half:], piece[rows:end])
         value = low[:, :HEAD_DIM] + high[:, HEAD_DIM:]
         held_ref[jnp.bitwise_xor(me, flip)] = jnp.concatenate([both, value], axis=1)
     return jnp.concatenate(
@@ -400,15 +429,18 @@
         out[...] = block_ref[jnp.bitwise_xor(me, flip)]
 
 
-def patch_kernel(segment_ref, shard_ref, slot_ref, w_ref, came_ref, *refs):
-    pieces, (patch_ref, attended_ref, held_ref) = refs[:HEADS], refs[HEADS:]
-    token_cap = shard_ref.shape[1]
+def patch_kernel(segment_ref, target_ref, w_ref, *refs):
+    pieces, (patch_ref, attended_ref, held_ref, part_ref) = refs[:HEADS], refs[HEADS:]
+    token_cap = target_ref.shape[1]
     local_rows = attended_ref.shape[0]
-    rows = came_ref.shape[0] * local_rows
-    shard = shard_ref[...]
-    target = jnp.where(shard >= 0, shard * local_rows + slot_ref[...], -1)
+    rows = HEADS * local_rows
+    me = lax.axis_index("seq")
+    for flip, piece in enumerate(pieces):
+        first = rows + rows // 2 + flip % 2 * local_rows // 2
+        part_ref[jnp.bitwise_xor(me, flip)] = unfold_half(piece[first : first + local_rows // 2])
+    attended_ref[...] = jnp.concatenate([part_ref[head] for head in range(HEADS)], axis=1)
     row_id = lax.broadcasted_iota(jnp.int32, (rows, token_cap), 0)
-    chooser = jnp.where(row_id == target, 1.0, 0.0).T.astype(jnp.bfloat16)
+    chooser = jnp.where(row_id == target_ref[...], 1.0, 0.0).T.astype(jnp.bfloat16)
     proj_grad = by_column(chooser, pieces, held_ref).astype(jnp.bfloat16)
     token_grad = dot(proj_grad, w_ref[...], NT).astype(jnp.bfloat16).astype(jnp.float32)
     member = (
@@ -417,9 +449,6 @@
     counts = jnp.sum(jnp.where(member, 1.0, 0.0), axis=1, keepdims=True)
     shared = (token_grad / jnp.maximum(counts, 1.0)).astype(jnp.bfloat16)
     patch_ref[...] = dot(one_hot(member), shared, TN).astype(jnp.bfloat16)
-    attended_ref[...] = jnp.concatenate(
-        [unfold_half(came_ref[head]) for head in range(came_ref.shape[0])], axis=1
-    )
 
 
 def sum_kernel(*refs):
@@ -432,10 +461,6 @@
 def exchange(rows, axis, flip):
     count = lax.axis_size(axis)
     return lax.ppermute(rows, axis, [(index, index ^ flip) for index in range(count)])
-
-
-def all_to_all(rows):
-    return lax.all_to_all(rows, "seq", split_axis=0, concat_axis=0, tiled=True)
 
 
 def shape(*sizes, dtype=jnp.bfloat16):
@@ -450,32 +475,43 @@
     rows = devices * local_rows
     model = patches.shape[2]
     width = model // devices
-    sent = token_cap + token_cap // 2 + 16 + local_rows // 2
-    send, blocks = call(
+    sent = token_cap + token_cap // 2 + 16 + local_rows // 2 + token_cap
+    sources = (segment, patches[0], dest_shard, dest_slot, out_grad[0], w_qkv)
+    outs = call(
         token_kernel,
-        [shape(devices, sent, 2 * HEAD_DIM), shape(devices, token_cap, width)],
-        patches[0],
-        segment,
-        dest_shard,
-        dest_slot,
-        w_qkv,
-        out_grad[0],
-    )
-    came = all_to_all(send)
-    came_blocks = all_to_all(blocks)
-    attended_send, proj, target = call(
+        [shape(sent, 2 * HEAD_DIM)] * devices
+        + [shape(1, token_cap, dtype=jnp.int32), shape(*segment.shape, dtype=jnp.int32)],
+        *sources,
+        scratch=[
+            pltpu.VMEM((devices, sent, 2 * HEAD_DIM), jnp.bfloat16),
+        ]
+        + [pltpu.VMEM(source.shape, source.dtype) for source in sources]
+        + [pltpu.SemaphoreType.DMA((len(sources),))],
+        space=pltpu.HBM,
+        limit=60 * 1024 * 1024,
+    )
+    sends, (target, segment) = outs[:devices], outs[devices:]
+    far_first = sorted(range(1, devices), key=lambda flip: (-(flip // 2).bit_count(), flip))
+    came = [sends[0]] + [None] * (devices - 1)
+    for flip in far_first:
+        came[flip] = exchange(sends[flip], "seq", flip)
+    *proj, targets = call(
         lambda *refs: head_kernel(token_cap, *refs),
-        [
-            shape(devices, local_rows // 2, 2 * HEAD_DIM),
-            shape(rows + rows // 2, 2 * HEAD_DIM),
-            shape(devices, token_cap, dtype=jnp.int32),
+        [shape(rows + rows // 2 + local_rows, 2 * HEAD_DIM)] * (devices // 2)
+        + [shape(devices, 1, token_cap, dtype=jnp.int32)],
+        *came,
+        scratch=[
+            pltpu.VMEM((devices, local_rows, HEAD_DIM), jnp.bfloat16),
+            pltpu.VMEM((devices, local_rows // 2, 2 * HEAD_DIM), jnp.bfloat16),
         ],
-        came,
-    )
-    placed = call(block_kernel, shape(width, rows), came_blocks, target)
-    even = [proj] + [exchange(proj, "seq", flip) for flip in range(2, devices, 2)]
-    odd = [exchange(piece, "seq", 1) for piece in even]
-    pieces = [piece for pair in zip(even, odd) for piece in pair]
+    )
+    pieces = [proj[0]] + [None] * (devices - 1)
+    for flip in far_first:
+        if flip % 2 == 0:
+            pieces[flip] = exchange(proj[flip // 2], "seq", flip)
+    for flip in range(1, devices, 2):
+        pieces[flip] = exchange(pieces[flip - 1], "seq", 1)
+    placed = call(block_kernel, shape(width, rows), targets, *came)
     weights = call(
         weight_kernel,
         [shape(width, 3 * inner // clips)] * clips,
@@ -491,12 +527,13 @@
         patch_kernel,
         [shape(patches.shape[1], model), shape(local_rows, inner)],
         segment,
-        dest_shard,
-        dest_slot,
+        target,
         w_qkv,
-        all_to_all(attended_send),
         *pieces,
-        scratch=[pltpu.VMEM((devices, token_cap, 3 * HEAD_DIM), jnp.float32)],
+        scratch=[
+            pltpu.VMEM((devices, token_cap, 3 * HEAD_DIM), jnp.float32),
+            pltpu.VMEM((devices, local_rows, HEAD_DIM), jnp.bfloat16),
+        ],
     )
     weight_grad = call(
         sum_kernel, shape(width, 3 * inner // clips, dtype=jnp.float32), *weights

time: 67.3 us -> 55.2 us (0.82)
  blocking collectives: 25 us -> 0 us
  waiting for transfers between devices: 7.8 us -> 23 us
  local copies, waits for them, and re-layouts: 7.81 us -> 0.92 us
  starting transfers between devices: 12.3 us -> 17.8 us
    all_to_all x2 -> x0, blocking collectives: 25 us -> none  [all_to_all(): return lax.all_to_all(rows, 'seq', split_axis=0, concat_axis=0, tiled=True)]
    ppermute x10 -> x17, waiting for transfers between devices: 4.86 us -> 23 us  [exchange(): lax.ppermute(rows, axis, [(index, index ^ flip) for index in range(count)])]
    ppermute x10 -> x17, starting transfers between devices: 8.86 us -> 17.8 us  [exchange(): lax.ppermute(rows, axis, [(index, index ^ flip) for index in range(count)])]
    unnamed x24 -> x8, local copies, waits for them, and re-layouts: 7.81 us -> 0.92 us
    all_to_all x1 -> x0, starting transfers between devices: 3.45 us -> none  [all_to_all(): return lax.all_to_all(rows, 'seq', split_axis=0, concat_axis=0, tiled=True)]
    all_to_all x1 -> x0, waiting for transfers between devices: 2.93 us -> none  [all_to_all(): return lax.all_to_all(rows, 'seq', split_axis=0, concat_axis=0, tiled=True)]
  transfers between devices with their start and end apart: 11 -> 17, of which waited for: 3 -> 7; matrix products, arithmetic and copies ran while one was open for 0% -> 0% of each run, Pallas kernels for 8% -> 7%
where the time goes in v2:
time: 55.2 us; the launch traced here: 55.1 us
  waiting for transfers between devices  23 us (42%)
  starting transfers between devices  17.8 us (32%)
  Pallas kernels  12.7 us (23%)
  local copies, waits for them, and re-layouts  0.92 us (2%)
  between operations  0.73 us (1%)
    ppermute x17, waiting for transfers between devices, exchange(): lax.ppermute(rows, axis, [(index, index ^ flip) for index in range(count)])  23 us
    ppermute x17, starting transfers between devices, exchange(): lax.ppermute(rows, axis, [(index, index ^ flip) for index in range(count)])  17.8 us
    pallas_call x6, Pallas kernels, call(): pl.pallas_call(body, out_shape=outs, in_specs=[pl.BlockSpec(memory_space=...  12.7 us
  transfers between devices with their start and end apart: 17, of which 7 were waited for; matrix products, arithmetic and copies ran while one was open for 0% of the time, Pallas kernels for 7%

profile of v2, /device:TPU:0, one launch (start us, length us, event | category | flops | bytes accessed | tf_op | source)
XLA Modules:
  0.0 55.1 jit_solution(14812454513147752248)
XLA Ops:
  0.6 4.2 %shard_map.85 = (bf16[528,128]{1,0:T(8,128)(2,1)}, bf16[528,128]{1,0:T(8,128)(2,1)}, bf16[528,128]{1,0:T(8,128)(2,1)}, bf16[528,128]{1,0:T(8,128)(2,1)}, bf16[52...) custom-call(s32[1,196]{1,0:T(1,128)} %refs_0_.1, ...), custom_call_target="tpu_custom_call" | custom-call | tf_op jit(solution)/shard_map/pallas_call | solution.py:241
  4.8 0.0 copy-start.2
  4.9 0.5 collective-permute-start
  5.4 2.6 %collective-permute-start.1 = (bf16[528,128]{1,0:T(8,128)(2,1)}, bf16[528,128]{1,0:T(8,128)(2,1)S(1)}, u32[]{:S(2)}, u32[]{:S(2)}) collective-permute-start(bf16[528,128]{1,0:T(8,128)(2,1)} %get-tuple-element.28), channel_id=1, source_target_pairs={{0,2},{1,3},{2,0},{3,1},{4,6},{5,7},{6,4},{7,5},{8,10},{9,11},{10,... | collective-permute-start | bytes 405512 | tf_op jit(solution)/shard_map/ppermute | solution.py:463
  7.9 0.1 collective-permute-start.2
  8.0 1.8 %collective-permute-start.3 = (bf16[528,128]{1,0:T(8,128)(2,1)}, bf16[528,128]{1,0:T(8,128)(2,1)S(1)}, u32[]{:S(2)}, u32[]{:S(2)}) collective-permute-start(bf16[528,128]{1,0:T(8,128)(2,1)} %get-tuple-element.30), channel_id=1, source_target_pairs={{0,4},{1,5},{2,6},{3,7},{4,0},{5,1},{6,2},{7,3},{8,12},{9,13},{10,... | collective-permute-start | bytes 405512 | tf_op jit(solution)/shard_map/ppermute | solution.py:463
  9.8 2.6 %collective-permute-start.5 = (bf16[528,128]{1,0:T(8,128)(2,1)}, bf16[528,128]{1,0:T(8,128)(2,1)S(1)}, u32[]{:S(2)}, u32[]{:S(2)}) collective-permute-start(bf16[528,128]{1,0:T(8,128)(2,1)} %get-tuple-element.32), channel_id=1, source_target_pairs={{0,6},{1,7},{2,4},{3,5},{4,2},{5,3},{6,0},{7,1},{8,14},{9,15},{10,... | collective-permute-start | bytes 405512 | tf_op jit(solution)/shard_map/ppermute | solution.py:463
  12.4 0.2 collective-permute-done.1.refs_2_
  12.6 1.7 %collective-permute-start.6 = (bf16[528,128]{1,0:T(8,128)(2,1)}, bf16[528,128]{1,0:T(8,128)(2,1)S(1)}, u32[]{:S(2)}, u32[]{:S(2)}) collective-permute-start(bf16[528,128]{1,0:T(8,128)(2,1)} %get-tuple-element.33), channel_id=1, source_target_pairs={{0,7},{1,6},{2,5},{3,4},{4,3},{5,2},{6,1},{7,0},{8,15},{9,14},{10,... | collective-permute-start | bytes 405512 | tf_op jit(solution)/shard_map/ppermute | solution.py:463
  14.3 0.8 %collective-permute-done.2.refs_3_ = bf16[528,128]{1,0:T(8,128)(2,1)S(1)} collective-permute-done((bf16[528,128]{1,0:T(8,128)(2,1)}, bf16[528,128]{1,0:T(8,128)(2,1)S(1)}, u32[]{:S(2)}, u32[]{:S(2)}) %collective-permute-start.2) | collective-permute-done | bytes 135200 | tf_op jit(solution)/shard_map/ppermute | solution.py:463
  15.1 7.1 %collective-permute-done.4.refs_5_ = bf16[528,128]{1,0:T(8,128)(2,1)S(1)} collective-permute-done((bf16[528,128]{1,0:T(8,128)(2,1)}, bf16[528,128]{1,0:T(8,128)(2,1)S(1)}, u32[]{:S(2)}, u32[]{:S(2)}) %collective-permute-start.4) | collective-permute-done | bytes 135200 | tf_op jit(solution)/shard_map/ppermute | solution.py:463
  22.1 0.0 collective-permute-done.5.refs_6_
  22.1 0.0 collective-permute-done.6.refs_7_
  22.1 0.9 %copy-done.1 = bf16[528,128]{1,0:T(8,128)(2,1)S(1)} copy-done((bf16[528,128]{1,0:T(8,128)(2,1)S(1)}, bf16[528,128]{1,0:T(8,128)(2,1)}, u32[]{:S(2)}) %copy-start.1) | copy-done | bytes 135192
  23.0 2.8 %shard_map.86 = (bf16[832,128]{1,0:T(8,128)(2,1)S(1)}, bf16[832,128]{1,0:T(8,128)(2,1)S(1)}, bf16[832,128]{1,0:T(8,128)(2,1)S(1)}, bf16[832,128]{1,0:T(8,128)(2,1)S(1)}, s32[8,1,192]{2,1,0:T(1,128)S(1)}) custom-call(bf16[528,128]{1,0:T(8,128)(2,1)S(1)} %copy-done.1, bf16[528,128]{1,0:T(8,128)(2,1)S(1)} %collective-permute-done.refs_1_, ...), custom_call_target="tpu_custom_call" | custom-call | tf_op jit(solution)/shard_map/pallas_call | solution.py:241
  25.9 1.9 %collective-permute-start.10 = (bf16[832,128]{1,0:T(8,128)(2,1)S(1)}, bf16[832,128]{1,0:T(8,128)(2,1)S(1)}, u32[]{:S(2)}, u32[]{:S(2)}) collective-permute-start(bf16[832,128]{1,0:T(8,128)(2,1)S(1)} %get-tuple-element.36), channel_id=1, source_target_pairs={{0,4},{1,5},{2,6},{3,7},{4,0},{5,1},{6,2},{7,3},{8,12},{9,13},{10,... | collective-permute-start | bytes 638984 | tf_op jit(solution)/shard_map/ppermute | solution.py:463
  27.7 1.4 %collective-permute-start.12 = (bf16[832,128]{1,0:T(8,128)(2,1)S(1)}, bf16[832,128]{1,0:T(8,128)(2,1)S(1)}, u32[]{:S(2)}, u32[]{:S(2)}) collective-permute-start(bf16[832,128]{1,0:T(8,128)(2,1)S(1)} %get-tuple-element.37), channel_id=1, source_target_pairs={{0,6},{1,7},{2,4},{3,5},{4,2},{5,3},{6,0},{7,1},{8,14},{9,15},{10,... | collective-permute-start | bytes 638984 | tf_op jit(solution)/shard_map/ppermute | solution.py:463
  29.2 0.3 collective-permute-start.8
  29.4 8.7 %collective-permute-done.10.refs_4_ = bf16[832,128]{1,0:T(8,128)(2,1)S(1)} collective-permute-done((bf16[832,128]{1,0:T(8,128)(2,1)S(1)}, bf16[832,128]{1,0:T(8,128)(2,1)S(1)}, u32[]{:S(2)}, u32[]{:S(2)}) %collective-permute-start.10) | collective-permute-done | bytes 213024 | tf_op jit(solution)/shard_map/ppermute | solution.py:463
  38.1 0.0 collective-permute-start.11
  38.1 0.0 collective-permute-done.12.refs_6_
  38.1 0.5 collective-permute-start.13
  38.6 0.8 %collective-permute-done.8.refs_2_ = bf16[832,128]{1,0:T(8,128)(2,1)S(1)} collective-permute-done((bf16[832,128]{1,0:T(8,128)(2,1)S(1)}, bf16[832,128]{1,0:T(8,128)(2,1)S(1)}, u32[]{:S(2)}, u32[]{:S(2)}) %collective-permute-start.8) | collective-permute-done | bytes 213024 | tf_op jit(solution)/shard_map/ppermute | solution.py:463
  39.4 0.8 %shard_map.88.placed_ref = bf16[128,512]{1,0:T(8,128)(2,1)S(1)} custom-call(s32[8,1,192]{2,1,0:T(1,128)S(1)} %get-tuple-element.40.target_ref, bf16[528,128]{1,0:T(8,128)(2,1)S(1)} %copy-done.1, bf16[528,128]{1,0:T(8,128)(2,1)S(1)} %collective-permute-done.refs_1_, bf16[528,128]{1,0:T(8,128)(2,1)S(1)} %collective-permute-done.1.refs_2_, ...), custom_call_target="tpu_custom_call" | custom-call | tf_op jit(solution)/shard_map/pallas_call | solution.py:241
  40.2 0.7 %collective-permute-done.9.refs_3_ = bf16[832,128]{1,0:T(8,128)(2,1)S(1)} collective-permute-done((bf16[832,128]{1,0:T(8,128)(2,1)S(1)}, bf16[832,128]{1,0:T(8,128)(2,1)S(1)}, u32[]{:S(2)}, u32[]{:S(2)}) %collective-permute-start.9) | collective-permute-done | bytes 213024 | tf_op jit(solution)/shard_map/ppermute | solution.py:463
  40.9 1.0 %shard_map.89 = (bf16[128,384]{1,0:T(8,128)(2,1)S(1)}, bf16[128,384]{1,0:T(8,128)(2,1)S(1)}, bf16[128,384]{1,0:T(8,128)(2,1)S(1)}, bf16[128,384]{1,0:T(8,128)(2,1)S(1)}) custom-call(bf16[128,512]{1,0:T(8,128)(2,1)S(1)} %shard_map.88.placed_ref, bf16[832,128]{1,0:T(8,128)(2,1)S(1)} %get-tuple-element.34.refs_0_, ...), custom_call_target="tpu_custom_call" | custom-call | tf_op jit(solution)/shard_map/pallas_call | solution.py:241
  41.9 1.8 %collective-permute-start.14 = (bf16[128,384]{1,0:T(8,128)(2,1)S(1)}, bf16[128,384]{1,0:T(8,128)(2,1)S(1)}, u32[]{:S(2)}, u32[]{:S(2)}) collective-permute-start(bf16[128,384]{1,0:T(8,128)(2,1)S(1)} %get-tuple-element.42), channel_id=1, source_target_pairs={{0,8},{8,0},{16,24},{24,16},{1,9},{9,1},{17,25},{25,17},{2,10},{10... | collective-permute-start | bytes 294920 | tf_op jit(solution)/shard_map/ppermute | solution.py:463
  43.7 2.6 %collective-permute-start.15 = (bf16[128,384]{1,0:T(8,128)(2,1)S(1)}, bf16[128,384]{1,0:T(8,128)(2,1)S(1)}, u32[]{:S(2)}, u32[]{:S(2)}) collective-permute-start(bf16[128,384]{1,0:T(8,128)(2,1)S(1)} %get-tuple-element.43), channel_id=1, source_target_pairs={{0,16},{8,24},{16,0},{24,8},{1,17},{9,25},{17,1},{25,9},{2,18},{10... | collective-permute-start | bytes 294920 | tf_op jit(solution)/shard_map/ppermute | solution.py:463
  46.3 0.0 collective-permute-start.16
  46.3 3.3 %shard_map.87 = (bf16[196,1024]{1,0:T(8,128)(2,1)}, bf16[64,512]{1,0:T(8,128)(2,1)}) custom-call(s32[1,196]{1,0:T(1,128)S(1)} %copy-done.3, s32[1,192]{1,0:T(1,128)S(1)} %copy-done.2, bf16[1024,1536]{1,0:T(8,128)(2,1)S(1)} %copy-done, bf16[832,128]{1,0:T(8,128)(2,1)S(1)} %get-tuple-element.34.refs_0_, bf16[832,128]{1,0:T(8,128)(2,1)S(1)} %collective-permute-done.7.refs_1_, ...), custom_call_target="tpu_custom_call" | custom-call | tf_op jit(solution)/shard_map/pallas_call | solution.py:241
  49.6 4.8 %collective-permute-done.15.refs_2_ = bf16[128,384]{1,0:T(8,128)(2,1)S(1)} collective-permute-done((bf16[128,384]{1,0:T(8,128)(2,1)S(1)}, bf16[128,384]{1,0:T(8,128)(2,1)S(1)}, u32[]{:S(2)}, u32[]{:S(2)}) %collective-permute-start.15) | collective-permute-done | bytes 98336 | tf_op jit(solution)/shard_map/ppermute | solution.py:463
  54.4 0.7 %shard_map.90 = f32[128,384]{1,0:T(8,128)} custom-call(bf16[128,384]{1,0:T(8,128)(2,1)S(1)} %get-tuple-element.41.refs_0_, bf16[128,384]{1,0:T(8,128)(2,1)S(1)} %collective-permute-done.14.refs_1_, bf16[128,384]{1,0:T(8,128)(2,1)S(1)} %collective-permute-done.15.refs_2_, bf16[128,384]{1,0:T(8,128)(2,1)S(1)} %collective-permute-done.16.refs_3_), custom_call_target="tpu_custom_call" | custom-call | tf_op jit(solution)/shard_map/pallas_call | solution.py:241
  (16 shorter events, 0.0 us)
Async XLA Ops:
  0.6 45.7 %copy-start = (bf16[1024,1536]{1,0:T(8,128)(2,1)S(1)}, bf16[1024,1536]{1,0:T(8,128)(2,1)}, u32[]{:S(2)}) copy-start(bf16[1024,1536]{1,0:T(8,128)(2,1)} %w_ref.1) | copy-start | bytes 9437188
  4.8 41.5 %copy-start.2 = (s32[1,192]{1,0:T(1,128)S(1)}, s32[1,192]{1,0:T(1,128)}, u32[]{:S(2)}) copy-start(s32[1,192]{1,0:T(1,128)} %get-tuple-element.25.target_ref) | copy-start | bytes 2308
  4.9 41.5 %copy-start.3 = (s32[1,196]{1,0:T(1,128)S(1)}, s32[1,196]{1,0:T(1,128)}, u32[]{:S(2)}) copy-start(s32[1,196]{1,0:T(1,128)} %get-tuple-element.24.segment_ref) | copy-start | bytes 2356
  4.9 4.9 %collective-permute-start = (bf16[528,128]{1,0:T(8,128)(2,1)}, bf16[528,128]{1,0:T(8,128)(2,1)S(1)}, u32[]{:S(2)}, u32[]{:S(2)}) collective-permute-start(bf16[528,128]{1,0:T(8,128)(2,1)} %get-tuple-element.27), channel_id=1, source_target_pairs={{0,1},{1,0},{2,3},{3,2},{4,5},{5,4},{6,7},{7,6},{8,9},{9,8},{10,11... | collective-permute-start | bytes 405512 | tf_op jit(solution)/shard_map/ppermute | solution.py:463
  5.4 7.2 %collective-permute-start.1 = (bf16[528,128]{1,0:T(8,128)(2,1)}, bf16[528,128]{1,0:T(8,128)(2,1)S(1)}, u32[]{:S(2)}, u32[]{:S(2)}) collective-permute-start(bf16[528,128]{1,0:T(8,128)(2,1)} %get-tuple-element.28), channel_id=1, source_target_pairs={{0,2},{1,3},{2,0},{3,1},{4,6},{5,7},{6,4},{7,5},{8,10},{9,11},{10,... | collective-permute-start | bytes 405512 | tf_op jit(solution)/shard_map/ppermute | solution.py:463
  7.9 7.1 %collective-permute-start.2 = (bf16[528,128]{1,0:T(8,128)(2,1)}, bf16[528,128]{1,0:T(8,128)(2,1)S(1)}, u32[]{:S(2)}, u32[]{:S(2)}) collective-permute-start(bf16[528,128]{1,0:T(8,128)(2,1)} %get-tuple-element.29), channel_id=1, source_target_pairs={{0,3},{1,2},{2,1},{3,0},{4,7},{5,6},{6,5},{7,4},{8,11},{9,10},{10,... | collective-permute-start | bytes 405512 | tf_op jit(solution)/shard_map/ppermute | solution.py:463
  8.0 7.0 %collective-permute-start.3 = (bf16[528,128]{1,0:T(8,128)(2,1)}, bf16[528,128]{1,0:T(8,128)(2,1)S(1)}, u32[]{:S(2)}, u32[]{:S(2)}) collective-permute-start(bf16[528,128]{1,0:T(8,128)(2,1)} %get-tuple-element.30), channel_id=1, source_target_pairs={{0,4},{1,5},{2,6},{3,7},{4,0},{5,1},{6,2},{7,3},{8,12},{9,13},{10,... | collective-permute-start | bytes 405512 | tf_op jit(solution)/shard_map/ppermute | solution.py:463
  9.8 12.3 %collective-permute-start.4 = (bf16[528,128]{1,0:T(8,128)(2,1)}, bf16[528,128]{1,0:T(8,128)(2,1)S(1)}, u32[]{:S(2)}, u32[]{:S(2)}) collective-permute-start(bf16[528,128]{1,0:T(8,128)(2,1)} %get-tuple-element.31), channel_id=1, source_target_pairs={{0,5},{1,4},{2,7},{3,6},{4,1},{5,0},{6,3},{7,2},{8,13},{9,12},{10,... | collective-permute-start | bytes 405512 | tf_op jit(solution)/shard_map/ppermute | solution.py:463
  9.8 12.3 %collective-permute-start.5 = (bf16[528,128]{1,0:T(8,128)(2,1)}, bf16[528,128]{1,0:T(8,128)(2,1)S(1)}, u32[]{:S(2)}, u32[]{:S(2)}) collective-permute-start(bf16[528,128]{1,0:T(8,128)(2,1)} %get-tuple-element.32), channel_id=1, source_target_pairs={{0,6},{1,7},{2,4},{3,5},{4,2},{5,3},{6,0},{7,1},{8,14},{9,15},{10,... | collective-permute-start | bytes 405512 | tf_op jit(solution)/shard_map/ppermute | solution.py:463
  12.6 9.5 %collective-permute-start.6 = (bf16[528,128]{1,0:T(8,128)(2,1)}, bf16[528,128]{1,0:T(8,128)(2,1)S(1)}, u32[]{:S(2)}, u32[]{:S(2)}) collective-permute-start(bf16[528,128]{1,0:T(8,128)(2,1)} %get-tuple-element.33), channel_id=1, source_target_pairs={{0,7},{1,6},{2,5},{3,4},{4,3},{5,2},{6,1},{7,0},{8,15},{9,14},{10,... | collective-permute-start | bytes 405512 | tf_op jit(solution)/shard_map/ppermute | solution.py:463
  22.1 0.9 %copy-start.1 = (bf16[528,128]{1,0:T(8,128)(2,1)S(1)}, bf16[528,128]{1,0:T(8,128)(2,1)}, u32[]{:S(2)}) copy-start(bf16[528,128]{1,0:T(8,128)(2,1)} %get-tuple-element.26.refs_0_) | copy-start | bytes 405508
  25.9 12.2 %collective-permute-start.10 = (bf16[832,128]{1,0:T(8,128)(2,1)S(1)}, bf16[832,128]{1,0:T(8,128)(2,1)S(1)}, u32[]{:S(2)}, u32[]{:S(2)}) collective-permute-start(bf16[832,128]{1,0:T(8,128)(2,1)S(1)} %get-tuple-element.36), channel_id=1, source_target_pairs={{0,4},{1,5},{2,6},{3,7},{4,0},{5,1},{6,2},{7,3},{8,12},{9,13},{10,... | collective-permute-start | bytes 638984 | tf_op jit(solution)/shard_map/ppermute | solution.py:463
  27.7 10.4 %collective-permute-start.12 = (bf16[832,128]{1,0:T(8,128)(2,1)S(1)}, bf16[832,128]{1,0:T(8,128)(2,1)S(1)}, u32[]{:S(2)}, u32[]{:S(2)}) collective-permute-start(bf16[832,128]{1,0:T(8,128)(2,1)S(1)} %get-tuple-element.37), channel_id=1, source_target_pairs={{0,6},{1,7},{2,4},{3,5},{4,2},{5,3},{6,0},{7,1},{8,14},{9,15},{10,... | collective-permute-start | bytes 638984 | tf_op jit(solution)/shard_map/ppermute | solution.py:463
  29.2 10.2 %collective-permute-start.8 = (bf16[832,128]{1,0:T(8,128)(2,1)S(1)}, bf16[832,128]{1,0:T(8,128)(2,1)S(1)}, u32[]{:S(2)}, u32[]{:S(2)}) collective-permute-start(bf16[832,128]{1,0:T(8,128)(2,1)S(1)} %get-tuple-element.35), channel_id=1, source_target_pairs={{0,2},{1,3},{2,0},{3,1},{4,6},{5,7},{6,4},{7,5},{8,10},{9,11},{10,... | collective-permute-start | bytes 638984 | tf_op jit(solution)/shard_map/ppermute | solution.py:463
  29.4 10.8 %collective-permute-start.7 = (bf16[832,128]{1,0:T(8,128)(2,1)S(1)}, bf16[832,128]{1,0:T(8,128)(2,1)S(1)}, u32[]{:S(2)}, u32[]{:S(2)}) collective-permute-start(bf16[832,128]{1,0:T(8,128)(2,1)S(1)} %get-tuple-element.34.refs_0_), channel_id=1, source_target_pairs={{0,1},{1,0},{2,3},{3,2},{4,5},{5,4},{6,7},{7,6},{8,9},{9,8},{10,11... | collective-permute-start | bytes 638984 | tf_op jit(solution)/shard_map/ppermute | solution.py:463
  38.1 2.1 %collective-permute-start.11 = (bf16[832,128]{1,0:T(8,128)(2,1)S(1)}, bf16[832,128]{1,0:T(8,128)(2,1)S(1)}, u32[]{:S(2)}, u32[]{:S(2)}) collective-permute-start(bf16[832,128]{1,0:T(8,128)(2,1)S(1)} %collective-permute-done.10.refs_4_), channel_id=1, source_target_pairs={{0,1},{1,0},{2,3},{3,2},{4,5},{5,4},{6,7},{7,6},{8,9},{9,8},{10,11... | collective-permute-start | bytes 638984 | tf_op jit(solution)/shard_map/ppermute | solution.py:463
  38.1 2.1 %collective-permute-start.13 = (bf16[832,128]{1,0:T(8,128)(2,1)S(1)}, bf16[832,128]{1,0:T(8,128)(2,1)S(1)}, u32[]{:S(2)}, u32[]{:S(2)}) collective-permute-start(bf16[832,128]{1,0:T(8,128)(2,1)S(1)} %collective-permute-done.12.refs_6_), channel_id=1, source_target_pairs={{0,1},{1,0},{2,3},{3,2},{4,5},{5,4},{6,7},{7,6},{8,9},{9,8},{10,11... | collective-permute-start | bytes 638984 | tf_op jit(solution)/shard_map/ppermute | solution.py:463
  39.4 1.5 %collective-permute-start.9 = (bf16[832,128]{1,0:T(8,128)(2,1)S(1)}, bf16[832,128]{1,0:T(8,128)(2,1)S(1)}, u32[]{:S(2)}, u32[]{:S(2)}) collective-permute-start(bf16[832,128]{1,0:T(8,128)(2,1)S(1)} %collective-permute-done.8.refs_2_), channel_id=1, source_target_pairs={{0,1},{1,0},{2,3},{3,2},{4,5},{5,4},{6,7},{7,6},{8,9},{9,8},{10,11... | collective-permute-start | bytes 638984 | tf_op jit(solution)/shard_map/ppermute | solution.py:463
  41.9 7.7 %collective-permute-start.14 = (bf16[128,384]{1,0:T(8,128)(2,1)S(1)}, bf16[128,384]{1,0:T(8,128)(2,1)S(1)}, u32[]{:S(2)}, u32[]{:S(2)}) collective-permute-start(bf16[128,384]{1,0:T(8,128)(2,1)S(1)} %get-tuple-element.42), channel_id=1, source_target_pairs={{0,8},{8,0},{16,24},{24,16},{1,9},{9,1},{17,25},{25,17},{2,10},{10... | collective-permute-start | bytes 294920 | tf_op jit(solution)/shard_map/ppermute | solution.py:463
  43.7 10.7 %collective-permute-start.15 = (bf16[128,384]{1,0:T(8,128)(2,1)S(1)}, bf16[128,384]{1,0:T(8,128)(2,1)S(1)}, u32[]{:S(2)}, u32[]{:S(2)}) collective-permute-start(bf16[128,384]{1,0:T(8,128)(2,1)S(1)} %get-tuple-element.43), channel_id=1, source_target_pairs={{0,16},{8,24},{16,0},{24,8},{1,17},{9,25},{17,1},{25,9},{2,18},{10... | collective-permute-start | bytes 294920 | tf_op jit(solution)/shard_map/ppermute | solution.py:463
  46.3 8.1 %collective-permute-start.16 = (bf16[128,384]{1,0:T(8,128)(2,1)S(1)}, bf16[128,384]{1,0:T(8,128)(2,1)S(1)}, u32[]{:S(2)}, u32[]{:S(2)}) collective-permute-start(bf16[128,384]{1,0:T(8,128)(2,1)S(1)} %get-tuple-element.44), channel_id=1, source_target_pairs={{0,24},{8,16},{16,8},{24,0},{1,25},{9,17},{17,9},{25,1},{2,26},{10... | collective-permute-start | bytes 294920 | tf_op jit(solution)/shard_map/ppermute | solution.py:463

commit v3 on v2

--- a/solution.py
+++ b/solution.py
@@ -1,3 +1,5 @@
+import functools
+
 import jax
 import jax.numpy as jnp
 from jax import lax
@@ -237,11 +239,12 @@
     return lax.dot_general(left, right, dims, preferred_element_type=jnp.float32)
 
 
-def call(body, outs, *args, scratch=(), space=pltpu.VMEM, limit=VMEM_LIMIT):
+def call(body, outs, *args, scratch=(), space=None, limit=VMEM_LIMIT):
+    space = space or [pltpu.VMEM] * len(args)
     return pl.pallas_call(
         body,
         out_shape=outs,
-        in_specs=[pl.BlockSpec(memory_space=space)] * len(args),
+        in_specs=[pl.BlockSpec(memory_space=each) for each in space],
         scratch_shapes=scratch,
         compiler_params=pltpu.CompilerParams(vmem_limit_bytes=limit),
     )(*args)
@@ -272,13 +275,17 @@
     sources, refs = refs[:6], refs[6:]
     sends, refs = refs[:HEADS], refs[HEADS:]
     (target_ref, segment_out, held_ref), refs = refs[:3], refs[3:]
+    segment_ref, patch_ref, shard_ref, slot_ref, grad_ref, w_ref, done = refs
+    pairs = list(zip(sources, refs))[:-1]
+    for part in range(3):
+        columns = pl.ds(part * grad_ref.shape[1], grad_ref.shape[1])
+        pairs.append((sources[5].at[:, columns], w_ref.at[part]))
     copies = [
-        pltpu.make_async_copy(source, held, refs[6].at[index])
-        for index, (source, held) in enumerate(zip(sources, refs))
+        pltpu.make_async_copy(source, held, done.at[index])
+        for index, (source, held) in enumerate(pairs)
     ]
     for copy in copies:
         copy.start()
-    segment_ref, patch_ref, shard_ref, slot_ref, grad_ref, w_ref = refs[:6]
     token_cap = shard_ref.shape[1]
     local_rows, inner = grad_ref.shape
     devices = len(sends)
@@ -304,24 +311,26 @@
         jnp.where(line == 1, shard_high, jnp.where(line == 2, slot_low, slot_high)),
     ).astype(jnp.bfloat16)
     grads = grad_ref[...]
-    copies[5].wait()
-    projected = dot(tokens, w_ref[...]).astype(jnp.bfloat16)
+    half = token_cap + token_cap // 2
     for head in range(devices):
         first = head * HEAD_DIM
-        query, key, value = (
-            projected[:, part * inner + first : part * inner + first + HEAD_DIM]
-            for part in range(3)
-        )
-        start = 0
+        start = half
         for piece in (
-            jnp.concatenate([query, key], axis=1),
-            fold_half(value),
             where_to,
             fold_half(grads[:, first : first + HEAD_DIM]),
             tokens[:, head * width : (head + 1) * width],
         ):
             held_ref[head, start : start + piece.shape[0]] = piece
             start += piece.shape[0]
+    for part, copy in enumerate(copies[5:]):
+        copy.wait()
+        projected = dot(tokens, w_ref[part]).astype(jnp.bfloat16)
+        for head in range(devices):
+            rows = projected[:, head * HEAD_DIM : (head + 1) * HEAD_DIM]
+            if part < 2:
+                held_ref[head, :token_cap, part * HEAD_DIM : (part + 1) * HEAD_DIM] = rows
+            else:
+                held_ref[head, token_cap:half] = fold_half(rows)
     me = lax.axis_index("seq")
     for flip, send in enumerate(sends):
         send[...] = held_ref[jnp.bitwise_xor(me, flip)]
@@ -334,7 +343,7 @@
     return (shard * local_rows + slot).astype(jnp.int32)
 
 
-def head_kernel(token_cap, *refs):
+def head_kernel(token_cap, flips, *refs):
     pieces, refs = refs[:HEADS], refs[HEADS:]
     outs, (target_ref, grad_ref, attended_ref) = refs[: HEADS // 2], refs[HEADS // 2 :]
     devices, local_rows = len(pieces), grad_ref.shape[1]
@@ -345,7 +354,7 @@
     row_id = lax.broadcasted_iota(jnp.int32, (rows, token_cap), 0)
     total = jnp.zeros((rows, 3 * HEAD_DIM), jnp.float32)
     me = lax.axis_index("seq")
-    for flip, piece in enumerate(pieces):
+    for flip, piece in zip(flips, pieces):
         sender = jnp.bitwise_xor(me, flip)
         target = target_row(piece[lines_at : lines_at + 16], token_cap, local_rows)
         target_ref[sender] = target
@@ -385,24 +394,24 @@
             out[first : first + local_rows // 2] = attended_ref[place]
 
 
-def block_kernel(target_ref, *refs):
+def block_kernel(flips, target_ref, *refs):
     pieces, placed_ref = refs[:-1], refs[-1]
     token_cap = target_ref.shape[2]
     width, rows = placed_ref.shape
     row_id = lax.broadcasted_iota(jnp.int32, (rows, token_cap), 0)
     total = jnp.zeros((rows, width), jnp.float32)
     me = lax.axis_index("seq")
-    for flip, piece in enumerate(pieces):
+    for flip, piece in zip(flips, pieces):
         target = target_ref[jnp.bitwise_xor(me, flip)]
         total = total + dot(one_hot(row_id == target), piece[piece.shape[0] - token_cap :])
     placed_ref[...] = total.T.astype(jnp.bfloat16)
 
 
-def by_column(left, pieces, held_ref):
+def by_column(left, flips, pieces, held_ref):
     rows = left.shape[1]
     half, end = rows // 2, rows + rows // 2
     me = lax.axis_index("seq")
-    for flip, piece in enumerate(pieces):
+    for flip, piece in zip(flips, pieces):
         both = dot(left, piece[:rows])
         low = dot(left[:, :half], piece[rows:end])
         high = dot(left[:, half:], piece[rows:end])
@@ -418,9 +427,9 @@
     )
 
 
-def weight_kernel(placed_ref, *refs):
+def weight_kernel(flips, placed_ref, *refs):
     pieces, outs, (held_ref, block_ref) = refs[:HEADS], refs[HEADS:-2], refs[-2:]
-    columns = by_column(placed_ref[...], pieces, held_ref).astype(jnp.bfloat16)
+    columns = by_column(placed_ref[...], flips, pieces, held_ref).astype(jnp.bfloat16)
     width = columns.shape[1] // len(outs)
     me = lax.axis_index("clip")
     for index in range(len(outs)):
@@ -429,19 +438,22 @@
         out[...] = block_ref[jnp.bitwise_xor(me, flip)]
 
 
-def patch_kernel(segment_ref, target_ref, w_ref, *refs):
-    pieces, (patch_ref, attended_ref, held_ref, part_ref) = refs[:HEADS], refs[HEADS:]
+def patch_kernel(flips, segment_ref, target_ref, w_hbm, *refs):
+    pieces, (patch_ref, attended_ref, held_ref, part_ref, w_ref, done) = refs[:HEADS], refs[HEADS:]
+    copy = pltpu.make_async_copy(w_hbm, w_ref, done)
+    copy.start()
     token_cap = target_ref.shape[1]
     local_rows = attended_ref.shape[0]
     rows = HEADS * local_rows
     me = lax.axis_index("seq")
-    for flip, piece in enumerate(pieces):
+    for flip, piece in zip(flips, pieces):
         first = rows + rows // 2 + flip % 2 * local_rows // 2
         part_ref[jnp.bitwise_xor(me, flip)] = unfold_half(piece[first : first + local_rows // 2])
     attended_ref[...] = jnp.concatenate([part_ref[head] for head in range(HEADS)], axis=1)
     row_id = lax.broadcasted_iota(jnp.int32, (rows, token_cap), 0)
     chooser = jnp.where(row_id == target_ref[...], 1.0, 0.0).T.astype(jnp.bfloat16)
-    proj_grad = by_column(chooser, pieces, held_ref).astype(jnp.bfloat16)
+    proj_grad = by_column(chooser, flips, pieces, held_ref).astype(jnp.bfloat16)
+    copy.wait()
     token_grad = dot(proj_grad, w_ref[...], NT).astype(jnp.bfloat16).astype(jnp.float32)
     member = (
         lax.broadcasted_iota(jnp.int32, (token_cap, segment_ref.shape[1]), 0) == segment_ref[...]
@@ -449,6 +461,10 @@
     counts = jnp.sum(jnp.where(member, 1.0, 0.0), axis=1, keepdims=True)
     shared = (token_grad / jnp.maximum(counts, 1.0)).astype(jnp.bfloat16)
     patch_ref[...] = dot(one_hot(member), shared, TN).astype(jnp.bfloat16)
+
+
+def copy_kernel(source_ref, target_ref):
+    target_ref[...] = source_ref[...]
 
 
 def sum_kernel(*refs):
@@ -485,18 +501,23 @@
         scratch=[
             pltpu.VMEM((devices, sent, 2 * HEAD_DIM), jnp.bfloat16),
         ]
-        + [pltpu.VMEM(source.shape, source.dtype) for source in sources]
-        + [pltpu.SemaphoreType.DMA((len(sources),))],
-        space=pltpu.HBM,
-        limit=60 * 1024 * 1024,
-    )
-    sends, (target, segment) = outs[:devices], outs[devices:]
-    far_first = sorted(range(1, devices), key=lambda flip: (-(flip // 2).bit_count(), flip))
-    came = [sends[0]] + [None] * (devices - 1)
-    for flip in far_first:
+        + [pltpu.VMEM(source.shape, source.dtype) for source in sources[:-1]]
+        + [
+            pltpu.VMEM((3, model, inner), w_qkv.dtype),
+            pltpu.SemaphoreType.DMA((len(sources) + 2,)),
+        ],
+        space=[pltpu.HBM] * len(sources),
+        limit=62 * 1024 * 1024,
+    )
+    sends, (target, segment) = list(outs[:devices]), outs[devices:]
+    order = [0] + sorted(range(1, devices), key=lambda flip: (-(flip // 2).bit_count(), flip))
+    sends[0] = call(copy_kernel, shape(sent, 2 * HEAD_DIM), sends[0])
+    came = {0: sends[0]}
+    for flip in order[1:]:
         came[flip] = exchange(sends[flip], "seq", flip)
+    came = [came[flip] for flip in order]
     *proj, targets = call(
-        lambda *refs: head_kernel(token_cap, *refs),
+        functools.partial(head_kernel, token_cap, order),
         [shape(rows + rows // 2 + local_rows, 2 * HEAD_DIM)] * (devices // 2)
         + [shape(devices, 1, token_cap, dtype=jnp.int32)],
         *came,
@@ -505,15 +526,19 @@
             pltpu.VMEM((devices, local_rows // 2, 2 * HEAD_DIM), jnp.bfloat16),
         ],
     )
-    pieces = [proj[0]] + [None] * (devices - 1)
-    for flip in far_first:
+    pieces = {0: proj[0]}
+    for flip in order[1:]:
         if flip % 2 == 0:
             pieces[flip] = exchange(proj[flip // 2], "seq", flip)
-    for flip in range(1, devices, 2):
-        pieces[flip] = exchange(pieces[flip - 1], "seq", 1)
-    placed = call(block_kernel, shape(width, rows), targets, *came)
+    for flip in list(pieces):
+        pieces[flip + 1] = exchange(pieces[flip], "seq", 1)
+    flips = order
+    pieces = [pieces[flip] for flip in flips]
+    placed = call(
+        functools.partial(block_kernel, order), shape(width, rows), targets, *came
+    )
     weights = call(
-        weight_kernel,
+        functools.partial(weight_kernel, flips),
         [shape(width, 3 * inner // clips)] * clips,
         placed,
         *pieces,
@@ -522,9 +547,9 @@
             pltpu.VMEM((clips, width, 3 * inner // clips), jnp.bfloat16),
         ],
     )
-    weights = [weights[0]] + [exchange(weights[flip], "clip", flip) for flip in range(1, clips)]
+    weights = [weights[0]] + [exchange(weights[flip], "clip", flip) for flip in range(clips - 1, 0, -1)]
     patch_grad, attended = call(
-        patch_kernel,
+        functools.partial(patch_kernel, flips),
         [shape(patches.shape[1], model), shape(local_rows, inner)],
         segment,
         target,
@@ -533,7 +558,10 @@
         scratch=[
             pltpu.VMEM((devices, token_cap, 3 * HEAD_DIM), jnp.float32),
             pltpu.VMEM((devices, local_rows, HEAD_DIM), jnp.bfloat16),
+            pltpu.VMEM(w_qkv.shape, w_qkv.dtype),
+            pltpu.SemaphoreType.DMA(()),
         ],
+        space=[pltpu.VMEM] * 2 + [pltpu.HBM] + [pltpu.VMEM] * devices,
     )
     weight_grad = call(
         sum_kernel, shape(width, 3 * inner // clips, dtype=jnp.float32), *weights

time: 55.2 us -> 53.1 us (0.962)
  starting transfers between devices: 17.8 us -> 15.9 us
  waiting for transfers between devices: 23 us -> 22.4 us
    ppermute x17, starting transfers between devices: 17.8 us -> 15.9 us  [exchange(): lax.ppermute(rows, axis, [(index, index ^ flip) for index in range(count)])]
    ppermute x17, waiting for transfers between devices: 23 us -> 22.4 us  [exchange(): lax.ppermute(rows, axis, [(index, index ^ flip) for index in range(count)])]
    pallas_call x6 -> x7, Pallas kernels: 12.7 us -> 12.9 us  [call(): pl.pallas_call(body, out_shape=outs, in_specs=[pl.BlockSpec(memory_space=...]
  transfers between devices with their start and end apart: 17 -> 17, of which waited for: 7 -> 10; matrix products, arithmetic and copies ran while one was open for 0% -> 0% of each run, Pallas kernels for 7% -> 8%
where the time goes in v3:
time: 53.1 us; the launch traced here: 52.9 us
  waiting for transfers between devices  22.4 us (42%)
  starting transfers between devices  15.9 us (30%)
  Pallas kernels  12.9 us (24%)
  local copies, waits for them, and re-layouts  0.92 us (2%)
  between operations  0.72 us (1%)
    ppermute x17, waiting for transfers between devices, exchange(): lax.ppermute(rows, axis, [(index, index ^ flip) for index in range(count)])  22.4 us
    ppermute x17, starting transfers between devices, exchange(): lax.ppermute(rows, axis, [(index, index ^ flip) for index in range(count)])  15.9 us
    pallas_call x7, Pallas kernels, call(): pl.pallas_call(body, out_shape=outs, in_specs=[pl.BlockSpec(memory_space=...  12.9 us
  transfers between devices with their start and end apart: 17, of which 10 were waited for; matrix products, arithmetic and copies ran while one was open for 0% of the time, Pallas kernels for 8%

profile of v3, /device:TPU:0, one launch (start us, length us, event | category | flops | bytes accessed | tf_op | source)
XLA Modules:
  0.0 52.9 jit_solution(16747366100675632020)
XLA Ops:
  0.6 3.9 %shard_map.85 = (bf16[528,128]{1,0:T(8,128)(2,1)}, bf16[528,128]{1,0:T(8,128)(2,1)}, bf16[528,128]{1,0:T(8,128)(2,1)}, bf16[528,128]{1,0:T(8,128)(2,1)}, bf16[52...) custom-call(s32[1,196]{1,0:T(1,128)} %refs_0_.1, ...), custom_call_target="tpu_custom_call" | custom-call | tf_op jit(solution)/shard_map/pallas_call | solution.py:244
  4.6 0.0 copy-start
  4.6 4.0 %collective-permute-start = (bf16[528,128]{1,0:T(8,128)(2,1)}, bf16[528,128]{1,0:T(8,128)(2,1)S(1)}, u32[]{:S(2)}, u32[]{:S(2)}) collective-permute-start(bf16[528,128]{1,0:T(8,128)(2,1)} %get-tuple-element.27), channel_id=1, source_target_pairs={{0,6},{1,7},{2,4},{3,5},{4,2},{5,3},{6,0},{7,1},{8,14},{9,15},{10,... | collective-permute-start | bytes 405512 | tf_op jit(solution)/shard_map/ppermute | solution.py:479
  8.6 0.0 collective-permute-start.1
  8.6 1.1 %collective-permute-start.2 = (bf16[528,128]{1,0:T(8,128)(2,1)}, bf16[528,128]{1,0:T(8,128)(2,1)S(1)}, u32[]{:S(2)}, u32[]{:S(2)}) collective-permute-start(bf16[528,128]{1,0:T(8,128)(2,1)} %get-tuple-element.29), channel_id=1, source_target_pairs={{0,2},{1,3},{2,0},{3,1},{4,6},{5,7},{6,4},{7,5},{8,10},{9,11},{10,... | collective-permute-start | bytes 405512 | tf_op jit(solution)/shard_map/ppermute | solution.py:479
  9.7 0.6 %collective-permute-start.3 = (bf16[528,128]{1,0:T(8,128)(2,1)}, bf16[528,128]{1,0:T(8,128)(2,1)S(1)}, u32[]{:S(2)}, u32[]{:S(2)}) collective-permute-start(bf16[528,128]{1,0:T(8,128)(2,1)} %get-tuple-element.30), channel_id=1, source_target_pairs={{0,3},{1,2},{2,1},{3,0},{4,7},{5,6},{6,5},{7,4},{8,11},{9,10},{10,... | collective-permute-start | bytes 405512 | tf_op jit(solution)/shard_map/ppermute | solution.py:479
  10.3 1.7 %collective-permute-start.4 = (bf16[528,128]{1,0:T(8,128)(2,1)}, bf16[528,128]{1,0:T(8,128)(2,1)S(1)}, u32[]{:S(2)}, u32[]{:S(2)}) collective-permute-start(bf16[528,128]{1,0:T(8,128)(2,1)} %get-tuple-element.31), channel_id=1, source_target_pairs={{0,4},{1,5},{2,6},{3,7},{4,0},{5,1},{6,2},{7,3},{8,12},{9,13},{10,... | collective-permute-start | bytes 405512 | tf_op jit(solution)/shard_map/ppermute | solution.py:479
  12.0 0.9 %collective-permute-done.refs_1_ = bf16[528,128]{1,0:T(8,128)(2,1)S(1)} collective-permute-done((bf16[528,128]{1,0:T(8,128)(2,1)}, bf16[528,128]{1,0:T(8,128)(2,1)S(1)}, u32[]{:S(2)}, u32[]{:S(2)}) %collective-permute-start) | collective-permute-done | bytes 135200 | tf_op jit(solution)/shard_map/ppermute | solution.py:479
  12.9 0.0 collective-permute-start.5
  12.9 2.9 %collective-permute-done.1.refs_2_ = bf16[528,128]{1,0:T(8,128)(2,1)S(1)} collective-permute-done((bf16[528,128]{1,0:T(8,128)(2,1)}, bf16[528,128]{1,0:T(8,128)(2,1)S(1)}, u32[]{:S(2)}, u32[]{:S(2)}) %collective-permute-start.1) | collective-permute-done | bytes 135200 | tf_op jit(solution)/shard_map/ppermute | solution.py:479
  15.8 0.0 collective-permute-start.6
  15.8 0.9 %copy-done.1 = bf16[528,128]{1,0:T(8,128)(2,1)S(1)} copy-done((bf16[528,128]{1,0:T(8,128)(2,1)S(1)}, bf16[528,128]{1,0:T(8,128)(2,1)}, u32[]{:S(2)}) %copy-start.1) | copy-done | bytes 135192
  16.7 2.6 %collective-permute-done.2.refs_3_ = bf16[528,128]{1,0:T(8,128)(2,1)S(1)} collective-permute-done((bf16[528,128]{1,0:T(8,128)(2,1)}, bf16[528,128]{1,0:T(8,128)(2,1)S(1)}, u32[]{:S(2)}, u32[]{:S(2)}) %collective-permute-start.2) | collective-permute-done | bytes 135200 | tf_op jit(solution)/shard_map/ppermute | solution.py:479
  19.3 1.1 %collective-permute-done.3.refs_4_ = bf16[528,128]{1,0:T(8,128)(2,1)S(1)} collective-permute-done((bf16[528,128]{1,0:T(8,128)(2,1)}, bf16[528,128]{1,0:T(8,128)(2,1)S(1)}, u32[]{:S(2)}, u32[]{:S(2)}) %collective-permute-start.3) | collective-permute-done | bytes 135200 | tf_op jit(solution)/shard_map/ppermute | solution.py:479
  20.4 0.6 %collective-permute-done.5.refs_6_ = bf16[528,128]{1,0:T(8,128)(2,1)S(1)} collective-permute-done((bf16[528,128]{1,0:T(8,128)(2,1)}, bf16[528,128]{1,0:T(8,128)(2,1)S(1)}, u32[]{:S(2)}, u32[]{:S(2)}) %collective-permute-start.5) | collective-permute-done | bytes 135200 | tf_op jit(solution)/shard_map/ppermute | solution.py:479
  21.0 0.0 collective-permute-done.6.refs_7_
  21.0 2.8 %shard_map.87 = (bf16[832,128]{1,0:T(8,128)(2,1)S(1)}, bf16[832,128]{1,0:T(8,128)(2,1)S(1)}, bf16[832,128]{1,0:T(8,128)(2,1)S(1)}, bf16[832,128]{1,0:T(8,128)(2,1)S(1)}, s32[8,1,192]{2,1,0:T(1,128)S(1)}) custom-call(bf16[528,128]{1,0:T(8,128)(2,1)S(1)} %shard_map.86.refs_0_, bf16[528,128]{1,0:T(8,128)(2,1)S(1)} %collective-permute-done.refs_1_, ...), custom_call_target="tpu_custom_call" | custom-call | tf_op jit(solution)/shard_map/pallas_call | solution.py:244
  23.9 1.7 %collective-permute-start.9 = (bf16[832,128]{1,0:T(8,128)(2,1)S(1)}, bf16[832,128]{1,0:T(8,128)(2,1)S(1)}, u32[]{:S(2)}, u32[]{:S(2)}) collective-permute-start(bf16[832,128]{1,0:T(8,128)(2,1)S(1)} %get-tuple-element.36), channel_id=1, source_target_pairs={{0,2},{1,3},{2,0},{3,1},{4,6},{5,7},{6,4},{7,5},{8,10},{9,11},{10,... | collective-permute-start | bytes 638984 | tf_op jit(solution)/shard_map/ppermute | solution.py:479
  25.5 1.5 %collective-permute-start.11 = (bf16[832,128]{1,0:T(8,128)(2,1)S(1)}, bf16[832,128]{1,0:T(8,128)(2,1)S(1)}, u32[]{:S(2)}, u32[]{:S(2)}) collective-permute-start(bf16[832,128]{1,0:T(8,128)(2,1)S(1)} %get-tuple-element.37), channel_id=1, source_target_pairs={{0,4},{1,5},{2,6},{3,7},{4,0},{5,1},{6,2},{7,3},{8,12},{9,13},{10,... | collective-permute-start | bytes 638984 | tf_op jit(solution)/shard_map/ppermute | solution.py:479
  27.0 0.4 collective-permute-start.7
  27.4 4.6 %collective-permute-done.9.refs_3_ = bf16[832,128]{1,0:T(8,128)(2,1)S(1)} collective-permute-done((bf16[832,128]{1,0:T(8,128)(2,1)S(1)}, bf16[832,128]{1,0:T(8,128)(2,1)S(1)}, u32[]{:S(2)}, u32[]{:S(2)}) %collective-permute-start.9) | collective-permute-done | bytes 213024 | tf_op jit(solution)/shard_map/ppermute | solution.py:479
  32.0 5.1 %collective-permute-done.11.refs_5_ = bf16[832,128]{1,0:T(8,128)(2,1)S(1)} collective-permute-done((bf16[832,128]{1,0:T(8,128)(2,1)S(1)}, bf16[832,128]{1,0:T(8,128)(2,1)S(1)}, u32[]{:S(2)}, u32[]{:S(2)}) %collective-permute-start.11) | collective-permute-done | bytes 213024 | tf_op jit(solution)/shard_map/ppermute | solution.py:479
  37.1 0.5 collective-permute-start.8
  37.6 0.8 %shard_map.89.placed_ref = bf16[128,512]{1,0:T(8,128)(2,1)S(1)} custom-call(s32[8,1,192]{2,1,0:T(1,128)S(1)} %get-tuple-element.40.target_ref, bf16[528,128]{1,0:T(8,128)(2,1)S(1)} %shard_map.86.refs_0_, bf16[528,128]{1,0:T(8,128)(2,1)S(1)} %collective-permute-done.refs_1_, bf16[528,128]{1,0:T(8,128)(2,1)S(1)} %collective-permute-done.1.refs_2_, ...), custom_call_target="tpu_custom_call" | custom-call | tf_op jit(solution)/shard_map/pallas_call | solution.py:244
  38.4 0.2 collective-permute-done.12.refs_6_
  38.5 0.3 collective-permute-done.8.refs_2_
  38.9 1.0 %shard_map.90 = (bf16[128,384]{1,0:T(8,128)(2,1)S(1)}, bf16[128,384]{1,0:T(8,128)(2,1)S(1)}, bf16[128,384]{1,0:T(8,128)(2,1)S(1)}, bf16[128,384]{1,0:T(8,128)(2,1)S(1)}) custom-call(bf16[128,512]{1,0:T(8,128)(2,1)S(1)} %shard_map.89.placed_ref, bf16[832,128]{1,0:T(8,128)(2,1)S(1)} %get-tuple-element.34.refs_0_, ...), custom_call_target="tpu_custom_call" | custom-call | tf_op jit(solution)/shard_map/pallas_call | solution.py:244
  39.8 3.7 %collective-permute-start.14 = (bf16[128,384]{1,0:T(8,128)(2,1)S(1)}, bf16[128,384]{1,0:T(8,128)(2,1)S(1)}, u32[]{:S(2)}, u32[]{:S(2)}) collective-permute-start(bf16[128,384]{1,0:T(8,128)(2,1)S(1)} %get-tuple-element.42), channel_id=1, source_target_pairs={{0,24},{8,16},{16,8},{24,0},{1,25},{9,17},{17,9},{25,1},{2,26},{10... | collective-permute-start | bytes 294920 | tf_op jit(solution)/shard_map/ppermute | solution.py:479
  43.5 0.8 %collective-permute-start.16 = (bf16[128,384]{1,0:T(8,128)(2,1)S(1)}, bf16[128,384]{1,0:T(8,128)(2,1)S(1)}, u32[]{:S(2)}, u32[]{:S(2)}) collective-permute-start(bf16[128,384]{1,0:T(8,128)(2,1)S(1)} %get-tuple-element.44), channel_id=1, source_target_pairs={{0,8},{8,0},{16,24},{24,16},{1,9},{9,1},{17,25},{25,17},{2,10},{10... | collective-permute-start | bytes 294920 | tf_op jit(solution)/shard_map/ppermute | solution.py:479
  44.3 3.7 %shard_map.88 = (bf16[196,1024]{1,0:T(8,128)(2,1)}, bf16[64,512]{1,0:T(8,128)(2,1)}) custom-call(s32[1,196]{1,0:T(1,128)S(1)} %copy-done.3, s32[1,192]{1,0:T(1,128)S(1)} %copy-done.2, bf16[1024,1536]{1,0:T(8,128)(2,1)S(1)} %copy-done, bf16[832,128]{1,0:T(8,128)(2,1)S(1)} %get-tuple-element.34.refs_0_, bf16[832,128]{1,0:T(8,128)(2,1)S(1)} %collective-permute-done.7.refs_1_, ...), custom_call_target="tpu_custom_call" | custom-call | tf_op jit(solution)/shard_map/pallas_call | solution.py:244
  48.0 4.2 %collective-permute-done.15.refs_2_ = bf16[128,384]{1,0:T(8,128)(2,1)S(1)} collective-permute-done((bf16[128,384]{1,0:T(8,128)(2,1)S(1)}, bf16[128,384]{1,0:T(8,128)(2,1)S(1)}, u32[]{:S(2)}, u32[]{:S(2)}) %collective-permute-start.15) | collective-permute-done | bytes 98336 | tf_op jit(solution)/shard_map/ppermute | solution.py:479
  52.1 0.7 %shard_map.91 = f32[128,384]{1,0:T(8,128)} custom-call(bf16[128,384]{1,0:T(8,128)(2,1)S(1)} %get-tuple-element.41.refs_0_, bf16[128,384]{1,0:T(8,128)(2,1)S(1)} %collective-permute-done.14.refs_1_, bf16[128,384]{1,0:T(8,128)(2,1)S(1)} %collective-permute-done.15.refs_2_, bf16[128,384]{1,0:T(8,128)(2,1)S(1)} %collective-permute-done.16.refs_3_), custom_call_target="tpu_custom_call" | custom-call | tf_op jit(solution)/shard_map/pallas_call | solution.py:244
  (17 shorter events, 0.0 us)
Async XLA Ops:
  4.6 39.7 %copy-start = (bf16[1024,1536]{1,0:T(8,128)(2,1)S(1)}, bf16[1024,1536]{1,0:T(8,128)(2,1)}, u32[]{:S(2)}) copy-start(bf16[1024,1536]{1,0:T(8,128)(2,1)} %w_hbm.1) | copy-start | bytes 9437188
  4.6 8.3 %collective-permute-start = (bf16[528,128]{1,0:T(8,128)(2,1)}, bf16[528,128]{1,0:T(8,128)(2,1)S(1)}, u32[]{:S(2)}, u32[]{:S(2)}) collective-permute-start(bf16[528,128]{1,0:T(8,128)(2,1)} %get-tuple-element.27), channel_id=1, source_target_pairs={{0,6},{1,7},{2,4},{3,5},{4,2},{5,3},{6,0},{7,1},{8,14},{9,15},{10,... | collective-permute-start | bytes 405512 | tf_op jit(solution)/shard_map/ppermute | solution.py:479
  8.6 7.2 %collective-permute-start.1 = (bf16[528,128]{1,0:T(8,128)(2,1)}, bf16[528,128]{1,0:T(8,128)(2,1)S(1)}, u32[]{:S(2)}, u32[]{:S(2)}) collective-permute-start(bf16[528,128]{1,0:T(8,128)(2,1)} %get-tuple-element.28), channel_id=1, source_target_pairs={{0,7},{1,6},{2,5},{3,4},{4,3},{5,2},{6,1},{7,0},{8,15},{9,14},{10,... | collective-permute-start | bytes 405512 | tf_op jit(solution)/shard_map/ppermute | solution.py:479
  8.6 10.7 %collective-permute-start.2 = (bf16[528,128]{1,0:T(8,128)(2,1)}, bf16[528,128]{1,0:T(8,128)(2,1)S(1)}, u32[]{:S(2)}, u32[]{:S(2)}) collective-permute-start(bf16[528,128]{1,0:T(8,128)(2,1)} %get-tuple-element.29), channel_id=1, source_target_pairs={{0,2},{1,3},{2,0},{3,1},{4,6},{5,7},{6,4},{7,5},{8,10},{9,11},{10,... | collective-permute-start | bytes 405512 | tf_op jit(solution)/shard_map/ppermute | solution.py:479
  9.7 10.7 %collective-permute-start.3 = (bf16[528,128]{1,0:T(8,128)(2,1)}, bf16[528,128]{1,0:T(8,128)(2,1)S(1)}, u32[]{:S(2)}, u32[]{:S(2)}) collective-permute-start(bf16[528,128]{1,0:T(8,128)(2,1)} %get-tuple-element.30), channel_id=1, source_target_pairs={{0,3},{1,2},{2,1},{3,0},{4,7},{5,6},{6,5},{7,4},{8,11},{9,10},{10,... | collective-permute-start | bytes 405512 | tf_op jit(solution)/shard_map/ppermute | solution.py:479
  10.3 10.1 %collective-permute-start.4 = (bf16[528,128]{1,0:T(8,128)(2,1)}, bf16[528,128]{1,0:T(8,128)(2,1)S(1)}, u32[]{:S(2)}, u32[]{:S(2)}) collective-permute-start(bf16[528,128]{1,0:T(8,128)(2,1)} %get-tuple-element.31), channel_id=1, source_target_pairs={{0,4},{1,5},{2,6},{3,7},{4,0},{5,1},{6,2},{7,3},{8,12},{9,13},{10,... | collective-permute-start | bytes 405512 | tf_op jit(solution)/shard_map/ppermute | solution.py:479
  12.9 8.2 %collective-permute-start.5 = (bf16[528,128]{1,0:T(8,128)(2,1)}, bf16[528,128]{1,0:T(8,128)(2,1)S(1)}, u32[]{:S(2)}, u32[]{:S(2)}) collective-permute-start(bf16[528,128]{1,0:T(8,128)(2,1)} %get-tuple-element.32), channel_id=1, source_target_pairs={{0,5},{1,4},{2,7},{3,6},{4,1},{5,0},{6,3},{7,2},{8,13},{9,12},{10,... | collective-permute-start | bytes 405512 | tf_op jit(solution)/shard_map/ppermute | solution.py:479
  15.8 5.3 %collective-permute-start.6 = (bf16[528,128]{1,0:T(8,128)(2,1)}, bf16[528,128]{1,0:T(8,128)(2,1)S(1)}, u32[]{:S(2)}, u32[]{:S(2)}) collective-permute-start(bf16[528,128]{1,0:T(8,128)(2,1)} %get-tuple-element.33), channel_id=1, source_target_pairs={{0,1},{1,0},{2,3},{3,2},{4,5},{5,4},{6,7},{7,6},{8,9},{9,8},{10,11... | collective-permute-start | bytes 405512 | tf_op jit(solution)/shard_map/ppermute | solution.py:479
  15.8 0.9 %copy-start.1 = (bf16[528,128]{1,0:T(8,128)(2,1)S(1)}, bf16[528,128]{1,0:T(8,128)(2,1)}, u32[]{:S(2)}) copy-start(bf16[528,128]{1,0:T(8,128)(2,1)} %get-tuple-element.26.source_ref) | copy-start | bytes 405508
  16.7 27.6 %copy-start.2 = (s32[1,192]{1,0:T(1,128)S(1)}, s32[1,192]{1,0:T(1,128)}, u32[]{:S(2)}) copy-start(s32[1,192]{1,0:T(1,128)} %get-tuple-element.25.target_ref) | copy-start | bytes 2308
  16.7 27.6 %copy-start.3 = (s32[1,196]{1,0:T(1,128)S(1)}, s32[1,196]{1,0:T(1,128)}, u32[]{:S(2)}) copy-start(s32[1,196]{1,0:T(1,128)} %get-tuple-element.24.segment_ref) | copy-start | bytes 2356
  23.9 8.2 %collective-permute-start.9 = (bf16[832,128]{1,0:T(8,128)(2,1)S(1)}, bf16[832,128]{1,0:T(8,128)(2,1)S(1)}, u32[]{:S(2)}, u32[]{:S(2)}) collective-permute-start(bf16[832,128]{1,0:T(8,128)(2,1)S(1)} %get-tuple-element.36), channel_id=1, source_target_pairs={{0,2},{1,3},{2,0},{3,1},{4,6},{5,7},{6,4},{7,5},{8,10},{9,11},{10,... | collective-permute-start | bytes 638984 | tf_op jit(solution)/shard_map/ppermute | solution.py:479
  25.5 11.6 %collective-permute-start.11 = (bf16[832,128]{1,0:T(8,128)(2,1)S(1)}, bf16[832,128]{1,0:T(8,128)(2,1)S(1)}, u32[]{:S(2)}, u32[]{:S(2)}) collective-permute-start(bf16[832,128]{1,0:T(8,128)(2,1)S(1)} %get-tuple-element.37), channel_id=1, source_target_pairs={{0,4},{1,5},{2,6},{3,7},{4,0},{5,1},{6,2},{7,3},{8,12},{9,13},{10,... | collective-permute-start | bytes 638984 | tf_op jit(solution)/shard_map/ppermute | solution.py:479
  27.0 10.1 %collective-permute-start.7 = (bf16[832,128]{1,0:T(8,128)(2,1)S(1)}, bf16[832,128]{1,0:T(8,128)(2,1)S(1)}, u32[]{:S(2)}, u32[]{:S(2)}) collective-permute-start(bf16[832,128]{1,0:T(8,128)(2,1)S(1)} %get-tuple-element.35), channel_id=1, source_target_pairs={{0,6},{1,7},{2,4},{3,5},{4,2},{5,3},{6,0},{7,1},{8,14},{9,15},{10,... | collective-permute-start | bytes 638984 | tf_op jit(solution)/shard_map/ppermute | solution.py:479
  27.4 11.0 %collective-permute-start.13 = (bf16[832,128]{1,0:T(8,128)(2,1)S(1)}, bf16[832,128]{1,0:T(8,128)(2,1)S(1)}, u32[]{:S(2)}, u32[]{:S(2)}) collective-permute-start(bf16[832,128]{1,0:T(8,128)(2,1)S(1)} %get-tuple-element.34.refs_0_), channel_id=1, source_target_pairs={{0,1},{1,0},{2,3},{3,2},{4,5},{5,4},{6,7},{7,6},{8,9},{9,8},{10,11... | collective-permute-start | bytes 638984 | tf_op jit(solution)/shard_map/ppermute | solution.py:479
  32.0 6.4 %collective-permute-start.10 = (bf16[832,128]{1,0:T(8,128)(2,1)S(1)}, bf16[832,128]{1,0:T(8,128)(2,1)S(1)}, u32[]{:S(2)}, u32[]{:S(2)}) collective-permute-start(bf16[832,128]{1,0:T(8,128)(2,1)S(1)} %collective-permute-done.9.refs_3_), channel_id=1, source_target_pairs={{0,1},{1,0},{2,3},{3,2},{4,5},{5,4},{6,7},{7,6},{8,9},{9,8},{10,11... | collective-permute-start | bytes 638984 | tf_op jit(solution)/shard_map/ppermute | solution.py:479
  37.1 1.5 %collective-permute-start.12 = (bf16[832,128]{1,0:T(8,128)(2,1)S(1)}, bf16[832,128]{1,0:T(8,128)(2,1)S(1)}, u32[]{:S(2)}, u32[]{:S(2)}) collective-permute-start(bf16[832,128]{1,0:T(8,128)(2,1)S(1)} %collective-permute-done.11.refs_5_), channel_id=1, source_target_pairs={{0,1},{1,0},{2,3},{3,2},{4,5},{5,4},{6,7},{7,6},{8,9},{9,8},{10,11... | collective-permute-start | bytes 638984 | tf_op jit(solution)/shard_map/ppermute | solution.py:479
  37.1 1.8 %collective-permute-start.8 = (bf16[832,128]{1,0:T(8,128)(2,1)S(1)}, bf16[832,128]{1,0:T(8,128)(2,1)S(1)}, u32[]{:S(2)}, u32[]{:S(2)}) collective-permute-start(bf16[832,128]{1,0:T(8,128)(2,1)S(1)} %collective-permute-done.7.refs_1_), channel_id=1, source_target_pairs={{0,1},{1,0},{2,3},{3,2},{4,5},{5,4},{6,7},{7,6},{8,9},{9,8},{10,11... | collective-permute-start | bytes 638984 | tf_op jit(solution)/shard_map/ppermute | solution.py:479
  39.8 8.1 %collective-permute-start.14 = (bf16[128,384]{1,0:T(8,128)(2,1)S(1)}, bf16[128,384]{1,0:T(8,128)(2,1)S(1)}, u32[]{:S(2)}, u32[]{:S(2)}) collective-permute-start(bf16[128,384]{1,0:T(8,128)(2,1)S(1)} %get-tuple-element.42), channel_id=1, source_target_pairs={{0,24},{8,16},{16,8},{24,0},{1,25},{9,17},{17,9},{25,1},{2,26},{10... | collective-permute-start | bytes 294920 | tf_op jit(solution)/shard_map/ppermute | solution.py:479
  43.5 8.6 %collective-permute-start.15 = (bf16[128,384]{1,0:T(8,128)(2,1)S(1)}, bf16[128,384]{1,0:T(8,128)(2,1)S(1)}, u32[]{:S(2)}, u32[]{:S(2)}) collective-permute-start(bf16[128,384]{1,0:T(8,128)(2,1)S(1)} %get-tuple-element.43), channel_id=1, source_target_pairs={{0,16},{8,24},{16,0},{24,8},{1,17},{9,25},{17,1},{25,9},{2,18},{10... | collective-permute-start | bytes 294920 | tf_op jit(solution)/shard_map/ppermute | solution.py:479
  43.5 8.6 %collective-permute-start.16 = (bf16[128,384]{1,0:T(8,128)(2,1)S(1)}, bf16[128,384]{1,0:T(8,128)(2,1)S(1)}, u32[]{:S(2)}, u32[]{:S(2)}) collective-permute-start(bf16[128,384]{1,0:T(8,128)(2,1)S(1)} %get-tuple-element.44), channel_id=1, source_target_pairs={{0,8},{8,0},{16,24},{24,16},{1,9},{9,1},{17,25},{25,17},{2,10},{10... | collective-permute-start | bytes 294920 | tf_op jit(solution)/shard_map/ppermute | solution.py:479

commit v4 on v3

--- a/solution.py
+++ b/solution.py
@@ -351,18 +351,19 @@
     scaling = HEAD_DIM ** (-0.5)
     half_cap = token_cap // 2
     lines_at = token_cap + half_cap
-    row_id = lax.broadcasted_iota(jnp.int32, (rows, token_cap), 0)
-    total = jnp.zeros((rows, 3 * HEAD_DIM), jnp.float32)
     me = lax.axis_index("seq")
+    targets, rows_in = [], []
     for flip, piece in zip(flips, pieces):
         sender = jnp.bitwise_xor(me, flip)
         target = target_row(piece[lines_at : lines_at + 16], token_cap, local_rows)
         target_ref[sender] = target
-        rows_in = jnp.concatenate(
-            [piece[:token_cap], unfold_half(piece[token_cap:lines_at])], axis=1
-        )
-        total = total + dot(one_hot(row_id == target), rows_in)
+        targets.append(target)
+        value = unfold_half(piece[token_cap:lines_at])
+        rows_in.append(jnp.concatenate([piece[:token_cap], value], axis=1))
         grad_ref[sender] = unfold_half(piece[lines_at + 16 : lines_at + 16 + local_rows // 2])
+    row_id = lax.broadcasted_iota(jnp.int32, (rows, devices * token_cap), 0)
+    placer = one_hot(row_id == jnp.concatenate(targets, axis=1))
+    total = dot(placer, jnp.concatenate(rows_in, axis=0))
     projected = total.astype(jnp.bfloat16)
     query = projected[:, :HEAD_DIM]
     key = projected[:, HEAD_DIM : 2 * HEAD_DIM]
@@ -483,6 +484,11 @@
     return jax.ShapeDtypeStruct(sizes, dtype)
 
 
+def start_order(flip):
+    steps = (flip // 2).bit_count()
+    return flip > 0, -steps, flip % 2, -flip
+
+
 def heads_plan(patches, segment, dest_shard, dest_slot, w_qkv, out_grad):
     devices = lax.axis_size("seq")
     clips = lax.axis_size("clip")
@@ -510,7 +516,7 @@
         limit=62 * 1024 * 1024,
     )
     sends, (target, segment) = list(outs[:devices]), outs[devices:]
-    order = [0] + sorted(range(1, devices), key=lambda flip: (-(flip // 2).bit_count(), flip))
+    order = sorted(range(devices), key=start_order)
     sends[0] = call(copy_kernel, shape(sent, 2 * HEAD_DIM), sends[0])
     came = {0: sends[0]}
     for flip in order[1:]:
@@ -547,7 +553,8 @@
             pltpu.VMEM((clips, width, 3 * inner // clips), jnp.bfloat16),
         ],
     )
-    weights = [weights[0]] + [exchange(weights[flip], "clip", flip) for flip in range(clips - 1, 0, -1)]
+    clip_flips = sorted(range(1, clips), key=lambda flip: (flip < clips // 2, flip))
+    weights = [weights[0]] + [exchange(weights[flip], "clip", flip) for flip in clip_flips]
     patch_grad, attended = call(
         functools.partial(patch_kernel, flips),
         [shape(patches.shape[1], model), shape(local_rows, inner)],

time: 53.1 us -> 51.4 us (0.968)
  starting transfers between devices: 15.9 us -> 15.1 us
    ppermute x17, starting transfers between devices: 15.9 us -> 15.1 us  [exchange(): lax.ppermute(rows, axis, [(index, index ^ flip) for index in range(count)])]
  transfers between devices with their start and end apart: 17 -> 17, of which waited for: 10 -> 11; matrix products, arithmetic and copies ran while one was open for 0% -> 0% of each run, Pallas kernels for 8% -> 9%
where the time goes in v4:
time: 51.4 us; the launch traced here: 51.3 us
  waiting for transfers between devices  22 us (43%)
  starting transfers between devices  15.1 us (29%)
  Pallas kernels  12.5 us (24%)
  local copies, waits for them, and re-layouts  0.92 us (2%)
  between operations  0.71 us (1%)
    ppermute x17, waiting for transfers between devices, exchange(): lax.ppermute(rows, axis, [(index, index ^ flip) for index in range(count)])  22 us
    ppermute x17, starting transfers between devices, exchange(): lax.ppermute(rows, axis, [(index, index ^ flip) for index in range(count)])  15.1 us
    pallas_call x7, Pallas kernels, call(): pl.pallas_call(body, out_shape=outs, in_specs=[pl.BlockSpec(memory_space=...  12.5 us
  transfers between devices with their start and end apart: 17, of which 11 were waited for; matrix products, arithmetic and copies ran while one was open for 0% of the time, Pallas kernels for 9%

profile of v4, /device:TPU:0, one launch (start us, length us, event | category | flops | bytes accessed | tf_op | source)
XLA Modules:
  0.0 51.3 jit_solution(9985106298285512602)
XLA Ops:
  0.6 3.9 %shard_map.85 = (bf16[528,128]{1,0:T(8,128)(2,1)}, bf16[528,128]{1,0:T(8,128)(2,1)}, bf16[528,128]{1,0:T(8,128)(2,1)}, bf16[528,128]{1,0:T(8,128)(2,1)}, bf16[52...) custom-call(s32[1,196]{1,0:T(1,128)} %refs_0_.1, ...), custom_call_target="tpu_custom_call" | custom-call | tf_op jit(solution)/shard_map/pallas_call | solution.py:244
  4.6 0.0 copy-start
  4.6 4.0 %collective-permute-start = (bf16[528,128]{1,0:T(8,128)(2,1)}, bf16[528,128]{1,0:T(8,128)(2,1)S(1)}, u32[]{:S(2)}, u32[]{:S(2)}) collective-permute-start(bf16[528,128]{1,0:T(8,128)(2,1)} %get-tuple-element.27), channel_id=1, source_target_pairs={{0,6},{1,7},{2,4},{3,5},{4,2},{5,3},{6,0},{7,1},{8,14},{9,15},{10,... | collective-permute-start | bytes 405512 | tf_op jit(solution)/shard_map/ppermute | solution.py:480
  8.6 1.1 %collective-permute-start.2 = (bf16[528,128]{1,0:T(8,128)(2,1)}, bf16[528,128]{1,0:T(8,128)(2,1)S(1)}, u32[]{:S(2)}, u32[]{:S(2)}) collective-permute-start(bf16[528,128]{1,0:T(8,128)(2,1)} %get-tuple-element.29), channel_id=1, source_target_pairs={{0,4},{1,5},{2,6},{3,7},{4,0},{5,1},{6,2},{7,3},{8,12},{9,13},{10,... | collective-permute-start | bytes 405512 | tf_op jit(solution)/shard_map/ppermute | solution.py:480
  9.7 1.5 %collective-permute-start.3 = (bf16[528,128]{1,0:T(8,128)(2,1)}, bf16[528,128]{1,0:T(8,128)(2,1)S(1)}, u32[]{:S(2)}, u32[]{:S(2)}) collective-permute-start(bf16[528,128]{1,0:T(8,128)(2,1)} %get-tuple-element.30), channel_id=1, source_target_pairs={{0,2},{1,3},{2,0},{3,1},{4,6},{5,7},{6,4},{7,5},{8,10},{9,11},{10,... | collective-permute-start | bytes 405512 | tf_op jit(solution)/shard_map/ppermute | solution.py:480
  11.2 0.5 %collective-permute-start.4 = (bf16[528,128]{1,0:T(8,128)(2,1)}, bf16[528,128]{1,0:T(8,128)(2,1)S(1)}, u32[]{:S(2)}, u32[]{:S(2)}) collective-permute-start(bf16[528,128]{1,0:T(8,128)(2,1)} %get-tuple-element.31), channel_id=1, source_target_pairs={{0,5},{1,4},{2,7},{3,6},{4,1},{5,0},{6,3},{7,2},{8,13},{9,12},{10,... | collective-permute-start | bytes 405512 | tf_op jit(solution)/shard_map/ppermute | solution.py:480
  11.7 1.2 %collective-permute-done.refs_1_ = bf16[528,128]{1,0:T(8,128)(2,1)S(1)} collective-permute-done((bf16[528,128]{1,0:T(8,128)(2,1)}, bf16[528,128]{1,0:T(8,128)(2,1)S(1)}, u32[]{:S(2)}, u32[]{:S(2)}) %collective-permute-start) | collective-permute-done | bytes 135200 | tf_op jit(solution)/shard_map/ppermute | solution.py:480
  12.9 0.0 collective-permute-start.5
  12.9 2.9 %collective-permute-done.1.refs_2_ = bf16[528,128]{1,0:T(8,128)(2,1)S(1)} collective-permute-done((bf16[528,128]{1,0:T(8,128)(2,1)}, bf16[528,128]{1,0:T(8,128)(2,1)S(1)}, u32[]{:S(2)}, u32[]{:S(2)}) %collective-permute-start.1) | collective-permute-done | bytes 135200 | tf_op jit(solution)/shard_map/ppermute | solution.py:480
  15.8 0.9 %copy-done.1 = bf16[528,128]{1,0:T(8,128)(2,1)S(1)} copy-done((bf16[528,128]{1,0:T(8,128)(2,1)S(1)}, bf16[528,128]{1,0:T(8,128)(2,1)}, u32[]{:S(2)}) %copy-start.1) | copy-done | bytes 135192
  16.7 1.5 %collective-permute-done.2.refs_3_ = bf16[528,128]{1,0:T(8,128)(2,1)S(1)} collective-permute-done((bf16[528,128]{1,0:T(8,128)(2,1)}, bf16[528,128]{1,0:T(8,128)(2,1)S(1)}, u32[]{:S(2)}, u32[]{:S(2)}) %collective-permute-start.2) | collective-permute-done | bytes 135200 | tf_op jit(solution)/shard_map/ppermute | solution.py:480
  18.2 1.2 %collective-permute-done.3.refs_4_ = bf16[528,128]{1,0:T(8,128)(2,1)S(1)} collective-permute-done((bf16[528,128]{1,0:T(8,128)(2,1)}, bf16[528,128]{1,0:T(8,128)(2,1)S(1)}, u32[]{:S(2)}, u32[]{:S(2)}) %collective-permute-start.3) | collective-permute-done | bytes 135200 | tf_op jit(solution)/shard_map/ppermute | solution.py:480
  19.4 1.6 %collective-permute-done.4.refs_5_ = bf16[528,128]{1,0:T(8,128)(2,1)S(1)} collective-permute-done((bf16[528,128]{1,0:T(8,128)(2,1)}, bf16[528,128]{1,0:T(8,128)(2,1)S(1)}, u32[]{:S(2)}, u32[]{:S(2)}) %collective-permute-start.4) | collective-permute-done | bytes 135200 | tf_op jit(solution)/shard_map/ppermute | solution.py:480
  21.0 0.0 collective-permute-done.5.refs_6_
  21.0 0.0 collective-permute-done.6.refs_7_
  21.0 2.4 %shard_map.87 = (bf16[832,128]{1,0:T(8,128)(2,1)S(1)}, bf16[832,128]{1,0:T(8,128)(2,1)S(1)}, bf16[832,128]{1,0:T(8,128)(2,1)S(1)}, bf16[832,128]{1,0:T(8,128)(2,1)S(1)}, s32[8,1,192]{2,1,0:T(1,128)S(1)}) custom-call(bf16[528,128]{1,0:T(8,128)(2,1)S(1)} %shard_map.86.refs_0_, bf16[528,128]{1,0:T(8,128)(2,1)S(1)} %collective-permute-done.refs_1_, ...), custom_call_target="tpu_custom_call" | custom-call | tf_op jit(solution)/shard_map/pallas_call | solution.py:244
  23.4 1.8 %collective-permute-start.9 = (bf16[832,128]{1,0:T(8,128)(2,1)S(1)}, bf16[832,128]{1,0:T(8,128)(2,1)S(1)}, u32[]{:S(2)}, u32[]{:S(2)}) collective-permute-start(bf16[832,128]{1,0:T(8,128)(2,1)S(1)} %get-tuple-element.36), channel_id=1, source_target_pairs={{0,4},{1,5},{2,6},{3,7},{4,0},{5,1},{6,2},{7,3},{8,12},{9,13},{10,... | collective-permute-start | bytes 638984 | tf_op jit(solution)/shard_map/ppermute | solution.py:480
  25.3 1.5 %collective-permute-start.10 = (bf16[832,128]{1,0:T(8,128)(2,1)S(1)}, bf16[832,128]{1,0:T(8,128)(2,1)S(1)}, u32[]{:S(2)}, u32[]{:S(2)}) collective-permute-start(bf16[832,128]{1,0:T(8,128)(2,1)S(1)} %get-tuple-element.37), channel_id=1, source_target_pairs={{0,2},{1,3},{2,0},{3,1},{4,6},{5,7},{6,4},{7,5},{8,10},{9,11},{10,... | collective-permute-start | bytes 638984 | tf_op jit(solution)/shard_map/ppermute | solution.py:480
  26.8 0.2 collective-permute-start.7
  27.0 3.8 %collective-permute-done.9.refs_3_ = bf16[832,128]{1,0:T(8,128)(2,1)S(1)} collective-permute-done((bf16[832,128]{1,0:T(8,128)(2,1)S(1)}, bf16[832,128]{1,0:T(8,128)(2,1)S(1)}, u32[]{:S(2)}, u32[]{:S(2)}) %collective-permute-start.9) | collective-permute-done | bytes 213024 | tf_op jit(solution)/shard_map/ppermute | solution.py:480
  30.8 2.6 %collective-permute-done.10.refs_4_ = bf16[832,128]{1,0:T(8,128)(2,1)S(1)} collective-permute-done((bf16[832,128]{1,0:T(8,128)(2,1)S(1)}, bf16[832,128]{1,0:T(8,128)(2,1)S(1)}, u32[]{:S(2)}, u32[]{:S(2)}) %collective-permute-start.10) | collective-permute-done | bytes 213024 | tf_op jit(solution)/shard_map/ppermute | solution.py:480
  33.4 3.2 %collective-permute-done.7.refs_1_ = bf16[832,128]{1,0:T(8,128)(2,1)S(1)} collective-permute-done((bf16[832,128]{1,0:T(8,128)(2,1)S(1)}, bf16[832,128]{1,0:T(8,128)(2,1)S(1)}, u32[]{:S(2)}, u32[]{:S(2)}) %collective-permute-start.7) | collective-permute-done | bytes 213024 | tf_op jit(solution)/shard_map/ppermute | solution.py:480
  36.6 0.8 %shard_map.89.placed_ref = bf16[128,512]{1,0:T(8,128)(2,1)S(1)} custom-call(s32[8,1,192]{2,1,0:T(1,128)S(1)} %get-tuple-element.40.target_ref, bf16[528,128]{1,0:T(8,128)(2,1)S(1)} %shard_map.86.refs_0_, bf16[528,128]{1,0:T(8,128)(2,1)S(1)} %collective-permute-done.refs_1_, bf16[528,128]{1,0:T(8,128)(2,1)S(1)} %collective-permute-done.1.refs_2_, ...), custom_call_target="tpu_custom_call" | custom-call | tf_op jit(solution)/shard_map/pallas_call | solution.py:244
  37.4 0.7 %collective-permute-done.8.refs_2_ = bf16[832,128]{1,0:T(8,128)(2,1)S(1)} collective-permute-done((bf16[832,128]{1,0:T(8,128)(2,1)S(1)}, bf16[832,128]{1,0:T(8,128)(2,1)S(1)}, u32[]{:S(2)}, u32[]{:S(2)}) %collective-permute-start.8) | collective-permute-done | bytes 213024 | tf_op jit(solution)/shard_map/ppermute | solution.py:480
  38.1 1.0 %shard_map.90 = (bf16[128,384]{1,0:T(8,128)(2,1)S(1)}, bf16[128,384]{1,0:T(8,128)(2,1)S(1)}, bf16[128,384]{1,0:T(8,128)(2,1)S(1)}, bf16[128,384]{1,0:T(8,128)(2,1)S(1)}) custom-call(bf16[128,512]{1,0:T(8,128)(2,1)S(1)} %shard_map.89.placed_ref, bf16[832,128]{1,0:T(8,128)(2,1)S(1)} %get-tuple-element.34.refs_0_, ...), custom_call_target="tpu_custom_call" | custom-call | tf_op jit(solution)/shard_map/pallas_call | solution.py:244
  39.1 2.8 %collective-permute-start.14 = (bf16[128,384]{1,0:T(8,128)(2,1)S(1)}, bf16[128,384]{1,0:T(8,128)(2,1)S(1)}, u32[]{:S(2)}, u32[]{:S(2)}) collective-permute-start(bf16[128,384]{1,0:T(8,128)(2,1)S(1)} %get-tuple-element.42), channel_id=1, source_target_pairs={{0,16},{8,24},{16,0},{24,8},{1,17},{9,25},{17,1},{25,9},{2,18},{10... | collective-permute-start | bytes 294920 | tf_op jit(solution)/shard_map/ppermute | solution.py:480
  41.8 1.3 %collective-permute-start.15 = (bf16[128,384]{1,0:T(8,128)(2,1)S(1)}, bf16[128,384]{1,0:T(8,128)(2,1)S(1)}, u32[]{:S(2)}, u32[]{:S(2)}) collective-permute-start(bf16[128,384]{1,0:T(8,128)(2,1)S(1)} %get-tuple-element.43), channel_id=1, source_target_pairs={{0,24},{8,16},{16,8},{24,0},{1,25},{9,17},{17,9},{25,1},{2,26},{10... | collective-permute-start | bytes 294920 | tf_op jit(solution)/shard_map/ppermute | solution.py:480
  43.2 0.3 collective-permute-start.16
  43.4 3.7 %shard_map.88 = (bf16[196,1024]{1,0:T(8,128)(2,1)}, bf16[64,512]{1,0:T(8,128)(2,1)}) custom-call(s32[1,196]{1,0:T(1,128)S(1)} %copy-done.3, s32[1,192]{1,0:T(1,128)S(1)} %copy-done.2, bf16[1024,1536]{1,0:T(8,128)(2,1)S(1)} %copy-done, bf16[832,128]{1,0:T(8,128)(2,1)S(1)} %get-tuple-element.34.refs_0_, bf16[832,128]{1,0:T(8,128)(2,1)S(1)} %collective-permute-done.7.refs_1_, ...), custom_call_target="tpu_custom_call" | custom-call | tf_op jit(solution)/shard_map/pallas_call | solution.py:244
  47.1 2.8 %collective-permute-done.14.refs_1_ = bf16[128,384]{1,0:T(8,128)(2,1)S(1)} collective-permute-done((bf16[128,384]{1,0:T(8,128)(2,1)S(1)}, bf16[128,384]{1,0:T(8,128)(2,1)S(1)}, u32[]{:S(2)}, u32[]{:S(2)}) %collective-permute-start.14) | collective-permute-done | bytes 98336 | tf_op jit(solution)/shard_map/ppermute | solution.py:480
  49.9 0.6 %collective-permute-done.16.refs_3_ = bf16[128,384]{1,0:T(8,128)(2,1)S(1)} collective-permute-done((bf16[128,384]{1,0:T(8,128)(2,1)S(1)}, bf16[128,384]{1,0:T(8,128)(2,1)S(1)}, u32[]{:S(2)}, u32[]{:S(2)}) %collective-permute-start.16) | collective-permute-done | bytes 98336 | tf_op jit(solution)/shard_map/ppermute | solution.py:480
  50.5 0.7 %shard_map.91 = f32[128,384]{1,0:T(8,128)} custom-call(bf16[128,384]{1,0:T(8,128)(2,1)S(1)} %get-tuple-element.41.refs_0_, bf16[128,384]{1,0:T(8,128)(2,1)S(1)} %collective-permute-done.14.refs_1_, bf16[128,384]{1,0:T(8,128)(2,1)S(1)} %collective-permute-done.15.refs_2_, bf16[128,384]{1,0:T(8,128)(2,1)S(1)} %collective-permute-done.16.refs_3_), custom_call_target="tpu_custom_call" | custom-call | tf_op jit(solution)/shard_map/pallas_call | solution.py:244
  (17 shorter events, 0.0 us)
Async XLA Ops:
  4.6 38.8 %copy-start = (bf16[1024,1536]{1,0:T(8,128)(2,1)S(1)}, bf16[1024,1536]{1,0:T(8,128)(2,1)}, u32[]{:S(2)}) copy-start(bf16[1024,1536]{1,0:T(8,128)(2,1)} %w_hbm.1) | copy-start | bytes 9437188
  4.6 8.3 %collective-permute-start = (bf16[528,128]{1,0:T(8,128)(2,1)}, bf16[528,128]{1,0:T(8,128)(2,1)S(1)}, u32[]{:S(2)}, u32[]{:S(2)}) collective-permute-start(bf16[528,128]{1,0:T(8,128)(2,1)} %get-tuple-element.27), channel_id=1, source_target_pairs={{0,6},{1,7},{2,4},{3,5},{4,2},{5,3},{6,0},{7,1},{8,14},{9,15},{10,... | collective-permute-start | bytes 405512 | tf_op jit(solution)/shard_map/ppermute | solution.py:480
  8.6 7.2 %collective-permute-start.1 = (bf16[528,128]{1,0:T(8,128)(2,1)}, bf16[528,128]{1,0:T(8,128)(2,1)S(1)}, u32[]{:S(2)}, u32[]{:S(2)}) collective-permute-start(bf16[528,128]{1,0:T(8,128)(2,1)} %get-tuple-element.28), channel_id=1, source_target_pairs={{0,7},{1,6},{2,5},{3,4},{4,3},{5,2},{6,1},{7,0},{8,15},{9,14},{10,... | collective-permute-start | bytes 405512 | tf_op jit(solution)/shard_map/ppermute | solution.py:480
  8.6 9.6 %collective-permute-start.2 = (bf16[528,128]{1,0:T(8,128)(2,1)}, bf16[528,128]{1,0:T(8,128)(2,1)S(1)}, u32[]{:S(2)}, u32[]{:S(2)}) collective-permute-start(bf16[528,128]{1,0:T(8,128)(2,1)} %get-tuple-element.29), channel_id=1, source_target_pairs={{0,4},{1,5},{2,6},{3,7},{4,0},{5,1},{6,2},{7,3},{8,12},{9,13},{10,... | collective-permute-start | bytes 405512 | tf_op jit(solution)/shard_map/ppermute | solution.py:480
  9.7 9.6 %collective-permute-start.3 = (bf16[528,128]{1,0:T(8,128)(2,1)}, bf16[528,128]{1,0:T(8,128)(2,1)S(1)}, u32[]{:S(2)}, u32[]{:S(2)}) collective-permute-start(bf16[528,128]{1,0:T(8,128)(2,1)} %get-tuple-element.30), channel_id=1, source_target_pairs={{0,2},{1,3},{2,0},{3,1},{4,6},{5,7},{6,4},{7,5},{8,10},{9,11},{10,... | collective-permute-start | bytes 405512 | tf_op jit(solution)/shard_map/ppermute | solution.py:480
  11.2 9.8 %collective-permute-start.4 = (bf16[528,128]{1,0:T(8,128)(2,1)}, bf16[528,128]{1,0:T(8,128)(2,1)S(1)}, u32[]{:S(2)}, u32[]{:S(2)}) collective-permute-start(bf16[528,128]{1,0:T(8,128)(2,1)} %get-tuple-element.31), channel_id=1, source_target_pairs={{0,5},{1,4},{2,7},{3,6},{4,1},{5,0},{6,3},{7,2},{8,13},{9,12},{10,... | collective-permute-start | bytes 405512 | tf_op jit(solution)/shard_map/ppermute | solution.py:480
  12.9 8.1 %collective-permute-start.5 = (bf16[528,128]{1,0:T(8,128)(2,1)}, bf16[528,128]{1,0:T(8,128)(2,1)S(1)}, u32[]{:S(2)}, u32[]{:S(2)}) collective-permute-start(bf16[528,128]{1,0:T(8,128)(2,1)} %get-tuple-element.32), channel_id=1, source_target_pairs={{0,3},{1,2},{2,1},{3,0},{4,7},{5,6},{6,5},{7,4},{8,11},{9,10},{10,... | collective-permute-start | bytes 405512 | tf_op jit(solution)/shard_map/ppermute | solution.py:480
  15.8 5.2 %collective-permute-start.6 = (bf16[528,128]{1,0:T(8,128)(2,1)}, bf16[528,128]{1,0:T(8,128)(2,1)S(1)}, u32[]{:S(2)}, u32[]{:S(2)}) collective-permute-start(bf16[528,128]{1,0:T(8,128)(2,1)} %get-tuple-element.33), channel_id=1, source_target_pairs={{0,1},{1,0},{2,3},{3,2},{4,5},{5,4},{6,7},{7,6},{8,9},{9,8},{10,11... | collective-permute-start | bytes 405512 | tf_op jit(solution)/shard_map/ppermute | solution.py:480
  15.8 0.9 %copy-start.1 = (bf16[528,128]{1,0:T(8,128)(2,1)S(1)}, bf16[528,128]{1,0:T(8,128)(2,1)}, u32[]{:S(2)}) copy-start(bf16[528,128]{1,0:T(8,128)(2,1)} %get-tuple-element.26.source_ref) | copy-start | bytes 405508
  16.7 26.7 %copy-start.2 = (s32[1,192]{1,0:T(1,128)S(1)}, s32[1,192]{1,0:T(1,128)}, u32[]{:S(2)}) copy-start(s32[1,192]{1,0:T(1,128)} %get-tuple-element.25.target_ref) | copy-start | bytes 2308
  16.7 26.7 %copy-start.3 = (s32[1,196]{1,0:T(1,128)S(1)}, s32[1,196]{1,0:T(1,128)}, u32[]{:S(2)}) copy-start(s32[1,196]{1,0:T(1,128)} %get-tuple-element.24.segment_ref) | copy-start | bytes 2356
  23.4 7.4 %collective-permute-start.9 = (bf16[832,128]{1,0:T(8,128)(2,1)S(1)}, bf16[832,128]{1,0:T(8,128)(2,1)S(1)}, u32[]{:S(2)}, u32[]{:S(2)}) collective-permute-start(bf16[832,128]{1,0:T(8,128)(2,1)S(1)} %get-tuple-element.36), channel_id=1, source_target_pairs={{0,4},{1,5},{2,6},{3,7},{4,0},{5,1},{6,2},{7,3},{8,12},{9,13},{10,... | collective-permute-start | bytes 638984 | tf_op jit(solution)/shard_map/ppermute | solution.py:480
  25.3 8.1 %collective-permute-start.10 = (bf16[832,128]{1,0:T(8,128)(2,1)S(1)}, bf16[832,128]{1,0:T(8,128)(2,1)S(1)}, u32[]{:S(2)}, u32[]{:S(2)}) collective-permute-start(bf16[832,128]{1,0:T(8,128)(2,1)S(1)} %get-tuple-element.37), channel_id=1, source_target_pairs={{0,2},{1,3},{2,0},{3,1},{4,6},{5,7},{6,4},{7,5},{8,10},{9,11},{10,... | collective-permute-start | bytes 638984 | tf_op jit(solution)/shard_map/ppermute | solution.py:480
  26.8 9.9 %collective-permute-start.7 = (bf16[832,128]{1,0:T(8,128)(2,1)S(1)}, bf16[832,128]{1,0:T(8,128)(2,1)S(1)}, u32[]{:S(2)}, u32[]{:S(2)}) collective-permute-start(bf16[832,128]{1,0:T(8,128)(2,1)S(1)} %get-tuple-element.35), channel_id=1, source_target_pairs={{0,6},{1,7},{2,4},{3,5},{4,2},{5,3},{6,0},{7,1},{8,14},{9,15},{10,... | collective-permute-start | bytes 638984 | tf_op jit(solution)/shard_map/ppermute | solution.py:480
  27.0 10.4 %collective-permute-start.13 = (bf16[832,128]{1,0:T(8,128)(2,1)S(1)}, bf16[832,128]{1,0:T(8,128)(2,1)S(1)}, u32[]{:S(2)}, u32[]{:S(2)}) collective-permute-start(bf16[832,128]{1,0:T(8,128)(2,1)S(1)} %get-tuple-element.34.refs_0_), channel_id=1, source_target_pairs={{0,1},{1,0},{2,3},{3,2},{4,5},{5,4},{6,7},{7,6},{8,9},{9,8},{10,11... | collective-permute-start | bytes 638984 | tf_op jit(solution)/shard_map/ppermute | solution.py:480
  30.8 6.6 %collective-permute-start.11 = (bf16[832,128]{1,0:T(8,128)(2,1)S(1)}, bf16[832,128]{1,0:T(8,128)(2,1)S(1)}, u32[]{:S(2)}, u32[]{:S(2)}) collective-permute-start(bf16[832,128]{1,0:T(8,128)(2,1)S(1)} %collective-permute-done.9.refs_3_), channel_id=1, source_target_pairs={{0,1},{1,0},{2,3},{3,2},{4,5},{5,4},{6,7},{7,6},{8,9},{9,8},{10,11... | collective-permute-start | bytes 638984 | tf_op jit(solution)/shard_map/ppermute | solution.py:480
  33.4 4.0 %collective-permute-start.12 = (bf16[832,128]{1,0:T(8,128)(2,1)S(1)}, bf16[832,128]{1,0:T(8,128)(2,1)S(1)}, u32[]{:S(2)}, u32[]{:S(2)}) collective-permute-start(bf16[832,128]{1,0:T(8,128)(2,1)S(1)} %collective-permute-done.10.refs_4_), channel_id=1, source_target_pairs={{0,1},{1,0},{2,3},{3,2},{4,5},{5,4},{6,7},{7,6},{8,9},{9,8},{10,11... | collective-permute-start | bytes 638984 | tf_op jit(solution)/shard_map/ppermute | solution.py:480
  36.6 1.5 %collective-permute-start.8 = (bf16[832,128]{1,0:T(8,128)(2,1)S(1)}, bf16[832,128]{1,0:T(8,128)(2,1)S(1)}, u32[]{:S(2)}, u32[]{:S(2)}) collective-permute-start(bf16[832,128]{1,0:T(8,128)(2,1)S(1)} %collective-permute-done.7.refs_1_), channel_id=1, source_target_pairs={{0,1},{1,0},{2,3},{3,2},{4,5},{5,4},{6,7},{7,6},{8,9},{9,8},{10,11... | collective-permute-start | bytes 638984 | tf_op jit(solution)/shard_map/ppermute | solution.py:480
  39.1 10.9 %collective-permute-start.14 = (bf16[128,384]{1,0:T(8,128)(2,1)S(1)}, bf16[128,384]{1,0:T(8,128)(2,1)S(1)}, u32[]{:S(2)}, u32[]{:S(2)}) collective-permute-start(bf16[128,384]{1,0:T(8,128)(2,1)S(1)} %get-tuple-element.42), channel_id=1, source_target_pairs={{0,16},{8,24},{16,0},{24,8},{1,17},{9,25},{17,1},{25,9},{2,18},{10... | collective-permute-start | bytes 294920 | tf_op jit(solution)/shard_map/ppermute | solution.py:480
  41.8 8.1 %collective-permute-start.15 = (bf16[128,384]{1,0:T(8,128)(2,1)S(1)}, bf16[128,384]{1,0:T(8,128)(2,1)S(1)}, u32[]{:S(2)}, u32[]{:S(2)}) collective-permute-start(bf16[128,384]{1,0:T(8,128)(2,1)S(1)} %get-tuple-element.43), channel_id=1, source_target_pairs={{0,24},{8,16},{16,8},{24,0},{1,25},{9,17},{17,9},{25,1},{2,26},{10... | collective-permute-start | bytes 294920 | tf_op jit(solution)/shard_map/ppermute | solution.py:480
  43.2 7.4 %collective-permute-start.16 = (bf16[128,384]{1,0:T(8,128)(2,1)S(1)}, bf16[128,384]{1,0:T(8,128)(2,1)S(1)}, u32[]{:S(2)}, u32[]{:S(2)}) collective-permute-start(bf16[128,384]{1,0:T(8,128)(2,1)S(1)} %get-tuple-element.44), channel_id=1, source_target_pairs={{0,8},{8,0},{16,24},{24,16},{1,9},{9,1},{17,25},{25,17},{2,10},{10... | collective-permute-start | bytes 294920 | tf_op jit(solution)/shard_map/ppermute | solution.py:480

commit v5 on v4

--- a/solution.py
+++ b/solution.py
@@ -239,13 +239,14 @@
     return lax.dot_general(left, right, dims, preferred_element_type=jnp.float32)
 
 
-def call(body, outs, *args, scratch=(), space=None, limit=VMEM_LIMIT):
+def call(body, outs, *args, scratch=(), space=None, limit=VMEM_LIMIT, flops=0):
     space = space or [pltpu.VMEM] * len(args)
     return pl.pallas_call(
         body,
         out_shape=outs,
         in_specs=[pl.BlockSpec(memory_space=each) for each in space],
         scratch_shapes=scratch,
+        cost_estimate=pl.CostEstimate(flops=flops, bytes_accessed=0, transcendentals=0),
         compiler_params=pltpu.CompilerParams(vmem_limit_bytes=limit),
     )(*args)
 
@@ -343,27 +344,41 @@
     return (shard * local_rows + slot).astype(jnp.int32)
 
 
-def head_kernel(token_cap, flips, *refs):
-    pieces, refs = refs[:HEADS], refs[HEADS:]
-    outs, (target_ref, grad_ref, attended_ref) = refs[: HEADS // 2], refs[HEADS // 2 :]
-    devices, local_rows = len(pieces), grad_ref.shape[1]
-    rows = devices * local_rows
-    scaling = HEAD_DIM ** (-0.5)
-    half_cap = token_cap // 2
-    lines_at = token_cap + half_cap
-    me = lax.axis_index("seq")
+def place_rows(token_cap, rows, pieces, target_ref, grad_ref):
+    local_rows = grad_ref.shape[1]
+    lines_at = token_cap + token_cap // 2
     targets, rows_in = [], []
-    for flip, piece in zip(flips, pieces):
-        sender = jnp.bitwise_xor(me, flip)
+    for index, piece in enumerate(pieces):
         target = target_row(piece[lines_at : lines_at + 16], token_cap, local_rows)
-        target_ref[sender] = target
+        target_ref[index] = target
         targets.append(target)
         value = unfold_half(piece[token_cap:lines_at])
         rows_in.append(jnp.concatenate([piece[:token_cap], value], axis=1))
-        grad_ref[sender] = unfold_half(piece[lines_at + 16 : lines_at + 16 + local_rows // 2])
-    row_id = lax.broadcasted_iota(jnp.int32, (rows, devices * token_cap), 0)
+        grad_ref[index] = unfold_half(piece[lines_at + 16 : lines_at + 16 + local_rows // 2])
+    row_id = lax.broadcasted_iota(jnp.int32, (rows, len(pieces) * token_cap), 0)
     placer = one_hot(row_id == jnp.concatenate(targets, axis=1))
-    total = dot(placer, jnp.concatenate(rows_in, axis=0))
+    return dot(placer, jnp.concatenate(rows_in, axis=0))
+
+
+def early_kernel(token_cap, *refs):
+    pieces, (total_ref, target_ref, grad_ref) = refs[:-3], refs[-3:]
+    total = place_rows(token_cap, total_ref.shape[0], pieces, target_ref, grad_ref)
+    total_ref[...] = total.astype(jnp.bfloat16)
+
+
+def head_kernel(token_cap, flips, early_ref, early_grad_ref, *refs):
+    early = early_grad_ref.shape[0]
+    pieces, refs = refs[: HEADS - early], refs[HEADS - early :]
+    outs, (target_ref, late_grad_ref, grad_ref, attended_ref) = refs[: HEADS // 2], refs[HEADS // 2 :]
+    devices, local_rows = len(flips), grad_ref.shape[1]
+    rows = devices * local_rows
+    scaling = HEAD_DIM ** (-0.5)
+    me = lax.axis_index("seq")
+    total = place_rows(token_cap, rows, pieces, target_ref, late_grad_ref)
+    total = total + early_ref[...].astype(jnp.float32)
+    for index, flip in enumerate(flips):
+        came = early_grad_ref[index] if index < early else late_grad_ref[index - early]
+        grad_ref[jnp.bitwise_xor(me, flip)] = came
     projected = total.astype(jnp.bfloat16)
     query = projected[:, :HEAD_DIM]
     key = projected[:, HEAD_DIM : 2 * HEAD_DIM]
@@ -395,48 +410,63 @@
             out[first : first + local_rows // 2] = attended_ref[place]
 
 
-def block_kernel(flips, target_ref, *refs):
+def block_kernel(early_ref, late_ref, *refs):
     pieces, placed_ref = refs[:-1], refs[-1]
-    token_cap = target_ref.shape[2]
-    width, rows = placed_ref.shape
-    row_id = lax.broadcasted_iota(jnp.int32, (rows, token_cap), 0)
-    total = jnp.zeros((rows, width), jnp.float32)
-    me = lax.axis_index("seq")
-    for flip, piece in zip(flips, pieces):
-        target = target_ref[jnp.bitwise_xor(me, flip)]
-        total = total + dot(one_hot(row_id == target), piece[piece.shape[0] - token_cap :])
-    placed_ref[...] = total.T.astype(jnp.bfloat16)
-
-
-def by_column(left, flips, pieces, held_ref):
+    early, _, token_cap = early_ref.shape
+    rows = placed_ref.shape[1]
+    targets = [early_ref[index] for index in range(early)]
+    targets += [late_ref[index] for index in range(len(pieces) - early)]
+    row_id = lax.broadcasted_iota(jnp.int32, (rows, len(pieces) * token_cap), 0)
+    placer = one_hot(row_id == jnp.concatenate(targets, axis=1))
+    rows_in = [piece[piece.shape[0] - token_cap :] for piece in pieces]
+    placed_ref[...] = dot(placer, jnp.concatenate(rows_in, axis=0)).T.astype(jnp.bfloat16)
+
+
+def head_columns(left, pieces):
     rows = left.shape[1]
     half, end = rows // 2, rows + rows // 2
-    me = lax.axis_index("seq")
-    for flip, piece in zip(flips, pieces):
-        both = dot(left, piece[:rows])
-        low = dot(left[:, :half], piece[rows:end])
-        high = dot(left[:, half:], piece[rows:end])
-        value = low[:, :HEAD_DIM] + high[:, HEAD_DIM:]
-        held_ref[jnp.bitwise_xor(me, flip)] = jnp.concatenate([both, value], axis=1)
+    wide = 2 * HEAD_DIM
+    both = dot(left, jnp.concatenate([piece[:rows] for piece in pieces], axis=1))
+    folded = jnp.concatenate([piece[rows:end] for piece in pieces], axis=1)
+    low, high = dot(left[:, :half], folded), dot(left[:, half:], folded)
+    columns = []
+    for first in range(0, both.shape[1], wide):
+        value = low[:, first : first + HEAD_DIM] + high[:, first + HEAD_DIM : first + wide]
+        columns.append(jnp.concatenate([both[:, first : first + wide], value], axis=1))
+    return columns
+
+
+def in_order(held_ref):
     return jnp.concatenate(
         [
             held_ref[head, :, part * HEAD_DIM : (part + 1) * HEAD_DIM]
             for part in range(3)
-            for head in range(len(pieces))
+            for head in range(held_ref.shape[0])
         ],
         axis=1,
     )
 
 
-def weight_kernel(flips, placed_ref, *refs):
-    pieces, outs, (held_ref, block_ref) = refs[:HEADS], refs[HEADS:-2], refs[-2:]
-    columns = by_column(placed_ref[...], flips, pieces, held_ref).astype(jnp.bfloat16)
+def near_kernel(placed_ref, *refs):
+    pieces, out_ref = refs[:-1], refs[-1]
+    for index, columns in enumerate(head_columns(placed_ref[...], pieces)):
+        out_ref[index] = columns.astype(jnp.bfloat16)
+
+
+def weight_kernel(flips, placed_ref, near_ref, *refs):
+    count = len(flips) - near_ref.shape[0]
+    pieces, outs, (held_ref, block_ref) = refs[:count], refs[count:-2], refs[-2:]
+    seq, clip = lax.axis_index("seq"), lax.axis_index("clip")
+    columns = [near_ref[index] for index in range(near_ref.shape[0])]
+    columns += head_columns(placed_ref[...], pieces)
+    for flip, each in zip(flips, columns):
+        held_ref[jnp.bitwise_xor(seq, flip)] = each.astype(jnp.bfloat16)
+    columns = in_order(held_ref)
     width = columns.shape[1] // len(outs)
-    me = lax.axis_index("clip")
     for index in range(len(outs)):
         block_ref[index] = columns[:, index * width : (index + 1) * width]
     for flip, out in enumerate(outs):
-        out[...] = block_ref[jnp.bitwise_xor(me, flip)]
+        out[...] = block_ref[jnp.bitwise_xor(clip, flip)]
 
 
 def patch_kernel(flips, segment_ref, target_ref, w_hbm, *refs):
@@ -453,7 +483,9 @@
     attended_ref[...] = jnp.concatenate([part_ref[head] for head in range(HEADS)], axis=1)
     row_id = lax.broadcasted_iota(jnp.int32, (rows, token_cap), 0)
     chooser = jnp.where(row_id == target_ref[...], 1.0, 0.0).T.astype(jnp.bfloat16)
-    proj_grad = by_column(chooser, flips, pieces, held_ref).astype(jnp.bfloat16)
+    for flip, columns in zip(flips, head_columns(chooser, pieces)):
+        held_ref[jnp.bitwise_xor(me, flip)] = columns.astype(jnp.bfloat16)
+    proj_grad = in_order(held_ref)
     copy.wait()
     token_grad = dot(proj_grad, w_ref[...], NT).astype(jnp.bfloat16).astype(jnp.float32)
     member = (
@@ -462,10 +494,6 @@
     counts = jnp.sum(jnp.where(member, 1.0, 0.0), axis=1, keepdims=True)
     shared = (token_grad / jnp.maximum(counts, 1.0)).astype(jnp.bfloat16)
     patch_ref[...] = dot(one_hot(member), shared, TN).astype(jnp.bfloat16)
-
-
-def copy_kernel(source_ref, target_ref):
-    target_ref[...] = source_ref[...]
 
 
 def sum_kernel(*refs):
@@ -517,17 +545,30 @@
     )
     sends, (target, segment) = list(outs[:devices]), outs[devices:]
     order = sorted(range(devices), key=start_order)
-    sends[0] = call(copy_kernel, shape(sent, 2 * HEAD_DIM), sends[0])
     came = {0: sends[0]}
     for flip in order[1:]:
         came[flip] = exchange(sends[flip], "seq", flip)
     came = [came[flip] for flip in order]
-    *proj, targets = call(
+    early = devices // 2
+    placed, early_targets, early_grads = call(
+        functools.partial(early_kernel, token_cap),
+        [
+            shape(rows, 3 * HEAD_DIM),
+            shape(early, 1, token_cap, dtype=jnp.int32),
+            shape(early, local_rows, HEAD_DIM),
+        ],
+        *came[:early],
+        flops=1_000_000_000,
+    )
+    *proj, late_targets = call(
         functools.partial(head_kernel, token_cap, order),
         [shape(rows + rows // 2 + local_rows, 2 * HEAD_DIM)] * (devices // 2)
-        + [shape(devices, 1, token_cap, dtype=jnp.int32)],
-        *came,
+        + [shape(devices - early, 1, token_cap, dtype=jnp.int32)],
+        placed,
+        early_grads,
+        *came[early:],
         scratch=[
+            pltpu.VMEM((devices - early, local_rows, HEAD_DIM), jnp.bfloat16),
             pltpu.VMEM((devices, local_rows, HEAD_DIM), jnp.bfloat16),
             pltpu.VMEM((devices, local_rows // 2, 2 * HEAD_DIM), jnp.bfloat16),
         ],
@@ -540,16 +581,23 @@
         pieces[flip + 1] = exchange(pieces[flip], "seq", 1)
     flips = order
     pieces = [pieces[flip] for flip in flips]
-    placed = call(
-        functools.partial(block_kernel, order), shape(width, rows), targets, *came
+    placed = call(block_kernel, shape(width, rows), early_targets, late_targets, *came)
+    near = [flip for flip in flips if flip % 2 == 0]
+    far = [flip for flip in flips if flip % 2 == 1]
+    columns = call(
+        near_kernel,
+        shape(len(near), width, 3 * HEAD_DIM),
+        placed,
+        *[pieces[flips.index(flip)] for flip in near],
     )
     weights = call(
-        functools.partial(weight_kernel, flips),
+        functools.partial(weight_kernel, near + far),
         [shape(width, 3 * inner // clips)] * clips,
         placed,
-        *pieces,
+        columns,
+        *[pieces[flips.index(flip)] for flip in far],
         scratch=[
-            pltpu.VMEM((devices, width, 3 * HEAD_DIM), jnp.float32),
+            pltpu.VMEM((devices, width, 3 * HEAD_DIM), jnp.bfloat16),
             pltpu.VMEM((clips, width, 3 * inner // clips), jnp.bfloat16),
         ],
     )
@@ -563,7 +611,7 @@
         w_qkv,
         *pieces,
         scratch=[
-            pltpu.VMEM((devices, token_cap, 3 * HEAD_DIM), jnp.float32),
+            pltpu.VMEM((devices, token_cap, 3 * HEAD_DIM), jnp.bfloat16),
             pltpu.VMEM((devices, local_rows, HEAD_DIM), jnp.bfloat16),
             pltpu.VMEM(w_qkv.shape, w_qkv.dtype),
             pltpu.SemaphoreType.DMA(()),

time: 51.4 us -> 50.6 us (0.984)
    pallas_call x7 -> x8, Pallas kernels: 12.5 us -> 12.1 us  [call(): pl.pallas_call(body, out_shape=outs, in_specs=[pl.BlockSpec(memory_space=...]
  transfers between devices with their start and end apart: 17 -> 17, of which waited for: 11 -> 10; matrix products, arithmetic and copies ran while one was open for 0% -> 0% of each run, Pallas kernels for 9% -> 10%
where the time goes in v5:
time: 50.6 us; the launch traced here: 50.5 us
  waiting for transfers between devices  21.6 us (43%)
  starting transfers between devices  15.1 us (30%)
  Pallas kernels  12.1 us (24%)
  local copies, waits for them, and re-layouts  0.92 us (2%)
  between operations  0.75 us (1%)
    ppermute x17, waiting for transfers between devices, exchange(): lax.ppermute(rows, axis, [(index, index ^ flip) for index in range(count)])  21.6 us
    ppermute x17, starting transfers between devices, exchange(): lax.ppermute(rows, axis, [(index, index ^ flip) for index in range(count)])  15.1 us
    pallas_call x8, Pallas kernels, call(): pl.pallas_call(body, out_shape=outs, in_specs=[pl.BlockSpec(memory_space=...  12.1 us
  transfers between devices with their start and end apart: 17, of which 10 were waited for; matrix products, arithmetic and copies ran while one was open for 0% of the time, Pallas kernels for 10%

profile of v5, /device:TPU:0, one launch (start us, length us, event | category | flops | bytes accessed | tf_op | source)
XLA Modules:
  0.0 50.5 jit_solution(17253782518303370345)
XLA Ops:
  0.6 3.9 %shard_map.85 = (bf16[528,128]{1,0:T(8,128)(2,1)}, bf16[528,128]{1,0:T(8,128)(2,1)}, bf16[528,128]{1,0:T(8,128)(2,1)}, bf16[528,128]{1,0:T(8,128)(2,1)}, bf16[52...) custom-call(s32[1,196]{1,0:T(1,128)} %refs_0_.1, ...), custom_call_target="tpu_custom_call" | custom-call | tf_op jit(solution)/shard_map/pallas_call | solution.py:244
  4.6 4.0 %collective-permute-start = (bf16[528,128]{1,0:T(8,128)(2,1)}, bf16[528,128]{1,0:T(8,128)(2,1)S(1)}, u32[]{:S(2)}, u32[]{:S(2)}) collective-permute-start(bf16[528,128]{1,0:T(8,128)(2,1)} %get-tuple-element.30), channel_id=1, source_target_pairs={{0,6},{1,7},{2,4},{3,5},{4,2},{5,3},{6,0},{7,1},{8,14},{9,15},{10,... | collective-permute-start | bytes 405512 | tf_op jit(solution)/shard_map/ppermute | solution.py:508
  8.6 0.0 collective-permute-start.1
  8.6 1.1 %collective-permute-start.2 = (bf16[528,128]{1,0:T(8,128)(2,1)}, bf16[528,128]{1,0:T(8,128)(2,1)S(1)}, u32[]{:S(2)}, u32[]{:S(2)}) collective-permute-start(bf16[528,128]{1,0:T(8,128)(2,1)} %get-tuple-element.32), channel_id=1, source_target_pairs={{0,4},{1,5},{2,6},{3,7},{4,0},{5,1},{6,2},{7,3},{8,12},{9,13},{10,... | collective-permute-start | bytes 405512 | tf_op jit(solution)/shard_map/ppermute | solution.py:508
  9.7 1.5 %collective-permute-start.3 = (bf16[528,128]{1,0:T(8,128)(2,1)}, bf16[528,128]{1,0:T(8,128)(2,1)S(1)}, u32[]{:S(2)}, u32[]{:S(2)}) collective-permute-start(bf16[528,128]{1,0:T(8,128)(2,1)} %get-tuple-element.35), channel_id=1, source_target_pairs={{0,2},{1,3},{2,0},{3,1},{4,6},{5,7},{6,4},{7,5},{8,10},{9,11},{10,... | collective-permute-start | bytes 405512 | tf_op jit(solution)/shard_map/ppermute | solution.py:508
  11.2 0.5 %collective-permute-start.4 = (bf16[528,128]{1,0:T(8,128)(2,1)}, bf16[528,128]{1,0:T(8,128)(2,1)S(1)}, u32[]{:S(2)}, u32[]{:S(2)}) collective-permute-start(bf16[528,128]{1,0:T(8,128)(2,1)} %get-tuple-element.36), channel_id=1, source_target_pairs={{0,5},{1,4},{2,7},{3,6},{4,1},{5,0},{6,3},{7,2},{8,13},{9,12},{10,... | collective-permute-start | bytes 405512 | tf_op jit(solution)/shard_map/ppermute | solution.py:508
  11.7 1.2 %collective-permute-done.refs_1_ = bf16[528,128]{1,0:T(8,128)(2,1)S(1)} collective-permute-done((bf16[528,128]{1,0:T(8,128)(2,1)}, bf16[528,128]{1,0:T(8,128)(2,1)S(1)}, u32[]{:S(2)}, u32[]{:S(2)}) %collective-permute-start) | collective-permute-done | bytes 135200 | tf_op jit(solution)/shard_map/ppermute | solution.py:508
  12.9 2.9 %collective-permute-done.1.refs_2_ = bf16[528,128]{1,0:T(8,128)(2,1)S(1)} collective-permute-done((bf16[528,128]{1,0:T(8,128)(2,1)}, bf16[528,128]{1,0:T(8,128)(2,1)S(1)}, u32[]{:S(2)}, u32[]{:S(2)}) %collective-permute-start.1) | collective-permute-done | bytes 135200 | tf_op jit(solution)/shard_map/ppermute | solution.py:508
  15.8 2.4 %collective-permute-done.2.refs_3_ = bf16[528,128]{1,0:T(8,128)(2,1)S(1)} collective-permute-done((bf16[528,128]{1,0:T(8,128)(2,1)}, bf16[528,128]{1,0:T(8,128)(2,1)S(1)}, u32[]{:S(2)}, u32[]{:S(2)}) %collective-permute-start.2) | collective-permute-done | bytes 135200 | tf_op jit(solution)/shard_map/ppermute | solution.py:508
  18.2 0.9 %copy-done.1 = bf16[528,128]{1,0:T(8,128)(2,1)S(1)} copy-done((bf16[528,128]{1,0:T(8,128)(2,1)S(1)}, bf16[528,128]{1,0:T(8,128)(2,1)}, u32[]{:S(2)}) %copy-start.1) | copy-done | bytes 135192
  19.1 0.4 shard_map.86
  19.5 0.0 copy-start
  19.6 0.0 copy-start.2
  19.6 1.4 %collective-permute-done.4.refs_1_.refs_5_ = bf16[528,128]{1,0:T(8,128)(2,1)S(1)} collective-permute-done((bf16[528,128]{1,0:T(8,128)(2,1)}, bf16[528,128]{1,0:T(8,128)(2,1)S(1)}, u32[]{:S(2)}, u32[]{:S(2)}) %collective-permute-start.4) | collective-permute-done | bytes 135200 | tf_op jit(solution)/shard_map/ppermute | solution.py:508
  21.0 1.9 %shard_map.87 = (bf16[832,128]{1,0:T(8,128)(2,1)S(1)}, bf16[832,128]{1,0:T(8,128)(2,1)S(1)}, bf16[832,128]{1,0:T(8,128)(2,1)S(1)}, bf16[832,128]{1,0:T(8,128)(2,1)S(1)}, s32[4,1,192]{2,1,0:T(1,128)S(1)}) custom-call(bf16[512,192]{1,0:T(8,128)(2,1)S(1)} %get-tuple-element.33.early_ref, bf16[4,64,64]{2,1,0:T(8,128)(2,1)S(1)} %get-tuple-element.34.early_grad_ref, ...), custom_call_target="tpu_custom_call" | custom-call | tf_op jit(solution)/shard_map/pallas_call | solution.py:244
  22.9 1.8 %collective-permute-start.9 = (bf16[832,128]{1,0:T(8,128)(2,1)S(1)}, bf16[832,128]{1,0:T(8,128)(2,1)S(1)}, u32[]{:S(2)}, u32[]{:S(2)}) collective-permute-start(bf16[832,128]{1,0:T(8,128)(2,1)S(1)} %get-tuple-element.41), channel_id=1, source_target_pairs={{0,4},{1,5},{2,6},{3,7},{4,0},{5,1},{6,2},{7,3},{8,12},{9,13},{10,... | collective-permute-start | bytes 638984 | tf_op jit(solution)/shard_map/ppermute | solution.py:508
  24.7 1.5 %collective-permute-start.10 = (bf16[832,128]{1,0:T(8,128)(2,1)S(1)}, bf16[832,128]{1,0:T(8,128)(2,1)S(1)}, u32[]{:S(2)}, u32[]{:S(2)}) collective-permute-start(bf16[832,128]{1,0:T(8,128)(2,1)S(1)} %get-tuple-element.42), channel_id=1, source_target_pairs={{0,2},{1,3},{2,0},{3,1},{4,6},{5,7},{6,4},{7,5},{8,10},{9,11},{10,... | collective-permute-start | bytes 638984 | tf_op jit(solution)/shard_map/ppermute | solution.py:508
  26.2 0.2 collective-permute-start.7
  26.4 3.8 %collective-permute-done.9.refs_3_.refs_2_ = bf16[832,128]{1,0:T(8,128)(2,1)S(1)} collective-permute-done((bf16[832,128]{1,0:T(8,128)(2,1)S(1)}, bf16[832,128]{1,0:T(8,128)(2,1)S(1)}, u32[]{:S(2)}, u32[]{:S(2)}) %collective-permute-start.9) | collective-permute-done | bytes 213024 | tf_op jit(solution)/shard_map/ppermute | solution.py:508
  30.3 2.6 %collective-permute-done.10.refs_4_.refs_3_ = bf16[832,128]{1,0:T(8,128)(2,1)S(1)} collective-permute-done((bf16[832,128]{1,0:T(8,128)(2,1)S(1)}, bf16[832,128]{1,0:T(8,128)(2,1)S(1)}, u32[]{:S(2)}, u32[]{:S(2)}) %collective-permute-start.10) | collective-permute-done | bytes 213024 | tf_op jit(solution)/shard_map/ppermute | solution.py:508
  32.8 3.2 %collective-permute-done.7.refs_1_ = bf16[832,128]{1,0:T(8,128)(2,1)S(1)} collective-permute-done((bf16[832,128]{1,0:T(8,128)(2,1)S(1)}, bf16[832,128]{1,0:T(8,128)(2,1)S(1)}, u32[]{:S(2)}, u32[]{:S(2)}) %collective-permute-start.7) | collective-permute-done | bytes 213024 | tf_op jit(solution)/shard_map/ppermute | solution.py:508
  36.0 0.7 %shard_map.89.placed_ref = bf16[128,512]{1,0:T(8,128)(2,1)S(1)} custom-call(s32[4,1,192]{2,1,0:T(1,128)S(1)} %get-tuple-element.45.early_ref, s32[4,1,192]{2,1,0:T(1,128)S(1)} %get-tuple-element.46.late_ref, bf16[528,128]{1,0:T(8,128)(2,1)S(1)} %copy-done.1, bf16[528,128]{1,0:T(8,128)(2,1)S(1)} %collective-permute-done.refs_1_, ...), custom_call_target="tpu_custom_call" | custom-call | tf_op jit(solution)/shard_map/pallas_call | solution.py:244
  36.7 0.4 shard_map.90.near_ref
  37.2 0.3 collective-permute-done.8.refs_2_.refs_0_
  37.5 0.6 %shard_map.91 = (bf16[128,384]{1,0:T(8,128)(2,1)S(1)}, bf16[128,384]{1,0:T(8,128)(2,1)S(1)}, bf16[128,384]{1,0:T(8,128)(2,1)S(1)}, bf16[128,384]{1,0:T(8,128)(2,1)S(1)}) custom-call(bf16[128,512]{1,0:T(8,128)(2,1)S(1)} %shard_map.89.placed_ref, bf16[4,128,192]{2,1,0:T(8,128)(2,1)S(1)} %shard_map.90.near_ref, ...), custom_call_target="tpu_custom_call" | custom-call | tf_op jit(solution)/shard_map/pallas_call | solution.py:244
  38.2 2.8 %collective-permute-start.14 = (bf16[128,384]{1,0:T(8,128)(2,1)S(1)}, bf16[128,384]{1,0:T(8,128)(2,1)S(1)}, u32[]{:S(2)}, u32[]{:S(2)}) collective-permute-start(bf16[128,384]{1,0:T(8,128)(2,1)S(1)} %get-tuple-element.48), channel_id=1, source_target_pairs={{0,16},{8,24},{16,0},{24,8},{1,17},{9,25},{17,1},{25,9},{2,18},{10... | collective-permute-start | bytes 294920 | tf_op jit(solution)/shard_map/ppermute | solution.py:508
  40.9 1.3 %collective-permute-start.15 = (bf16[128,384]{1,0:T(8,128)(2,1)S(1)}, bf16[128,384]{1,0:T(8,128)(2,1)S(1)}, u32[]{:S(2)}, u32[]{:S(2)}) collective-permute-start(bf16[128,384]{1,0:T(8,128)(2,1)S(1)} %get-tuple-element.49), channel_id=1, source_target_pairs={{0,24},{8,16},{16,8},{24,0},{1,25},{9,17},{17,9},{25,1},{2,26},{10... | collective-permute-start | bytes 294920 | tf_op jit(solution)/shard_map/ppermute | solution.py:508
  42.3 0.3 collective-permute-start.16
  42.5 3.4 %shard_map.88 = (bf16[196,1024]{1,0:T(8,128)(2,1)}, bf16[64,512]{1,0:T(8,128)(2,1)}) custom-call(s32[1,196]{1,0:T(1,128)S(1)} %copy-done.3, s32[1,192]{1,0:T(1,128)S(1)} %copy-done.2, bf16[1024,1536]{1,0:T(8,128)(2,1)S(1)} %copy-done, bf16[832,128]{1,0:T(8,128)(2,1)S(1)} %get-tuple-element.39.refs_0_, bf16[832,128]{1,0:T(8,128)(2,1)S(1)} %collective-permute-done.7.refs_1_, ...), custom_call_target="tpu_custom_call" | custom-call | tf_op jit(solution)/shard_map/pallas_call | solution.py:244
  45.9 3.1 %collective-permute-done.14.refs_1_ = bf16[128,384]{1,0:T(8,128)(2,1)S(1)} collective-permute-done((bf16[128,384]{1,0:T(8,128)(2,1)S(1)}, bf16[128,384]{1,0:T(8,128)(2,1)S(1)}, u32[]{:S(2)}, u32[]{:S(2)}) %collective-permute-start.14) | collective-permute-done | bytes 98336 | tf_op jit(solution)/shard_map/ppermute | solution.py:508
  49.0 0.7 %collective-permute-done.16.refs_3_ = bf16[128,384]{1,0:T(8,128)(2,1)S(1)} collective-permute-done((bf16[128,384]{1,0:T(8,128)(2,1)S(1)}, bf16[128,384]{1,0:T(8,128)(2,1)S(1)}, u32[]{:S(2)}, u32[]{:S(2)}) %collective-permute-start.16) | collective-permute-done | bytes 98336 | tf_op jit(solution)/shard_map/ppermute | solution.py:508
  49.7 0.7 %shard_map.92 = f32[128,384]{1,0:T(8,128)} custom-call(bf16[128,384]{1,0:T(8,128)(2,1)S(1)} %get-tuple-element.47.refs_0_, bf16[128,384]{1,0:T(8,128)(2,1)S(1)} %collective-permute-done.14.refs_1_, bf16[128,384]{1,0:T(8,128)(2,1)S(1)} %collective-permute-done.15.refs_2_, bf16[128,384]{1,0:T(8,128)(2,1)S(1)} %collective-permute-done.16.refs_3_), custom_call_target="tpu_custom_call" | custom-call | tf_op jit(solution)/shard_map/pallas_call | solution.py:244
  (18 shorter events, 0.0 us)
Async XLA Ops:
  4.6 8.3 %collective-permute-start = (bf16[528,128]{1,0:T(8,128)(2,1)}, bf16[528,128]{1,0:T(8,128)(2,1)S(1)}, u32[]{:S(2)}, u32[]{:S(2)}) collective-permute-start(bf16[528,128]{1,0:T(8,128)(2,1)} %get-tuple-element.30), channel_id=1, source_target_pairs={{0,6},{1,7},{2,4},{3,5},{4,2},{5,3},{6,0},{7,1},{8,14},{9,15},{10,... | collective-permute-start | bytes 405512 | tf_op jit(solution)/shard_map/ppermute | solution.py:508
  8.6 7.2 %collective-permute-start.1 = (bf16[528,128]{1,0:T(8,128)(2,1)}, bf16[528,128]{1,0:T(8,128)(2,1)S(1)}, u32[]{:S(2)}, u32[]{:S(2)}) collective-permute-start(bf16[528,128]{1,0:T(8,128)(2,1)} %get-tuple-element.31), channel_id=1, source_target_pairs={{0,7},{1,6},{2,5},{3,4},{4,3},{5,2},{6,1},{7,0},{8,15},{9,14},{10,... | collective-permute-start | bytes 405512 | tf_op jit(solution)/shard_map/ppermute | solution.py:508
  8.6 9.6 %collective-permute-start.2 = (bf16[528,128]{1,0:T(8,128)(2,1)}, bf16[528,128]{1,0:T(8,128)(2,1)S(1)}, u32[]{:S(2)}, u32[]{:S(2)}) collective-permute-start(bf16[528,128]{1,0:T(8,128)(2,1)} %get-tuple-element.32), channel_id=1, source_target_pairs={{0,4},{1,5},{2,6},{3,7},{4,0},{5,1},{6,2},{7,3},{8,12},{9,13},{10,... | collective-permute-start | bytes 405512 | tf_op jit(solution)/shard_map/ppermute | solution.py:508
  9.7 9.9 %collective-permute-start.3 = (bf16[528,128]{1,0:T(8,128)(2,1)}, bf16[528,128]{1,0:T(8,128)(2,1)S(1)}, u32[]{:S(2)}, u32[]{:S(2)}) collective-permute-start(bf16[528,128]{1,0:T(8,128)(2,1)} %get-tuple-element.35), channel_id=1, source_target_pairs={{0,2},{1,3},{2,0},{3,1},{4,6},{5,7},{6,4},{7,5},{8,10},{9,11},{10,... | collective-permute-start | bytes 405512 | tf_op jit(solution)/shard_map/ppermute | solution.py:508
  11.2 9.8 %collective-permute-start.4 = (bf16[528,128]{1,0:T(8,128)(2,1)}, bf16[528,128]{1,0:T(8,128)(2,1)S(1)}, u32[]{:S(2)}, u32[]{:S(2)}) collective-permute-start(bf16[528,128]{1,0:T(8,128)(2,1)} %get-tuple-element.36), channel_id=1, source_target_pairs={{0,5},{1,4},{2,7},{3,6},{4,1},{5,0},{6,3},{7,2},{8,13},{9,12},{10,... | collective-permute-start | bytes 405512 | tf_op jit(solution)/shard_map/ppermute | solution.py:508
  12.9 8.1 %collective-permute-start.5 = (bf16[528,128]{1,0:T(8,128)(2,1)}, bf16[528,128]{1,0:T(8,128)(2,1)S(1)}, u32[]{:S(2)}, u32[]{:S(2)}) collective-permute-start(bf16[528,128]{1,0:T(8,128)(2,1)} %get-tuple-element.37), channel_id=1, source_target_pairs={{0,3},{1,2},{2,1},{3,0},{4,7},{5,6},{6,5},{7,4},{8,11},{9,10},{10,... | collective-permute-start | bytes 405512 | tf_op jit(solution)/shard_map/ppermute | solution.py:508
  15.8 5.2 %collective-permute-start.6 = (bf16[528,128]{1,0:T(8,128)(2,1)}, bf16[528,128]{1,0:T(8,128)(2,1)S(1)}, u32[]{:S(2)}, u32[]{:S(2)}) collective-permute-start(bf16[528,128]{1,0:T(8,128)(2,1)} %get-tuple-element.38), channel_id=1, source_target_pairs={{0,1},{1,0},{2,3},{3,2},{4,5},{5,4},{6,7},{7,6},{8,9},{9,8},{10,11... | collective-permute-start | bytes 405512 | tf_op jit(solution)/shard_map/ppermute | solution.py:508
  18.2 0.9 %copy-start.1 = (bf16[528,128]{1,0:T(8,128)(2,1)S(1)}, bf16[528,128]{1,0:T(8,128)(2,1)}, u32[]{:S(2)}) copy-start(bf16[528,128]{1,0:T(8,128)(2,1)} %get-tuple-element.29.refs_0_) | copy-start | bytes 405508
  19.5 23.0 %copy-start = (bf16[1024,1536]{1,0:T(8,128)(2,1)S(1)}, bf16[1024,1536]{1,0:T(8,128)(2,1)}, u32[]{:S(2)}) copy-start(bf16[1024,1536]{1,0:T(8,128)(2,1)} %w_hbm.1) | copy-start | bytes 9437188
  19.6 23.0 %copy-start.2 = (s32[1,192]{1,0:T(1,128)S(1)}, s32[1,192]{1,0:T(1,128)}, u32[]{:S(2)}) copy-start(s32[1,192]{1,0:T(1,128)} %get-tuple-element.28.target_ref) | copy-start | bytes 2308
  19.6 23.0 %copy-start.3 = (s32[1,196]{1,0:T(1,128)S(1)}, s32[1,196]{1,0:T(1,128)}, u32[]{:S(2)}) copy-start(s32[1,196]{1,0:T(1,128)} %get-tuple-element.27.segment_ref) | copy-start | bytes 2356
  22.9 7.4 %collective-permute-start.9 = (bf16[832,128]{1,0:T(8,128)(2,1)S(1)}, bf16[832,128]{1,0:T(8,128)(2,1)S(1)}, u32[]{:S(2)}, u32[]{:S(2)}) collective-permute-start(bf16[832,128]{1,0:T(8,128)(2,1)S(1)} %get-tuple-element.41), channel_id=1, source_target_pairs={{0,4},{1,5},{2,6},{3,7},{4,0},{5,1},{6,2},{7,3},{8,12},{9,13},{10,... | collective-permute-start | bytes 638984 | tf_op jit(solution)/shard_map/ppermute | solution.py:508
  24.7 8.1 %collective-permute-start.10 = (bf16[832,128]{1,0:T(8,128)(2,1)S(1)}, bf16[832,128]{1,0:T(8,128)(2,1)S(1)}, u32[]{:S(2)}, u32[]{:S(2)}) collective-permute-start(bf16[832,128]{1,0:T(8,128)(2,1)S(1)} %get-tuple-element.42), channel_id=1, source_target_pairs={{0,2},{1,3},{2,0},{3,1},{4,6},{5,7},{6,4},{7,5},{8,10},{9,11},{10,... | collective-permute-start | bytes 638984 | tf_op jit(solution)/shard_map/ppermute | solution.py:508
  26.2 9.9 %collective-permute-start.7 = (bf16[832,128]{1,0:T(8,128)(2,1)S(1)}, bf16[832,128]{1,0:T(8,128)(2,1)S(1)}, u32[]{:S(2)}, u32[]{:S(2)}) collective-permute-start(bf16[832,128]{1,0:T(8,128)(2,1)S(1)} %get-tuple-element.40), channel_id=1, source_target_pairs={{0,6},{1,7},{2,4},{3,5},{4,2},{5,3},{6,0},{7,1},{8,14},{9,15},{10,... | collective-permute-start | bytes 638984 | tf_op jit(solution)/shard_map/ppermute | solution.py:508
  26.4 10.7 %collective-permute-start.13 = (bf16[832,128]{1,0:T(8,128)(2,1)S(1)}, bf16[832,128]{1,0:T(8,128)(2,1)S(1)}, u32[]{:S(2)}, u32[]{:S(2)}) collective-permute-start(bf16[832,128]{1,0:T(8,128)(2,1)S(1)} %get-tuple-element.39.refs_0_), channel_id=1, source_target_pairs={{0,1},{1,0},{2,3},{3,2},{4,5},{5,4},{6,7},{7,6},{8,9},{9,8},{10,11... | collective-permute-start | bytes 638984 | tf_op jit(solution)/shard_map/ppermute | solution.py:508
  30.3 6.9 %collective-permute-start.11 = (bf16[832,128]{1,0:T(8,128)(2,1)S(1)}, bf16[832,128]{1,0:T(8,128)(2,1)S(1)}, u32[]{:S(2)}, u32[]{:S(2)}) collective-permute-start(bf16[832,128]{1,0:T(8,128)(2,1)S(1)} %collective-permute-done.9.refs_3_.refs_2_), channel_id=1, source_target_pairs={{0,1},{1,0},{2,3},{3,2},{4,5},{5,4},{6,7},{7,6},{8,9},{9,8},{10,11... | collective-permute-start | bytes 638984 | tf_op jit(solution)/shard_map/ppermute | solution.py:508
  32.8 4.3 %collective-permute-start.12 = (bf16[832,128]{1,0:T(8,128)(2,1)S(1)}, bf16[832,128]{1,0:T(8,128)(2,1)S(1)}, u32[]{:S(2)}, u32[]{:S(2)}) collective-permute-start(bf16[832,128]{1,0:T(8,128)(2,1)S(1)} %collective-permute-done.10.refs_4_.refs_3_), channel_id=1, source_target_pairs={{0,1},{1,0},{2,3},{3,2},{4,5},{5,4},{6,7},{7,6},{8,9},{9,8},{10,11... | collective-permute-start | bytes 638984 | tf_op jit(solution)/shard_map/ppermute | solution.py:508
  36.0 1.5 %collective-permute-start.8 = (bf16[832,128]{1,0:T(8,128)(2,1)S(1)}, bf16[832,128]{1,0:T(8,128)(2,1)S(1)}, u32[]{:S(2)}, u32[]{:S(2)}) collective-permute-start(bf16[832,128]{1,0:T(8,128)(2,1)S(1)} %collective-permute-done.7.refs_1_), channel_id=1, source_target_pairs={{0,1},{1,0},{2,3},{3,2},{4,5},{5,4},{6,7},{7,6},{8,9},{9,8},{10,11... | collective-permute-start | bytes 638984 | tf_op jit(solution)/shard_map/ppermute | solution.py:508
  38.2 10.8 %collective-permute-start.14 = (bf16[128,384]{1,0:T(8,128)(2,1)S(1)}, bf16[128,384]{1,0:T(8,128)(2,1)S(1)}, u32[]{:S(2)}, u32[]{:S(2)}) collective-permute-start(bf16[128,384]{1,0:T(8,128)(2,1)S(1)} %get-tuple-element.48), channel_id=1, source_target_pairs={{0,16},{8,24},{16,0},{24,8},{1,17},{9,25},{17,1},{25,9},{2,18},{10... | collective-permute-start | bytes 294920 | tf_op jit(solution)/shard_map/ppermute | solution.py:508
  40.9 8.1 %collective-permute-start.15 = (bf16[128,384]{1,0:T(8,128)(2,1)S(1)}, bf16[128,384]{1,0:T(8,128)(2,1)S(1)}, u32[]{:S(2)}, u32[]{:S(2)}) collective-permute-start(bf16[128,384]{1,0:T(8,128)(2,1)S(1)} %get-tuple-element.49), channel_id=1, source_target_pairs={{0,24},{8,16},{16,8},{24,0},{1,25},{9,17},{17,9},{25,1},{2,26},{10... | collective-permute-start | bytes 294920 | tf_op jit(solution)/shard_map/ppermute | solution.py:508
  42.3 7.5 %collective-permute-start.16 = (bf16[128,384]{1,0:T(8,128)(2,1)S(1)}, bf16[128,384]{1,0:T(8,128)(2,1)S(1)}, u32[]{:S(2)}, u32[]{:S(2)}) collective-permute-start(bf16[128,384]{1,0:T(8,128)(2,1)S(1)} %get-tuple-element.50), channel_id=1, source_target_pairs={{0,8},{8,0},{16,24},{24,16},{1,9},{9,1},{17,25},{25,17},{2,10},{10... | collective-permute-start | bytes 294920 | tf_op jit(solution)/shard_map/ppermute | solution.py:508

commit v6 on v5

--- a/solution.py
+++ b/solution.py
@@ -239,12 +239,14 @@
     return lax.dot_general(left, right, dims, preferred_element_type=jnp.float32)
 
 
-def call(body, outs, *args, scratch=(), space=None, limit=VMEM_LIMIT, flops=0):
+def call(body, outs, *args, scratch=(), space=None, limit=VMEM_LIMIT, outer=None, alias={}, flops=0):
     space = space or [pltpu.VMEM] * len(args)
     return pl.pallas_call(
         body,
         out_shape=outs,
         in_specs=[pl.BlockSpec(memory_space=each) for each in space],
+        out_specs=jax.tree.map(lambda _: pl.BlockSpec(memory_space=outer or pltpu.VMEM), outs),
+        input_output_aliases=alias,
         scratch_shapes=scratch,
         cost_estimate=pl.CostEstimate(flops=flops, bytes_accessed=0, transcendentals=0),
         compiler_params=pltpu.CompilerParams(vmem_limit_bytes=limit),
@@ -496,6 +498,10 @@
     patch_ref[...] = dot(one_hot(member), shared, TN).astype(jnp.bfloat16)
 
 
+def follow_kernel(*refs):
+    pass
+
+
 def sum_kernel(*refs):
     total = refs[0][...].astype(jnp.float32)
     for ref in refs[1:-1]:
@@ -577,13 +583,23 @@
     for flip in order[1:]:
         if flip % 2 == 0:
             pieces[flip] = exchange(proj[flip // 2], "seq", flip)
+    placed = call(block_kernel, shape(width, rows), early_targets, late_targets, *came)
+    first = devices // 2
+    pieces[first] = call(
+        follow_kernel,
+        shape(*pieces[first].shape),
+        pieces[first],
+        placed,
+        space=[pl.ANY] * 2,
+        outer=pl.ANY,
+        alias={0: 0},
+    )
     for flip in list(pieces):
         pieces[flip + 1] = exchange(pieces[flip], "seq", 1)
-    flips = order
+    flips = [chip ^ core for chip in range(devices - 2, -1, -2) for core in range(2)]
     pieces = [pieces[flip] for flip in flips]
-    placed = call(block_kernel, shape(width, rows), early_targets, late_targets, *came)
-    near = [flip for flip in flips if flip % 2 == 0]
-    far = [flip for flip in flips if flip % 2 == 1]
+    far = [devices - 1]
+    near = [flip for flip in order if flip not in far]
     columns = call(
         near_kernel,
         shape(len(near), width, 3 * HEAD_DIM),
@@ -601,7 +617,7 @@
             pltpu.VMEM((clips, width, 3 * inner // clips), jnp.bfloat16),
         ],
     )
-    clip_flips = sorted(range(1, clips), key=lambda flip: (flip < clips // 2, flip))
+    clip_flips = sorted(range(1, clips), key=lambda flip: (flip != clips // 2, flip))
     weights = [weights[0]] + [exchange(weights[flip], "clip", flip) for flip in clip_flips]
     patch_grad, attended = call(
         functools.partial(patch_kernel, flips),

time: 50.6 us -> 50.2 us (level)
    pallas_call x8 -> x9, Pallas kernels: 12.1 us -> 12.2 us  [call(): pl.pallas_call(body, out_shape=outs, in_specs=[pl.BlockSpec(memory_space=...]
where the time goes in v6:
time: 50.2 us; the launch traced here: 50 us
  waiting for transfers between devices  21.1 us (42%)
  starting transfers between devices  15.2 us (30%)
  Pallas kernels  12.2 us (24%)
  local copies, waits for them, and re-layouts  0.92 us (2%)
  between operations  0.73 us (1%)
    ppermute x17, waiting for transfers between devices, exchange(): lax.ppermute(rows, axis, [(index, index ^ flip) for index in range(count)])  21.1 us
    ppermute x17, starting transfers between devices, exchange(): lax.ppermute(rows, axis, [(index, index ^ flip) for index in range(count)])  15.2 us
    pallas_call x9, Pallas kernels, call(): pl.pallas_call(body, out_shape=outs, in_specs=[pl.BlockSpec(memory_space=...  12.2 us
  transfers between devices with their start and end apart: 17, of which 10 were waited for; matrix products, arithmetic and copies ran while one was open for 0% of the time, Pallas kernels for 10%

profile of v6, /device:TPU:0, one launch (start us, length us, event | category | flops | bytes accessed | tf_op | source)
XLA Modules:
  0.0 50.0 jit_solution(10438364895707150590)
XLA Ops:
  0.6 3.9 %shard_map.85 = (bf16[528,128]{1,0:T(8,128)(2,1)}, bf16[528,128]{1,0:T(8,128)(2,1)}, bf16[528,128]{1,0:T(8,128)(2,1)}, bf16[528,128]{1,0:T(8,128)(2,1)}, bf16[52...) custom-call(s32[1,196]{1,0:T(1,128)} %refs_0_.1, ...), custom_call_target="tpu_custom_call" | custom-call | tf_op jit(solution)/shard_map/pallas_call | solution.py:244
  4.6 4.0 %collective-permute-start = (bf16[528,128]{1,0:T(8,128)(2,1)}, bf16[528,128]{1,0:T(8,128)(2,1)S(1)}, u32[]{:S(2)}, u32[]{:S(2)}) collective-permute-start(bf16[528,128]{1,0:T(8,128)(2,1)} %get-tuple-element.30), channel_id=1, source_target_pairs={{0,6},{1,7},{2,4},{3,5},{4,2},{5,3},{6,0},{7,1},{8,14},{9,15},{10,... | collective-permute-start | bytes 405512 | tf_op jit(solution)/shard_map/ppermute | solution.py:514
  8.6 0.0 collective-permute-start.1
  8.6 1.1 %collective-permute-start.2 = (bf16[528,128]{1,0:T(8,128)(2,1)}, bf16[528,128]{1,0:T(8,128)(2,1)S(1)}, u32[]{:S(2)}, u32[]{:S(2)}) collective-permute-start(bf16[528,128]{1,0:T(8,128)(2,1)} %get-tuple-element.32), channel_id=1, source_target_pairs={{0,4},{1,5},{2,6},{3,7},{4,0},{5,1},{6,2},{7,3},{8,12},{9,13},{10,... | collective-permute-start | bytes 405512 | tf_op jit(solution)/shard_map/ppermute | solution.py:514
  9.7 1.5 %collective-permute-start.3 = (bf16[528,128]{1,0:T(8,128)(2,1)}, bf16[528,128]{1,0:T(8,128)(2,1)S(1)}, u32[]{:S(2)}, u32[]{:S(2)}) collective-permute-start(bf16[528,128]{1,0:T(8,128)(2,1)} %get-tuple-element.35), channel_id=1, source_target_pairs={{0,2},{1,3},{2,0},{3,1},{4,6},{5,7},{6,4},{7,5},{8,10},{9,11},{10,... | collective-permute-start | bytes 405512 | tf_op jit(solution)/shard_map/ppermute | solution.py:514
  11.2 0.5 %collective-permute-start.4 = (bf16[528,128]{1,0:T(8,128)(2,1)}, bf16[528,128]{1,0:T(8,128)(2,1)S(1)}, u32[]{:S(2)}, u32[]{:S(2)}) collective-permute-start(bf16[528,128]{1,0:T(8,128)(2,1)} %get-tuple-element.36), channel_id=1, source_target_pairs={{0,5},{1,4},{2,7},{3,6},{4,1},{5,0},{6,3},{7,2},{8,13},{9,12},{10,... | collective-permute-start | bytes 405512 | tf_op jit(solution)/shard_map/ppermute | solution.py:514
  11.7 1.2 %collective-permute-done.refs_1_ = bf16[528,128]{1,0:T(8,128)(2,1)S(1)} collective-permute-done((bf16[528,128]{1,0:T(8,128)(2,1)}, bf16[528,128]{1,0:T(8,128)(2,1)S(1)}, u32[]{:S(2)}, u32[]{:S(2)}) %collective-permute-start) | collective-permute-done | bytes 135200 | tf_op jit(solution)/shard_map/ppermute | solution.py:514
  12.9 2.9 %collective-permute-done.1.refs_2_ = bf16[528,128]{1,0:T(8,128)(2,1)S(1)} collective-permute-done((bf16[528,128]{1,0:T(8,128)(2,1)}, bf16[528,128]{1,0:T(8,128)(2,1)S(1)}, u32[]{:S(2)}, u32[]{:S(2)}) %collective-permute-start.1) | collective-permute-done | bytes 135200 | tf_op jit(solution)/shard_map/ppermute | solution.py:514
  15.8 2.4 %collective-permute-done.2.refs_3_ = bf16[528,128]{1,0:T(8,128)(2,1)S(1)} collective-permute-done((bf16[528,128]{1,0:T(8,128)(2,1)}, bf16[528,128]{1,0:T(8,128)(2,1)S(1)}, u32[]{:S(2)}, u32[]{:S(2)}) %collective-permute-start.2) | collective-permute-done | bytes 135200 | tf_op jit(solution)/shard_map/ppermute | solution.py:514
  18.2 0.9 %copy-done.1 = bf16[528,128]{1,0:T(8,128)(2,1)S(1)} copy-done((bf16[528,128]{1,0:T(8,128)(2,1)S(1)}, bf16[528,128]{1,0:T(8,128)(2,1)}, u32[]{:S(2)}) %copy-start.1) | copy-done | bytes 135192
  19.1 0.4 shard_map.86
  19.5 0.0 copy-start
  19.6 0.0 copy-start.2
  19.6 1.4 %collective-permute-done.4.refs_1_.refs_5_ = bf16[528,128]{1,0:T(8,128)(2,1)S(1)} collective-permute-done((bf16[528,128]{1,0:T(8,128)(2,1)}, bf16[528,128]{1,0:T(8,128)(2,1)S(1)}, u32[]{:S(2)}, u32[]{:S(2)}) %collective-permute-start.4) | collective-permute-done | bytes 135200 | tf_op jit(solution)/shard_map/ppermute | solution.py:514
  21.0 1.9 %shard_map.87 = (bf16[832,128]{1,0:T(8,128)(2,1)S(1)}, bf16[832,128]{1,0:T(8,128)(2,1)S(1)}, bf16[832,128]{1,0:T(8,128)(2,1)S(1)}, bf16[832,128]{1,0:T(8,128)(2,1)S(1)}, s32[4,1,192]{2,1,0:T(1,128)S(1)}) custom-call(bf16[512,192]{1,0:T(8,128)(2,1)S(1)} %get-tuple-element.33.early_ref, bf16[4,64,64]{2,1,0:T(8,128)(2,1)S(1)} %get-tuple-element.34.early_grad_ref, ...), custom_call_target="tpu_custom_call" | custom-call | tf_op jit(solution)/shard_map/pallas_call | solution.py:244
  22.9 1.8 %collective-permute-start.9 = (bf16[832,128]{1,0:T(8,128)(2,1)S(1)}, bf16[832,128]{1,0:T(8,128)(2,1)S(1)}, u32[]{:S(2)}, u32[]{:S(2)}) collective-permute-start(bf16[832,128]{1,0:T(8,128)(2,1)S(1)} %get-tuple-element.40), channel_id=1, source_target_pairs={{0,4},{1,5},{2,6},{3,7},{4,0},{5,1},{6,2},{7,3},{8,12},{9,13},{10,... | collective-permute-start | bytes 638984 | tf_op jit(solution)/shard_map/ppermute | solution.py:514
  24.7 1.5 %collective-permute-start.11 = (bf16[832,128]{1,0:T(8,128)(2,1)S(1)}, bf16[832,128]{1,0:T(8,128)(2,1)S(1)}, u32[]{:S(2)}, u32[]{:S(2)}) collective-permute-start(bf16[832,128]{1,0:T(8,128)(2,1)S(1)} %get-tuple-element.43), channel_id=1, source_target_pairs={{0,2},{1,3},{2,0},{3,1},{4,6},{5,7},{6,4},{7,5},{8,10},{9,11},{10,... | collective-permute-start | bytes 638984 | tf_op jit(solution)/shard_map/ppermute | solution.py:514
  26.2 0.2 collective-permute-start.7
  26.4 0.7 %shard_map.88.refs_1_.placed_ref = bf16[128,512]{1,0:T(8,128)(2,1)S(1)} custom-call(s32[4,1,192]{2,1,0:T(1,128)S(1)} %get-tuple-element.41.early_ref, s32[4,1,192]{2,1,0:T(1,128)S(1)} %get-tuple-element.42.late_ref, bf16[528,128]{1,0:T(8,128)(2,1)S(1)} %copy-done.1, bf16[528,128]{1,0:T(8,128)(2,1)S(1)} %collective-permute-done.refs_1_, ...), custom_call_target="tpu_custom_call" | custom-call | tf_op jit(solution)/shard_map/pallas_call | solution.py:244
  27.1 3.1 %collective-permute-done.9.refs_0_ = bf16[832,128]{1,0:T(8,128)(2,1)S(1)} collective-permute-done((bf16[832,128]{1,0:T(8,128)(2,1)S(1)}, bf16[832,128]{1,0:T(8,128)(2,1)S(1)}, u32[]{:S(2)}, u32[]{:S(2)}) %collective-permute-start.9) | collective-permute-done | bytes 213024 | tf_op jit(solution)/shard_map/ppermute | solution.py:514
  30.3 2.6 %collective-permute-done.11.refs_4_.refs_3_ = bf16[832,128]{1,0:T(8,128)(2,1)S(1)} collective-permute-done((bf16[832,128]{1,0:T(8,128)(2,1)S(1)}, bf16[832,128]{1,0:T(8,128)(2,1)S(1)}, u32[]{:S(2)}, u32[]{:S(2)}) %collective-permute-start.11) | collective-permute-done | bytes 213024 | tf_op jit(solution)/shard_map/ppermute | solution.py:514
  32.8 3.2 %collective-permute-done.7.refs_0_.refs_1_ = bf16[832,128]{1,0:T(8,128)(2,1)S(1)} collective-permute-done((bf16[832,128]{1,0:T(8,128)(2,1)S(1)}, bf16[832,128]{1,0:T(8,128)(2,1)S(1)}, u32[]{:S(2)}, u32[]{:S(2)}) %collective-permute-start.7) | collective-permute-done | bytes 213024 | tf_op jit(solution)/shard_map/ppermute | solution.py:514
  36.1 0.6 %shard_map.91.near_ref = bf16[7,128,192]{2,1,0:T(8,128)(2,1)S(1)} custom-call(bf16[128,512]{1,0:T(8,128)(2,1)S(1)} %shard_map.88.refs_1_.placed_ref, bf16[832,128]{1,0:T(8,128)(2,1)S(1)} %get-tuple-element.44.refs_6_.refs_0_, bf16[832,128]{1,0:T(8,128)(2,1)S(1)} %collective-permute-done.7.refs_0_.refs_1_, bf16[832,128]{1,0:T(8,128)(2,1)S(1)} %shard_map.89.refs_2_, ...), custom_call_target="tpu_custom_call" | custom-call | tf_op jit(solution)/shard_map/pallas_call | solution.py:244
  36.6 0.9 %collective-permute-done.8.refs_1_.refs_0_ = bf16[832,128]{1,0:T(8,128)(2,1)S(1)} collective-permute-done((bf16[832,128]{1,0:T(8,128)(2,1)S(1)}, bf16[832,128]{1,0:T(8,128)(2,1)S(1)}, u32[]{:S(2)}, u32[]{:S(2)}) %collective-permute-start.8) | collective-permute-done | bytes 213024 | tf_op jit(solution)/shard_map/ppermute | solution.py:514
  37.5 0.5 %shard_map.92 = (bf16[128,384]{1,0:T(8,128)(2,1)S(1)}, bf16[128,384]{1,0:T(8,128)(2,1)S(1)}, bf16[128,384]{1,0:T(8,128)(2,1)S(1)}, bf16[128,384]{1,0:T(8,128)(2,1)S(1)}) custom-call(bf16[128,512]{1,0:T(8,128)(2,1)S(1)} %shard_map.88.refs_1_.placed_ref, bf16[7,128,192]{2,1,0:T(8,128)(2,1)S(1)} %shard_map.91.near_ref, ...), custom_call_target="tpu_custom_call" | custom-call | tf_op jit(solution)/shard_map/pallas_call | solution.py:244
  38.0 2.8 %collective-permute-start.14 = (bf16[128,384]{1,0:T(8,128)(2,1)S(1)}, bf16[128,384]{1,0:T(8,128)(2,1)S(1)}, u32[]{:S(2)}, u32[]{:S(2)}) collective-permute-start(bf16[128,384]{1,0:T(8,128)(2,1)S(1)} %get-tuple-element.48), channel_id=1, source_target_pairs={{0,16},{8,24},{16,0},{24,8},{1,17},{9,25},{17,1},{25,9},{2,18},{10... | collective-permute-start | bytes 294920 | tf_op jit(solution)/shard_map/ppermute | solution.py:514
  40.8 1.6 %collective-permute-start.15 = (bf16[128,384]{1,0:T(8,128)(2,1)S(1)}, bf16[128,384]{1,0:T(8,128)(2,1)S(1)}, u32[]{:S(2)}, u32[]{:S(2)}) collective-permute-start(bf16[128,384]{1,0:T(8,128)(2,1)S(1)} %get-tuple-element.49), channel_id=1, source_target_pairs={{0,8},{8,0},{16,24},{24,16},{1,9},{9,1},{17,25},{25,17},{2,10},{10... | collective-permute-start | bytes 294920 | tf_op jit(solution)/shard_map/ppermute | solution.py:514
  42.4 0.1 collective-permute-start.16
  42.5 3.4 %shard_map.90 = (bf16[196,1024]{1,0:T(8,128)(2,1)}, bf16[64,512]{1,0:T(8,128)(2,1)}) custom-call(s32[1,196]{1,0:T(1,128)S(1)} %copy-done.3, s32[1,192]{1,0:T(1,128)S(1)} %copy-done.2, bf16[1024,1536]{1,0:T(8,128)(2,1)S(1)} %copy-done, bf16[832,128]{1,0:T(8,128)(2,1)S(1)} %collective-permute-done.7.refs_0_.refs_1_, ...), custom_call_target="tpu_custom_call" | custom-call | tf_op jit(solution)/shard_map/pallas_call | solution.py:244
  45.9 1.1 %collective-permute-done.14.refs_1_ = bf16[128,384]{1,0:T(8,128)(2,1)S(1)} collective-permute-done((bf16[128,384]{1,0:T(8,128)(2,1)S(1)}, bf16[128,384]{1,0:T(8,128)(2,1)S(1)}, u32[]{:S(2)}, u32[]{:S(2)}) %collective-permute-start.14) | collective-permute-done | bytes 98336 | tf_op jit(solution)/shard_map/ppermute | solution.py:514
  47.0 2.3 %collective-permute-done.16.refs_3_ = bf16[128,384]{1,0:T(8,128)(2,1)S(1)} collective-permute-done((bf16[128,384]{1,0:T(8,128)(2,1)S(1)}, bf16[128,384]{1,0:T(8,128)(2,1)S(1)}, u32[]{:S(2)}, u32[]{:S(2)}) %collective-permute-start.16) | collective-permute-done | bytes 98336 | tf_op jit(solution)/shard_map/ppermute | solution.py:514
  49.3 0.7 %shard_map.93 = f32[128,384]{1,0:T(8,128)} custom-call(bf16[128,384]{1,0:T(8,128)(2,1)S(1)} %get-tuple-element.47.refs_0_, bf16[128,384]{1,0:T(8,128)(2,1)S(1)} %collective-permute-done.14.refs_1_, bf16[128,384]{1,0:T(8,128)(2,1)S(1)} %collective-permute-done.15.refs_2_, bf16[128,384]{1,0:T(8,128)(2,1)S(1)} %collective-permute-done.16.refs_3_), custom_call_target="tpu_custom_call" | custom-call | tf_op jit(solution)/shard_map/pallas_call | solution.py:244
  (19 shorter events, 0.0 us)
Async XLA Ops:
  4.6 8.3 %collective-permute-start = (bf16[528,128]{1,0:T(8,128)(2,1)}, bf16[528,128]{1,0:T(8,128)(2,1)S(1)}, u32[]{:S(2)}, u32[]{:S(2)}) collective-permute-start(bf16[528,128]{1,0:T(8,128)(2,1)} %get-tuple-element.30), channel_id=1, source_target_pairs={{0,6},{1,7},{2,4},{3,5},{4,2},{5,3},{6,0},{7,1},{8,14},{9,15},{10,... | collective-permute-start | bytes 405512 | tf_op jit(solution)/shard_map/ppermute | solution.py:514
  8.6 7.2 %collective-permute-start.1 = (bf16[528,128]{1,0:T(8,128)(2,1)}, bf16[528,128]{1,0:T(8,128)(2,1)S(1)}, u32[]{:S(2)}, u32[]{:S(2)}) collective-permute-start(bf16[528,128]{1,0:T(8,128)(2,1)} %get-tuple-element.31), channel_id=1, source_target_pairs={{0,7},{1,6},{2,5},{3,4},{4,3},{5,2},{6,1},{7,0},{8,15},{9,14},{10,... | collective-permute-start | bytes 405512 | tf_op jit(solution)/shard_map/ppermute | solution.py:514
  8.6 9.6 %collective-permute-start.2 = (bf16[528,128]{1,0:T(8,128)(2,1)}, bf16[528,128]{1,0:T(8,128)(2,1)S(1)}, u32[]{:S(2)}, u32[]{:S(2)}) collective-permute-start(bf16[528,128]{1,0:T(8,128)(2,1)} %get-tuple-element.32), channel_id=1, source_target_pairs={{0,4},{1,5},{2,6},{3,7},{4,0},{5,1},{6,2},{7,3},{8,12},{9,13},{10,... | collective-permute-start | bytes 405512 | tf_op jit(solution)/shard_map/ppermute | solution.py:514
  9.7 9.9 %collective-permute-start.3 = (bf16[528,128]{1,0:T(8,128)(2,1)}, bf16[528,128]{1,0:T(8,128)(2,1)S(1)}, u32[]{:S(2)}, u32[]{:S(2)}) collective-permute-start(bf16[528,128]{1,0:T(8,128)(2,1)} %get-tuple-element.35), channel_id=1, source_target_pairs={{0,2},{1,3},{2,0},{3,1},{4,6},{5,7},{6,4},{7,5},{8,10},{9,11},{10,... | collective-permute-start | bytes 405512 | tf_op jit(solution)/shard_map/ppermute | solution.py:514
  11.2 9.8 %collective-permute-start.4 = (bf16[528,128]{1,0:T(8,128)(2,1)}, bf16[528,128]{1,0:T(8,128)(2,1)S(1)}, u32[]{:S(2)}, u32[]{:S(2)}) collective-permute-start(bf16[528,128]{1,0:T(8,128)(2,1)} %get-tuple-element.36), channel_id=1, source_target_pairs={{0,5},{1,4},{2,7},{3,6},{4,1},{5,0},{6,3},{7,2},{8,13},{9,12},{10,... | collective-permute-start | bytes 405512 | tf_op jit(solution)/shard_map/ppermute | solution.py:514
  12.9 8.1 %collective-permute-start.5 = (bf16[528,128]{1,0:T(8,128)(2,1)}, bf16[528,128]{1,0:T(8,128)(2,1)S(1)}, u32[]{:S(2)}, u32[]{:S(2)}) collective-permute-start(bf16[528,128]{1,0:T(8,128)(2,1)} %get-tuple-element.37), channel_id=1, source_target_pairs={{0,3},{1,2},{2,1},{3,0},{4,7},{5,6},{6,5},{7,4},{8,11},{9,10},{10,... | collective-permute-start | bytes 405512 | tf_op jit(solution)/shard_map/ppermute | solution.py:514
  15.8 5.2 %collective-permute-start.6 = (bf16[528,128]{1,0:T(8,128)(2,1)}, bf16[528,128]{1,0:T(8,128)(2,1)S(1)}, u32[]{:S(2)}, u32[]{:S(2)}) collective-permute-start(bf16[528,128]{1,0:T(8,128)(2,1)} %get-tuple-element.38), channel_id=1, source_target_pairs={{0,1},{1,0},{2,3},{3,2},{4,5},{5,4},{6,7},{7,6},{8,9},{9,8},{10,11... | collective-permute-start | bytes 405512 | tf_op jit(solution)/shard_map/ppermute | solution.py:514
  18.2 0.9 %copy-start.1 = (bf16[528,128]{1,0:T(8,128)(2,1)S(1)}, bf16[528,128]{1,0:T(8,128)(2,1)}, u32[]{:S(2)}) copy-start(bf16[528,128]{1,0:T(8,128)(2,1)} %get-tuple-element.29.refs_0_) | copy-start | bytes 405508
  19.5 22.9 %copy-start = (bf16[1024,1536]{1,0:T(8,128)(2,1)S(1)}, bf16[1024,1536]{1,0:T(8,128)(2,1)}, u32[]{:S(2)}) copy-start(bf16[1024,1536]{1,0:T(8,128)(2,1)} %w_hbm.1) | copy-start | bytes 9437188
  19.6 22.9 %copy-start.2 = (s32[1,192]{1,0:T(1,128)S(1)}, s32[1,192]{1,0:T(1,128)}, u32[]{:S(2)}) copy-start(s32[1,192]{1,0:T(1,128)} %get-tuple-element.28.target_ref) | copy-start | bytes 2308
  19.6 22.9 %copy-start.3 = (s32[1,196]{1,0:T(1,128)S(1)}, s32[1,196]{1,0:T(1,128)}, u32[]{:S(2)}) copy-start(s32[1,196]{1,0:T(1,128)} %get-tuple-element.27.segment_ref) | copy-start | bytes 2356
  22.9 7.4 %collective-permute-start.9 = (bf16[832,128]{1,0:T(8,128)(2,1)S(1)}, bf16[832,128]{1,0:T(8,128)(2,1)S(1)}, u32[]{:S(2)}, u32[]{:S(2)}) collective-permute-start(bf16[832,128]{1,0:T(8,128)(2,1)S(1)} %get-tuple-element.40), channel_id=1, source_target_pairs={{0,4},{1,5},{2,6},{3,7},{4,0},{5,1},{6,2},{7,3},{8,12},{9,13},{10,... | collective-permute-start | bytes 638984 | tf_op jit(solution)/shard_map/ppermute | solution.py:514
  24.7 8.1 %collective-permute-start.11 = (bf16[832,128]{1,0:T(8,128)(2,1)S(1)}, bf16[832,128]{1,0:T(8,128)(2,1)S(1)}, u32[]{:S(2)}, u32[]{:S(2)}) collective-permute-start(bf16[832,128]{1,0:T(8,128)(2,1)S(1)} %get-tuple-element.43), channel_id=1, source_target_pairs={{0,2},{1,3},{2,0},{3,1},{4,6},{5,7},{6,4},{7,5},{8,10},{9,11},{10,... | collective-permute-start | bytes 638984 | tf_op jit(solution)/shard_map/ppermute | solution.py:514
  26.2 9.8 %collective-permute-start.7 = (bf16[832,128]{1,0:T(8,128)(2,1)S(1)}, bf16[832,128]{1,0:T(8,128)(2,1)S(1)}, u32[]{:S(2)}, u32[]{:S(2)}) collective-permute-start(bf16[832,128]{1,0:T(8,128)(2,1)S(1)} %get-tuple-element.39), channel_id=1, source_target_pairs={{0,6},{1,7},{2,4},{3,5},{4,2},{5,3},{6,0},{7,1},{8,14},{9,15},{10,... | collective-permute-start | bytes 638984 | tf_op jit(solution)/shard_map/ppermute | solution.py:514
  26.4 9.6 %collective-permute-start.13 = (bf16[832,128]{1,0:T(8,128)(2,1)S(1)}, bf16[832,128]{1,0:T(8,128)(2,1)S(1)}, u32[]{:S(2)}, u32[]{:S(2)}) collective-permute-start(bf16[832,128]{1,0:T(8,128)(2,1)S(1)} %get-tuple-element.44.refs_6_.refs_0_), channel_id=1, source_target_pairs={{0,1},{1,0},{2,3},{3,2},{4,5},{5,4},{6,7},{7,6},{8,9},{9,8},{10,11... | collective-permute-start | bytes 638984 | tf_op jit(solution)/shard_map/ppermute | solution.py:514
  30.3 5.8 %collective-permute-start.10 = (bf16[832,128]{1,0:T(8,128)(2,1)S(1)}, bf16[832,128]{1,0:T(8,128)(2,1)S(1)}, u32[]{:S(2)}, u32[]{:S(2)}) collective-permute-start(bf16[832,128]{1,0:T(8,128)(2,1)S(1)} %shard_map.89.refs_2_), channel_id=1, source_target_pairs={{0,1},{1,0},{2,3},{3,2},{4,5},{5,4},{6,7},{7,6},{8,9},{9,8},{10,11... | collective-permute-start | bytes 638984 | tf_op jit(solution)/shard_map/ppermute | solution.py:514
  32.8 3.2 %collective-permute-start.12 = (bf16[832,128]{1,0:T(8,128)(2,1)S(1)}, bf16[832,128]{1,0:T(8,128)(2,1)S(1)}, u32[]{:S(2)}, u32[]{:S(2)}) collective-permute-start(bf16[832,128]{1,0:T(8,128)(2,1)S(1)} %collective-permute-done.11.refs_4_.refs_3_), channel_id=1, source_target_pairs={{0,1},{1,0},{2,3},{3,2},{4,5},{5,4},{6,7},{7,6},{8,9},{9,8},{10,11... | collective-permute-start | bytes 638984 | tf_op jit(solution)/shard_map/ppermute | solution.py:514
  36.0 1.5 %collective-permute-start.8 = (bf16[832,128]{1,0:T(8,128)(2,1)S(1)}, bf16[832,128]{1,0:T(8,128)(2,1)S(1)}, u32[]{:S(2)}, u32[]{:S(2)}) collective-permute-start(bf16[832,128]{1,0:T(8,128)(2,1)S(1)} %collective-permute-done.7.refs_0_.refs_1_), channel_id=1, source_target_pairs={{0,1},{1,0},{2,3},{3,2},{4,5},{5,4},{6,7},{7,6},{8,9},{9,8},{10,11... | collective-permute-start | bytes 638984 | tf_op jit(solution)/shard_map/ppermute | solution.py:514
  38.0 9.0 %collective-permute-start.14 = (bf16[128,384]{1,0:T(8,128)(2,1)S(1)}, bf16[128,384]{1,0:T(8,128)(2,1)S(1)}, u32[]{:S(2)}, u32[]{:S(2)}) collective-permute-start(bf16[128,384]{1,0:T(8,128)(2,1)S(1)} %get-tuple-element.48), channel_id=1, source_target_pairs={{0,16},{8,24},{16,0},{24,8},{1,17},{9,25},{17,1},{25,9},{2,18},{10... | collective-permute-start | bytes 294920 | tf_op jit(solution)/shard_map/ppermute | solution.py:514
  40.8 6.2 %collective-permute-start.15 = (bf16[128,384]{1,0:T(8,128)(2,1)S(1)}, bf16[128,384]{1,0:T(8,128)(2,1)S(1)}, u32[]{:S(2)}, u32[]{:S(2)}) collective-permute-start(bf16[128,384]{1,0:T(8,128)(2,1)S(1)} %get-tuple-element.49), channel_id=1, source_target_pairs={{0,8},{8,0},{16,24},{24,16},{1,9},{9,1},{17,25},{25,17},{2,10},{10... | collective-permute-start | bytes 294920 | tf_op jit(solution)/shard_map/ppermute | solution.py:514
  42.4 6.9 %collective-permute-start.16 = (bf16[128,384]{1,0:T(8,128)(2,1)S(1)}, bf16[128,384]{1,0:T(8,128)(2,1)S(1)}, u32[]{:S(2)}, u32[]{:S(2)}) collective-permute-start(bf16[128,384]{1,0:T(8,128)(2,1)S(1)} %get-tuple-element.50), channel_id=1, source_target_pairs={{0,24},{8,16},{16,8},{24,0},{1,25},{9,17},{17,9},{25,1},{2,26},{10... | collective-permute-start | bytes 294920 | tf_op jit(solution)/shard_map/ppermute | solution.py:514

commit v7 on v6

--- a/solution.py
+++ b/solution.py
@@ -386,21 +386,23 @@
     key = projected[:, HEAD_DIM : 2 * HEAD_DIM]
     value = projected[:, 2 * HEAD_DIM :]
     grad = jnp.concatenate([grad_ref[place] for place in range(devices)], axis=0)
-    scores = dot(key, query, NT) * scaling
+    query = query * jnp.bfloat16(scaling)
+    scores = dot(key, query, NT)
     weights = jnp.exp(scores - jnp.max(scores, axis=0, keepdims=True))
     row_total = jnp.sum(weights, axis=0, keepdims=True)
-    attended = (dot(value, weights.astype(jnp.bfloat16), TN) / row_total).astype(jnp.bfloat16)
-    attended = attended.astype(jnp.float32)
-    grad_dot = jnp.sum(grad.astype(jnp.float32).T * attended, axis=0, keepdims=True)
-    probability = weights * (1.0 / row_total)
+    inverse = 1.0 / row_total
+    attended = (dot(value, weights.astype(jnp.bfloat16), TN) * inverse).astype(jnp.bfloat16)
+    products = grad.T.astype(jnp.float32) * attended.astype(jnp.float32)
+    grad_dot = jnp.sum(products, axis=0, keepdims=True)
+    probability = weights * inverse
     score_grad = (probability * (dot(value, grad, NT) - grad_dot)).astype(jnp.bfloat16)
     value_grad = dot(probability.astype(jnp.bfloat16), grad)
-    key_grad = dot(score_grad, query) * scaling
-    query_grad = (dot(key, score_grad, TN) * scaling).T
-    attended = attended.T.astype(jnp.bfloat16)
+    key_grad = dot(score_grad, query)
+    query_grad = (dot(key, score_grad, TN) * scaling).astype(jnp.bfloat16).T
+    attended = attended.T
     for place in range(devices):
         attended_ref[place] = fold_half(attended[place * local_rows : (place + 1) * local_rows])
-    proj_grad = jnp.concatenate([query_grad, key_grad], axis=1).astype(jnp.bfloat16)
+    proj_grad = jnp.concatenate([query_grad, key_grad.astype(jnp.bfloat16)], axis=1)
     value_grad = fold_half(value_grad.astype(jnp.bfloat16))
     end = rows + rows // 2
     for chip, out in enumerate(outs):
@@ -449,26 +451,39 @@
     )
 
 
-def near_kernel(placed_ref, *refs):
-    pieces, out_ref = refs[:-1], refs[-1]
-    for index, columns in enumerate(head_columns(placed_ref[...], pieces)):
-        out_ref[index] = columns.astype(jnp.bfloat16)
-
-
-def weight_kernel(flips, placed_ref, near_ref, *refs):
-    count = len(flips) - near_ref.shape[0]
-    pieces, outs, (held_ref, block_ref) = refs[:count], refs[count:-2], refs[-2:]
+def near_kernel(flips, last, placed_ref, *refs):
+    pieces, outs, (held_ref, block_ref) = refs[: len(flips)], refs[len(flips) : -2], refs[-2:]
     seq, clip = lax.axis_index("seq"), lax.axis_index("clip")
-    columns = [near_ref[index] for index in range(near_ref.shape[0])]
-    columns += head_columns(placed_ref[...], pieces)
-    for flip, each in zip(flips, columns):
-        held_ref[jnp.bitwise_xor(seq, flip)] = each.astype(jnp.bfloat16)
+    held_ref[jnp.bitwise_xor(seq, last)] = jnp.zeros(held_ref.shape[1:], held_ref.dtype)
+    for flip, columns in zip(flips, head_columns(placed_ref[...], pieces)):
+        held_ref[jnp.bitwise_xor(seq, flip)] = columns.astype(jnp.bfloat16)
     columns = in_order(held_ref)
     width = columns.shape[1] // len(outs)
     for index in range(len(outs)):
         block_ref[index] = columns[:, index * width : (index + 1) * width]
     for flip, out in enumerate(outs):
         out[...] = block_ref[jnp.bitwise_xor(clip, flip)]
+
+
+def weight_kernel(last, placed_ref, piece_ref, *refs):
+    count = len(refs) // 2
+    head = jnp.bitwise_xor(lax.axis_index("seq"), last)
+    columns = head_columns(placed_ref[...], [piece_ref])[0]
+    width = refs[0].shape[1]
+    groups = width // HEAD_DIM
+    wide = [
+        jnp.concatenate([columns[:, part * HEAD_DIM : (part + 1) * HEAD_DIM]] * groups, axis=1)
+        for part in range(3)
+    ]
+    lane = lax.broadcasted_iota(jnp.int32, (1, width), 1)
+    for flip in range(count):
+        place = jnp.bitwise_xor(lax.axis_index("clip"), flip) * width + lane
+        others = refs[flip][...].astype(jnp.float32)
+        for part in range(3):
+            first = (part * HEADS + head) * HEAD_DIM
+            mine = (place >= first) & (place < first + HEAD_DIM)
+            others = jnp.where(mine, wide[part], others)
+        refs[count + flip][...] = others.astype(jnp.bfloat16)
 
 
 def patch_kernel(flips, segment_ref, target_ref, w_hbm, *refs):
@@ -598,24 +613,25 @@
         pieces[flip + 1] = exchange(pieces[flip], "seq", 1)
     flips = [chip ^ core for chip in range(devices - 2, -1, -2) for core in range(2)]
     pieces = [pieces[flip] for flip in flips]
-    far = [devices - 1]
-    near = [flip for flip in order if flip not in far]
-    columns = call(
-        near_kernel,
-        shape(len(near), width, 3 * HEAD_DIM),
+    last = devices - 1
+    near = [flip for flip in order if flip != last]
+    blocks = [shape(width, 3 * inner // clips)] * clips
+    weights = call(
+        functools.partial(near_kernel, near, last),
+        blocks,
         placed,
         *[pieces[flips.index(flip)] for flip in near],
-    )
-    weights = call(
-        functools.partial(weight_kernel, near + far),
-        [shape(width, 3 * inner // clips)] * clips,
-        placed,
-        columns,
-        *[pieces[flips.index(flip)] for flip in far],
         scratch=[
             pltpu.VMEM((devices, width, 3 * HEAD_DIM), jnp.bfloat16),
             pltpu.VMEM((clips, width, 3 * inner // clips), jnp.bfloat16),
         ],
+    )
+    weights = call(
+        functools.partial(weight_kernel, last),
+        blocks,
+        placed,
+        pieces[flips.index(last)],
+        *weights,
     )
     clip_flips = sorted(range(1, clips), key=lambda flip: (flip != clips // 2, flip))
     weights = [weights[0]] + [exchange(weights[flip], "clip", flip) for flip in clip_flips]

time: 50.2 us -> 50.1 us (level)
  transfers between devices with their start and end apart: 17 -> 17, of which waited for: 10 -> 10; matrix products, arithmetic and copies ran while one was open for 0% -> 0% of each run, Pallas kernels for 10% -> 11%
where the time goes in v7:
time: 50.1 us; the launch traced here: 49.9 us
  waiting for transfers between devices  20.8 us (42%)
  starting transfers between devices  15.2 us (30%)
  Pallas kernels  12.3 us (25%)
  local copies, waits for them, and re-layouts  0.92 us (2%)
  between operations  0.74 us (1%)
    ppermute x17, waiting for transfers between devices, exchange(): lax.ppermute(rows, axis, [(index, index ^ flip) for index in range(count)])  20.8 us
    ppermute x17, starting transfers between devices, exchange(): lax.ppermute(rows, axis, [(index, index ^ flip) for index in range(count)])  15.2 us
    pallas_call x9, Pallas kernels, call(): pl.pallas_call(body, out_shape=outs, in_specs=[pl.BlockSpec(memory_space=...  12.3 us
  transfers between devices with their start and end apart: 17, of which 10 were waited for; matrix products, arithmetic and copies ran while one was open for 0% of the time, Pallas kernels for 11%

profile of v7, /device:TPU:0, one launch (start us, length us, event | category | flops | bytes accessed | tf_op | source)
XLA Modules:
  0.0 49.9 jit_solution(13539991938709429300)
XLA Ops:
  0.6 3.9 %shard_map.85 = (bf16[528,128]{1,0:T(8,128)(2,1)}, bf16[528,128]{1,0:T(8,128)(2,1)}, bf16[528,128]{1,0:T(8,128)(2,1)}, bf16[528,128]{1,0:T(8,128)(2,1)}, bf16[52...) custom-call(s32[1,196]{1,0:T(1,128)} %refs_0_.1, ...), custom_call_target="tpu_custom_call" | custom-call | tf_op jit(solution)/shard_map/pallas_call | solution.py:244
  4.6 4.0 %collective-permute-start = (bf16[528,128]{1,0:T(8,128)(2,1)}, bf16[528,128]{1,0:T(8,128)(2,1)S(1)}, u32[]{:S(2)}, u32[]{:S(2)}) collective-permute-start(bf16[528,128]{1,0:T(8,128)(2,1)} %get-tuple-element.34), channel_id=1, source_target_pairs={{0,6},{1,7},{2,4},{3,5},{4,2},{5,3},{6,0},{7,1},{8,14},{9,15},{10,... | collective-permute-start | bytes 405512 | tf_op jit(solution)/shard_map/ppermute | solution.py:529
  8.5 1.1 %collective-permute-start.2 = (bf16[528,128]{1,0:T(8,128)(2,1)}, bf16[528,128]{1,0:T(8,128)(2,1)S(1)}, u32[]{:S(2)}, u32[]{:S(2)}) collective-permute-start(bf16[528,128]{1,0:T(8,128)(2,1)} %get-tuple-element.36), channel_id=1, source_target_pairs={{0,4},{1,5},{2,6},{3,7},{4,0},{5,1},{6,2},{7,3},{8,12},{9,13},{10,... | collective-permute-start | bytes 405512 | tf_op jit(solution)/shard_map/ppermute | solution.py:529
  9.7 1.5 %collective-permute-start.3 = (bf16[528,128]{1,0:T(8,128)(2,1)}, bf16[528,128]{1,0:T(8,128)(2,1)S(1)}, u32[]{:S(2)}, u32[]{:S(2)}) collective-permute-start(bf16[528,128]{1,0:T(8,128)(2,1)} %get-tuple-element.39), channel_id=1, source_target_pairs={{0,2},{1,3},{2,0},{3,1},{4,6},{5,7},{6,4},{7,5},{8,10},{9,11},{10,... | collective-permute-start | bytes 405512 | tf_op jit(solution)/shard_map/ppermute | solution.py:529
  11.2 0.5 %collective-permute-start.4 = (bf16[528,128]{1,0:T(8,128)(2,1)}, bf16[528,128]{1,0:T(8,128)(2,1)S(1)}, u32[]{:S(2)}, u32[]{:S(2)}) collective-permute-start(bf16[528,128]{1,0:T(8,128)(2,1)} %get-tuple-element.40), channel_id=1, source_target_pairs={{0,5},{1,4},{2,7},{3,6},{4,1},{5,0},{6,3},{7,2},{8,13},{9,12},{10,... | collective-permute-start | bytes 405512 | tf_op jit(solution)/shard_map/ppermute | solution.py:529
  11.7 1.2 %collective-permute-done.refs_1_ = bf16[528,128]{1,0:T(8,128)(2,1)S(1)} collective-permute-done((bf16[528,128]{1,0:T(8,128)(2,1)}, bf16[528,128]{1,0:T(8,128)(2,1)S(1)}, u32[]{:S(2)}, u32[]{:S(2)}) %collective-permute-start) | collective-permute-done | bytes 135200 | tf_op jit(solution)/shard_map/ppermute | solution.py:529
  12.9 0.0 collective-permute-start.5
  12.9 2.9 %collective-permute-done.1.refs_2_ = bf16[528,128]{1,0:T(8,128)(2,1)S(1)} collective-permute-done((bf16[528,128]{1,0:T(8,128)(2,1)}, bf16[528,128]{1,0:T(8,128)(2,1)S(1)}, u32[]{:S(2)}, u32[]{:S(2)}) %collective-permute-start.1) | collective-permute-done | bytes 135200 | tf_op jit(solution)/shard_map/ppermute | solution.py:529
  15.8 2.4 %collective-permute-done.2.refs_3_ = bf16[528,128]{1,0:T(8,128)(2,1)S(1)} collective-permute-done((bf16[528,128]{1,0:T(8,128)(2,1)}, bf16[528,128]{1,0:T(8,128)(2,1)S(1)}, u32[]{:S(2)}, u32[]{:S(2)}) %collective-permute-start.2) | collective-permute-done | bytes 135200 | tf_op jit(solution)/shard_map/ppermute | solution.py:529
  18.2 0.9 %copy-done.1 = bf16[528,128]{1,0:T(8,128)(2,1)S(1)} copy-done((bf16[528,128]{1,0:T(8,128)(2,1)S(1)}, bf16[528,128]{1,0:T(8,128)(2,1)}, u32[]{:S(2)}) %copy-start.1) | copy-done | bytes 135192
  19.1 0.4 shard_map.86
  19.5 0.0 copy-start
  19.5 0.0 copy-start.2
  19.6 1.4 %collective-permute-done.4.refs_1_.refs_5_ = bf16[528,128]{1,0:T(8,128)(2,1)S(1)} collective-permute-done((bf16[528,128]{1,0:T(8,128)(2,1)}, bf16[528,128]{1,0:T(8,128)(2,1)S(1)}, u32[]{:S(2)}, u32[]{:S(2)}) %collective-permute-start.4) | collective-permute-done | bytes 135200 | tf_op jit(solution)/shard_map/ppermute | solution.py:529
  21.0 1.8 %shard_map.87 = (bf16[832,128]{1,0:T(8,128)(2,1)S(1)}, bf16[832,128]{1,0:T(8,128)(2,1)S(1)}, bf16[832,128]{1,0:T(8,128)(2,1)S(1)}, bf16[832,128]{1,0:T(8,128)(2,1)S(1)}, s32[4,1,192]{2,1,0:T(1,128)S(1)}) custom-call(bf16[512,192]{1,0:T(8,128)(2,1)S(1)} %get-tuple-element.37.early_ref, bf16[4,64,64]{2,1,0:T(8,128)(2,1)S(1)} %get-tuple-element.38.early_grad_ref, ...), custom_call_target="tpu_custom_call" | custom-call | tf_op jit(solution)/shard_map/pallas_call | solution.py:244
  22.8 1.8 %collective-permute-start.9 = (bf16[832,128]{1,0:T(8,128)(2,1)S(1)}, bf16[832,128]{1,0:T(8,128)(2,1)S(1)}, u32[]{:S(2)}, u32[]{:S(2)}) collective-permute-start(bf16[832,128]{1,0:T(8,128)(2,1)S(1)} %get-tuple-element.44), channel_id=1, source_target_pairs={{0,4},{1,5},{2,6},{3,7},{4,0},{5,1},{6,2},{7,3},{8,12},{9,13},{10,... | collective-permute-start | bytes 638984 | tf_op jit(solution)/shard_map/ppermute | solution.py:529
  24.6 1.5 %collective-permute-start.11 = (bf16[832,128]{1,0:T(8,128)(2,1)S(1)}, bf16[832,128]{1,0:T(8,128)(2,1)S(1)}, u32[]{:S(2)}, u32[]{:S(2)}) collective-permute-start(bf16[832,128]{1,0:T(8,128)(2,1)S(1)} %get-tuple-element.47), channel_id=1, source_target_pairs={{0,2},{1,3},{2,0},{3,1},{4,6},{5,7},{6,4},{7,5},{8,10},{9,11},{10,... | collective-permute-start | bytes 638984 | tf_op jit(solution)/shard_map/ppermute | solution.py:529
  26.1 0.2 collective-permute-start.7
  26.4 0.7 %shard_map.88.refs_1_.placed_ref = bf16[128,512]{1,0:T(8,128)(2,1)S(1)} custom-call(s32[4,1,192]{2,1,0:T(1,128)S(1)} %get-tuple-element.45.early_ref, s32[4,1,192]{2,1,0:T(1,128)S(1)} %get-tuple-element.46.late_ref, bf16[528,128]{1,0:T(8,128)(2,1)S(1)} %copy-done.1, bf16[528,128]{1,0:T(8,128)(2,1)S(1)} %collective-permute-done.refs_1_, ...), custom_call_target="tpu_custom_call" | custom-call | tf_op jit(solution)/shard_map/pallas_call | solution.py:244
  27.1 3.1 %collective-permute-done.9.refs_0_ = bf16[832,128]{1,0:T(8,128)(2,1)S(1)} collective-permute-done((bf16[832,128]{1,0:T(8,128)(2,1)S(1)}, bf16[832,128]{1,0:T(8,128)(2,1)S(1)}, u32[]{:S(2)}, u32[]{:S(2)}) %collective-permute-start.9) | collective-permute-done | bytes 213024 | tf_op jit(solution)/shard_map/ppermute | solution.py:529
  30.2 2.6 %collective-permute-done.11.refs_4_.refs_3_ = bf16[832,128]{1,0:T(8,128)(2,1)S(1)} collective-permute-done((bf16[832,128]{1,0:T(8,128)(2,1)S(1)}, bf16[832,128]{1,0:T(8,128)(2,1)S(1)}, u32[]{:S(2)}, u32[]{:S(2)}) %collective-permute-start.11) | collective-permute-done | bytes 213024 | tf_op jit(solution)/shard_map/ppermute | solution.py:529
  32.8 3.2 %collective-permute-done.7.refs_0_.refs_1_ = bf16[832,128]{1,0:T(8,128)(2,1)S(1)} collective-permute-done((bf16[832,128]{1,0:T(8,128)(2,1)S(1)}, bf16[832,128]{1,0:T(8,128)(2,1)S(1)}, u32[]{:S(2)}, u32[]{:S(2)}) %collective-permute-start.7) | collective-permute-done | bytes 213024 | tf_op jit(solution)/shard_map/ppermute | solution.py:529
  36.0 0.8 %shard_map.91 = (bf16[128,384]{1,0:T(8,128)(2,1)S(1)}, bf16[128,384]{1,0:T(8,128)(2,1)S(1)}, bf16[128,384]{1,0:T(8,128)(2,1)S(1)}, bf16[128,384]{1,0:T(8,128)(2,1)S(1)}) custom-call(bf16[128,512]{1,0:T(8,128)(2,1)S(1)} %shard_map.88.refs_1_.placed_ref, bf16[832,128]{1,0:T(8,128)(2,1)S(1)} %get-tuple-element.48.refs_6_.refs_0_, ...), custom_call_target="tpu_custom_call" | custom-call | tf_op jit(solution)/shard_map/pallas_call | solution.py:244
  36.8 0.7 %collective-permute-done.8.refs_1_.piece_ref = bf16[832,128]{1,0:T(8,128)(2,1)S(1)} collective-permute-done((bf16[832,128]{1,0:T(8,128)(2,1)S(1)}, bf16[832,128]{1,0:T(8,128)(2,1)S(1)}, u32[]{:S(2)}, u32[]{:S(2)}) %collective-permute-start.8) | collective-permute-done | bytes 213024 | tf_op jit(solution)/shard_map/ppermute | solution.py:529
  37.5 0.5 shard_map.92
  37.9 2.8 %collective-permute-start.14 = (bf16[128,384]{1,0:T(8,128)(2,1)S(1)}, bf16[128,384]{1,0:T(8,128)(2,1)S(1)}, u32[]{:S(2)}, u32[]{:S(2)}) collective-permute-start(bf16[128,384]{1,0:T(8,128)(2,1)S(1)} %get-tuple-element.56), channel_id=1, source_target_pairs={{0,16},{8,24},{16,0},{24,8},{1,17},{9,25},{17,1},{25,9},{2,18},{10... | collective-permute-start | bytes 294920 | tf_op jit(solution)/shard_map/ppermute | solution.py:529
  40.7 1.6 %collective-permute-start.15 = (bf16[128,384]{1,0:T(8,128)(2,1)S(1)}, bf16[128,384]{1,0:T(8,128)(2,1)S(1)}, u32[]{:S(2)}, u32[]{:S(2)}) collective-permute-start(bf16[128,384]{1,0:T(8,128)(2,1)S(1)} %get-tuple-element.57), channel_id=1, source_target_pairs={{0,8},{8,0},{16,24},{24,16},{1,9},{9,1},{17,25},{25,17},{2,10},{10... | collective-permute-start | bytes 294920 | tf_op jit(solution)/shard_map/ppermute | solution.py:529
  42.3 0.1 collective-permute-start.16
  42.4 3.4 %shard_map.90 = (bf16[196,1024]{1,0:T(8,128)(2,1)}, bf16[64,512]{1,0:T(8,128)(2,1)}) custom-call(s32[1,196]{1,0:T(1,128)S(1)} %copy-done.3, s32[1,192]{1,0:T(1,128)S(1)} %copy-done.2, bf16[1024,1536]{1,0:T(8,128)(2,1)S(1)} %copy-done, bf16[832,128]{1,0:T(8,128)(2,1)S(1)} %collective-permute-done.7.refs_0_.refs_1_, ...), custom_call_target="tpu_custom_call" | custom-call | tf_op jit(solution)/shard_map/pallas_call | solution.py:244
  45.8 1.1 %collective-permute-done.14.refs_1_ = bf16[128,384]{1,0:T(8,128)(2,1)S(1)} collective-permute-done((bf16[128,384]{1,0:T(8,128)(2,1)S(1)}, bf16[128,384]{1,0:T(8,128)(2,1)S(1)}, u32[]{:S(2)}, u32[]{:S(2)}) %collective-permute-start.14) | collective-permute-done | bytes 98336 | tf_op jit(solution)/shard_map/ppermute | solution.py:529
  47.0 2.3 %collective-permute-done.16.refs_3_ = bf16[128,384]{1,0:T(8,128)(2,1)S(1)} collective-permute-done((bf16[128,384]{1,0:T(8,128)(2,1)S(1)}, bf16[128,384]{1,0:T(8,128)(2,1)S(1)}, u32[]{:S(2)}, u32[]{:S(2)}) %collective-permute-start.16) | collective-permute-done | bytes 98336 | tf_op jit(solution)/shard_map/ppermute | solution.py:529
  49.2 0.7 %shard_map.93 = f32[128,384]{1,0:T(8,128)} custom-call(bf16[128,384]{1,0:T(8,128)(2,1)S(1)} %get-tuple-element.55.refs_0_, bf16[128,384]{1,0:T(8,128)(2,1)S(1)} %collective-permute-done.14.refs_1_, bf16[128,384]{1,0:T(8,128)(2,1)S(1)} %collective-permute-done.15.refs_2_, bf16[128,384]{1,0:T(8,128)(2,1)S(1)} %collective-permute-done.16.refs_3_), custom_call_target="tpu_custom_call" | custom-call | tf_op jit(solution)/shard_map/pallas_call | solution.py:244
  (19 shorter events, 0.0 us)
Async XLA Ops:
  4.6 8.3 %collective-permute-start = (bf16[528,128]{1,0:T(8,128)(2,1)}, bf16[528,128]{1,0:T(8,128)(2,1)S(1)}, u32[]{:S(2)}, u32[]{:S(2)}) collective-permute-start(bf16[528,128]{1,0:T(8,128)(2,1)} %get-tuple-element.34), channel_id=1, source_target_pairs={{0,6},{1,7},{2,4},{3,5},{4,2},{5,3},{6,0},{7,1},{8,14},{9,15},{10,... | collective-permute-start | bytes 405512 | tf_op jit(solution)/shard_map/ppermute | solution.py:529
  8.5 7.2 %collective-permute-start.1 = (bf16[528,128]{1,0:T(8,128)(2,1)}, bf16[528,128]{1,0:T(8,128)(2,1)S(1)}, u32[]{:S(2)}, u32[]{:S(2)}) collective-permute-start(bf16[528,128]{1,0:T(8,128)(2,1)} %get-tuple-element.35), channel_id=1, source_target_pairs={{0,7},{1,6},{2,5},{3,4},{4,3},{5,2},{6,1},{7,0},{8,15},{9,14},{10,... | collective-permute-start | bytes 405512 | tf_op jit(solution)/shard_map/ppermute | solution.py:529
  8.5 9.6 %collective-permute-start.2 = (bf16[528,128]{1,0:T(8,128)(2,1)}, bf16[528,128]{1,0:T(8,128)(2,1)S(1)}, u32[]{:S(2)}, u32[]{:S(2)}) collective-permute-start(bf16[528,128]{1,0:T(8,128)(2,1)} %get-tuple-element.36), channel_id=1, source_target_pairs={{0,4},{1,5},{2,6},{3,7},{4,0},{5,1},{6,2},{7,3},{8,12},{9,13},{10,... | collective-permute-start | bytes 405512 | tf_op jit(solution)/shard_map/ppermute | solution.py:529
  9.7 9.9 %collective-permute-start.3 = (bf16[528,128]{1,0:T(8,128)(2,1)}, bf16[528,128]{1,0:T(8,128)(2,1)S(1)}, u32[]{:S(2)}, u32[]{:S(2)}) collective-permute-start(bf16[528,128]{1,0:T(8,128)(2,1)} %get-tuple-element.39), channel_id=1, source_target_pairs={{0,2},{1,3},{2,0},{3,1},{4,6},{5,7},{6,4},{7,5},{8,10},{9,11},{10,... | collective-permute-start | bytes 405512 | tf_op jit(solution)/shard_map/ppermute | solution.py:529
  11.2 9.8 %collective-permute-start.4 = (bf16[528,128]{1,0:T(8,128)(2,1)}, bf16[528,128]{1,0:T(8,128)(2,1)S(1)}, u32[]{:S(2)}, u32[]{:S(2)}) collective-permute-start(bf16[528,128]{1,0:T(8,128)(2,1)} %get-tuple-element.40), channel_id=1, source_target_pairs={{0,5},{1,4},{2,7},{3,6},{4,1},{5,0},{6,3},{7,2},{8,13},{9,12},{10,... | collective-permute-start | bytes 405512 | tf_op jit(solution)/shard_map/ppermute | solution.py:529
  12.9 8.1 %collective-permute-start.5 = (bf16[528,128]{1,0:T(8,128)(2,1)}, bf16[528,128]{1,0:T(8,128)(2,1)S(1)}, u32[]{:S(2)}, u32[]{:S(2)}) collective-permute-start(bf16[528,128]{1,0:T(8,128)(2,1)} %get-tuple-element.41), channel_id=1, source_target_pairs={{0,3},{1,2},{2,1},{3,0},{4,7},{5,6},{6,5},{7,4},{8,11},{9,10},{10,... | collective-permute-start | bytes 405512 | tf_op jit(solution)/shard_map/ppermute | solution.py:529
  15.8 5.2 %collective-permute-start.6 = (bf16[528,128]{1,0:T(8,128)(2,1)}, bf16[528,128]{1,0:T(8,128)(2,1)S(1)}, u32[]{:S(2)}, u32[]{:S(2)}) collective-permute-start(bf16[528,128]{1,0:T(8,128)(2,1)} %get-tuple-element.42), channel_id=1, source_target_pairs={{0,1},{1,0},{2,3},{3,2},{4,5},{5,4},{6,7},{7,6},{8,9},{9,8},{10,11... | collective-permute-start | bytes 405512 | tf_op jit(solution)/shard_map/ppermute | solution.py:529
  18.2 0.9 %copy-start.1 = (bf16[528,128]{1,0:T(8,128)(2,1)S(1)}, bf16[528,128]{1,0:T(8,128)(2,1)}, u32[]{:S(2)}) copy-start(bf16[528,128]{1,0:T(8,128)(2,1)} %get-tuple-element.33.refs_0_) | copy-start | bytes 405508
  19.5 22.9 %copy-start = (bf16[1024,1536]{1,0:T(8,128)(2,1)S(1)}, bf16[1024,1536]{1,0:T(8,128)(2,1)}, u32[]{:S(2)}) copy-start(bf16[1024,1536]{1,0:T(8,128)(2,1)} %w_hbm.1) | copy-start | bytes 9437188
  19.5 22.8 %copy-start.2 = (s32[1,192]{1,0:T(1,128)S(1)}, s32[1,192]{1,0:T(1,128)}, u32[]{:S(2)}) copy-start(s32[1,192]{1,0:T(1,128)} %get-tuple-element.32.target_ref) | copy-start | bytes 2308
  19.6 22.8 %copy-start.3 = (s32[1,196]{1,0:T(1,128)S(1)}, s32[1,196]{1,0:T(1,128)}, u32[]{:S(2)}) copy-start(s32[1,196]{1,0:T(1,128)} %get-tuple-element.31.segment_ref) | copy-start | bytes 2356
  22.8 7.4 %collective-permute-start.9 = (bf16[832,128]{1,0:T(8,128)(2,1)S(1)}, bf16[832,128]{1,0:T(8,128)(2,1)S(1)}, u32[]{:S(2)}, u32[]{:S(2)}) collective-permute-start(bf16[832,128]{1,0:T(8,128)(2,1)S(1)} %get-tuple-element.44), channel_id=1, source_target_pairs={{0,4},{1,5},{2,6},{3,7},{4,0},{5,1},{6,2},{7,3},{8,12},{9,13},{10,... | collective-permute-start | bytes 638984 | tf_op jit(solution)/shard_map/ppermute | solution.py:529
  24.6 8.1 %collective-permute-start.11 = (bf16[832,128]{1,0:T(8,128)(2,1)S(1)}, bf16[832,128]{1,0:T(8,128)(2,1)S(1)}, u32[]{:S(2)}, u32[]{:S(2)}) collective-permute-start(bf16[832,128]{1,0:T(8,128)(2,1)S(1)} %get-tuple-element.47), channel_id=1, source_target_pairs={{0,2},{1,3},{2,0},{3,1},{4,6},{5,7},{6,4},{7,5},{8,10},{9,11},{10,... | collective-permute-start | bytes 638984 | tf_op jit(solution)/shard_map/ppermute | solution.py:529
  26.1 9.9 %collective-permute-start.7 = (bf16[832,128]{1,0:T(8,128)(2,1)S(1)}, bf16[832,128]{1,0:T(8,128)(2,1)S(1)}, u32[]{:S(2)}, u32[]{:S(2)}) collective-permute-start(bf16[832,128]{1,0:T(8,128)(2,1)S(1)} %get-tuple-element.43), channel_id=1, source_target_pairs={{0,6},{1,7},{2,4},{3,5},{4,2},{5,3},{6,0},{7,1},{8,14},{9,15},{10,... | collective-permute-start | bytes 638984 | tf_op jit(solution)/shard_map/ppermute | solution.py:529
  26.4 9.6 %collective-permute-start.13 = (bf16[832,128]{1,0:T(8,128)(2,1)S(1)}, bf16[832,128]{1,0:T(8,128)(2,1)S(1)}, u32[]{:S(2)}, u32[]{:S(2)}) collective-permute-start(bf16[832,128]{1,0:T(8,128)(2,1)S(1)} %get-tuple-element.48.refs_6_.refs_0_), channel_id=1, source_target_pairs={{0,1},{1,0},{2,3},{3,2},{4,5},{5,4},{6,7},{7,6},{8,9},{9,8},{10,11... | collective-permute-start | bytes 638984 | tf_op jit(solution)/shard_map/ppermute | solution.py:529
  30.2 5.8 %collective-permute-start.10 = (bf16[832,128]{1,0:T(8,128)(2,1)S(1)}, bf16[832,128]{1,0:T(8,128)(2,1)S(1)}, u32[]{:S(2)}, u32[]{:S(2)}) collective-permute-start(bf16[832,128]{1,0:T(8,128)(2,1)S(1)} %shard_map.89.refs_2_), channel_id=1, source_target_pairs={{0,1},{1,0},{2,3},{3,2},{4,5},{5,4},{6,7},{7,6},{8,9},{9,8},{10,11... | collective-permute-start | bytes 638984 | tf_op jit(solution)/shard_map/ppermute | solution.py:529
  32.8 3.2 %collective-permute-start.12 = (bf16[832,128]{1,0:T(8,128)(2,1)S(1)}, bf16[832,128]{1,0:T(8,128)(2,1)S(1)}, u32[]{:S(2)}, u32[]{:S(2)}) collective-permute-start(bf16[832,128]{1,0:T(8,128)(2,1)S(1)} %collective-permute-done.11.refs_4_.refs_3_), channel_id=1, source_target_pairs={{0,1},{1,0},{2,3},{3,2},{4,5},{5,4},{6,7},{7,6},{8,9},{9,8},{10,11... | collective-permute-start | bytes 638984 | tf_op jit(solution)/shard_map/ppermute | solution.py:529
  36.0 1.5 %collective-permute-start.8 = (bf16[832,128]{1,0:T(8,128)(2,1)S(1)}, bf16[832,128]{1,0:T(8,128)(2,1)S(1)}, u32[]{:S(2)}, u32[]{:S(2)}) collective-permute-start(bf16[832,128]{1,0:T(8,128)(2,1)S(1)} %collective-permute-done.7.refs_0_.refs_1_), channel_id=1, source_target_pairs={{0,1},{1,0},{2,3},{3,2},{4,5},{5,4},{6,7},{7,6},{8,9},{9,8},{10,11... | collective-permute-start | bytes 638984 | tf_op jit(solution)/shard_map/ppermute | solution.py:529
  37.9 9.0 %collective-permute-start.14 = (bf16[128,384]{1,0:T(8,128)(2,1)S(1)}, bf16[128,384]{1,0:T(8,128)(2,1)S(1)}, u32[]{:S(2)}, u32[]{:S(2)}) collective-permute-start(bf16[128,384]{1,0:T(8,128)(2,1)S(1)} %get-tuple-element.56), channel_id=1, source_target_pairs={{0,16},{8,24},{16,0},{24,8},{1,17},{9,25},{17,1},{25,9},{2,18},{10... | collective-permute-start | bytes 294920 | tf_op jit(solution)/shard_map/ppermute | solution.py:529
  40.7 6.2 %collective-permute-start.15 = (bf16[128,384]{1,0:T(8,128)(2,1)S(1)}, bf16[128,384]{1,0:T(8,128)(2,1)S(1)}, u32[]{:S(2)}, u32[]{:S(2)}) collective-permute-start(bf16[128,384]{1,0:T(8,128)(2,1)S(1)} %get-tuple-element.57), channel_id=1, source_target_pairs={{0,8},{8,0},{16,24},{24,16},{1,9},{9,1},{17,25},{25,17},{2,10},{10... | collective-permute-start | bytes 294920 | tf_op jit(solution)/shard_map/ppermute | solution.py:529
  42.3 6.9 %collective-permute-start.16 = (bf16[128,384]{1,0:T(8,128)(2,1)S(1)}, bf16[128,384]{1,0:T(8,128)(2,1)S(1)}, u32[]{:S(2)}, u32[]{:S(2)}) collective-permute-start(bf16[128,384]{1,0:T(8,128)(2,1)S(1)} %get-tuple-element.58), channel_id=1, source_target_pairs={{0,24},{8,16},{16,8},{24,0},{1,25},{9,17},{17,9},{25,1},{2,26},{10... | collective-permute-start | bytes 294920 | tf_op jit(solution)/shard_map/ppermute | solution.py:529

commit v8 on v7

--- a/solution.py
+++ b/solution.py
@@ -570,7 +570,7 @@
     for flip in order[1:]:
         came[flip] = exchange(sends[flip], "seq", flip)
     came = [came[flip] for flip in order]
-    early = devices // 2
+    early = devices // 2 + 1
     placed, early_targets, early_grads = call(
         functools.partial(early_kernel, token_cap),
         [

time: 50.1 us -> 50.1 us (level)
  transfers between devices with their start and end apart: 17 -> 17, of which waited for: 10 -> 11; matrix products, arithmetic and copies ran while one was open for 0% -> 0% of each run, Pallas kernels for 11% -> 11%
where the time goes in v8:
time: 50.1 us; the launch traced here: 49.9 us
  waiting for transfers between devices  20.8 us (42%)
  starting transfers between devices  15.2 us (30%)
  Pallas kernels  12.3 us (25%)
  local copies, waits for them, and re-layouts  0.92 us (2%)
  between operations  0.73 us (1%)
    ppermute x17, waiting for transfers between devices, exchange(): lax.ppermute(rows, axis, [(index, index ^ flip) for index in range(count)])  20.8 us
    ppermute x17, starting transfers between devices, exchange(): lax.ppermute(rows, axis, [(index, index ^ flip) for index in range(count)])  15.2 us
    pallas_call x9, Pallas kernels, call(): pl.pallas_call(body, out_shape=outs, in_specs=[pl.BlockSpec(memory_space=...  12.3 us
  transfers between devices with their start and end apart: 17, of which 11 were waited for; matrix products, arithmetic and copies ran while one was open for 0% of the time, Pallas kernels for 11%

profile of v8, /device:TPU:0, one launch (start us, length us, event | category | flops | bytes accessed | tf_op | source)
XLA Modules:
  0.0 49.9 jit_solution(14832256528580510684)
XLA Ops:
  0.6 3.9 %shard_map.85 = (bf16[528,128]{1,0:T(8,128)(2,1)}, bf16[528,128]{1,0:T(8,128)(2,1)}, bf16[528,128]{1,0:T(8,128)(2,1)}, bf16[528,128]{1,0:T(8,128)(2,1)}, bf16[52...) custom-call(s32[1,196]{1,0:T(1,128)} %refs_0_.1, ...), custom_call_target="tpu_custom_call" | custom-call | tf_op jit(solution)/shard_map/pallas_call | solution.py:244
  4.6 4.0 %collective-permute-start = (bf16[528,128]{1,0:T(8,128)(2,1)}, bf16[528,128]{1,0:T(8,128)(2,1)S(1)}, u32[]{:S(2)}, u32[]{:S(2)}) collective-permute-start(bf16[528,128]{1,0:T(8,128)(2,1)} %get-tuple-element.34), channel_id=1, source_target_pairs={{0,6},{1,7},{2,4},{3,5},{4,2},{5,3},{6,0},{7,1},{8,14},{9,15},{10,... | collective-permute-start | bytes 405512 | tf_op jit(solution)/shard_map/ppermute | solution.py:529
  8.5 1.1 %collective-permute-start.2 = (bf16[528,128]{1,0:T(8,128)(2,1)}, bf16[528,128]{1,0:T(8,128)(2,1)S(1)}, u32[]{:S(2)}, u32[]{:S(2)}) collective-permute-start(bf16[528,128]{1,0:T(8,128)(2,1)} %get-tuple-element.36), channel_id=1, source_target_pairs={{0,4},{1,5},{2,6},{3,7},{4,0},{5,1},{6,2},{7,3},{8,12},{9,13},{10,... | collective-permute-start | bytes 405512 | tf_op jit(solution)/shard_map/ppermute | solution.py:529
  9.7 1.5 %collective-permute-start.3 = (bf16[528,128]{1,0:T(8,128)(2,1)}, bf16[528,128]{1,0:T(8,128)(2,1)S(1)}, u32[]{:S(2)}, u32[]{:S(2)}) collective-permute-start(bf16[528,128]{1,0:T(8,128)(2,1)} %get-tuple-element.37), channel_id=1, source_target_pairs={{0,2},{1,3},{2,0},{3,1},{4,6},{5,7},{6,4},{7,5},{8,10},{9,11},{10,... | collective-permute-start | bytes 405512 | tf_op jit(solution)/shard_map/ppermute | solution.py:529
  11.2 0.5 %collective-permute-start.4 = (bf16[528,128]{1,0:T(8,128)(2,1)}, bf16[528,128]{1,0:T(8,128)(2,1)S(1)}, u32[]{:S(2)}, u32[]{:S(2)}) collective-permute-start(bf16[528,128]{1,0:T(8,128)(2,1)} %get-tuple-element.40), channel_id=1, source_target_pairs={{0,5},{1,4},{2,7},{3,6},{4,1},{5,0},{6,3},{7,2},{8,13},{9,12},{10,... | collective-permute-start | bytes 405512 | tf_op jit(solution)/shard_map/ppermute | solution.py:529
  11.7 1.2 %collective-permute-done.refs_1_ = bf16[528,128]{1,0:T(8,128)(2,1)S(1)} collective-permute-done((bf16[528,128]{1,0:T(8,128)(2,1)}, bf16[528,128]{1,0:T(8,128)(2,1)S(1)}, u32[]{:S(2)}, u32[]{:S(2)}) %collective-permute-start) | collective-permute-done | bytes 135200 | tf_op jit(solution)/shard_map/ppermute | solution.py:529
  12.9 2.9 %collective-permute-done.1.refs_2_ = bf16[528,128]{1,0:T(8,128)(2,1)S(1)} collective-permute-done((bf16[528,128]{1,0:T(8,128)(2,1)}, bf16[528,128]{1,0:T(8,128)(2,1)S(1)}, u32[]{:S(2)}, u32[]{:S(2)}) %collective-permute-start.1) | collective-permute-done | bytes 135200 | tf_op jit(solution)/shard_map/ppermute | solution.py:529
  15.8 2.4 %collective-permute-done.2.refs_3_ = bf16[528,128]{1,0:T(8,128)(2,1)S(1)} collective-permute-done((bf16[528,128]{1,0:T(8,128)(2,1)}, bf16[528,128]{1,0:T(8,128)(2,1)S(1)}, u32[]{:S(2)}, u32[]{:S(2)}) %collective-permute-start.2) | collective-permute-done | bytes 135200 | tf_op jit(solution)/shard_map/ppermute | solution.py:529
  18.2 1.2 %collective-permute-done.3.refs_4_ = bf16[528,128]{1,0:T(8,128)(2,1)S(1)} collective-permute-done((bf16[528,128]{1,0:T(8,128)(2,1)}, bf16[528,128]{1,0:T(8,128)(2,1)S(1)}, u32[]{:S(2)}, u32[]{:S(2)}) %collective-permute-start.3) | collective-permute-done | bytes 135200 | tf_op jit(solution)/shard_map/ppermute | solution.py:529
  19.3 0.9 %copy-done.1 = bf16[528,128]{1,0:T(8,128)(2,1)S(1)} copy-done((bf16[528,128]{1,0:T(8,128)(2,1)S(1)}, bf16[528,128]{1,0:T(8,128)(2,1)}, u32[]{:S(2)}) %copy-start.1) | copy-done | bytes 135192
  20.2 0.5 %shard_map.86 = (bf16[512,192]{1,0:T(8,128)(2,1)S(1)}, s32[5,1,192]{2,1,0:T(1,128)S(1)}, bf16[5,64,64]{2,1,0:T(8,128)(2,1)S(1)}) custom-call(bf16[528,128]{1,0:T(8,128)(2,1)S(1)} %copy-done.1, bf16[528,128]{1,0:T(8,128)(2,1)S(1)} %collective-permute-done.refs_1_, bf16[528,128]{1,0:T(8,128)(2,1)S(1)} %collective-permute-done.1.refs_2_, ...), custom_call_target="tpu_custom_call" | custom-call | flops 1000000000 | tf_op jit(solution)/shard_map/pallas_call | solution.py:244
  20.7 0.0 copy-start
  20.8 0.0 copy-start.2
  20.8 0.2 collective-permute-done.4.refs_0_.refs_5_
  21.0 1.8 %shard_map.87 = (bf16[832,128]{1,0:T(8,128)(2,1)S(1)}, bf16[832,128]{1,0:T(8,128)(2,1)S(1)}, bf16[832,128]{1,0:T(8,128)(2,1)S(1)}, bf16[832,128]{1,0:T(8,128)(2,1)S(1)}, s32[3,1,192]{2,1,0:T(1,128)S(1)}) custom-call(bf16[512,192]{1,0:T(8,128)(2,1)S(1)} %get-tuple-element.38.early_ref, bf16[5,64,64]{2,1,0:T(8,128)(2,1)S(1)} %get-tuple-element.39.early_grad_ref, ...), custom_call_target="tpu_custom_call" | custom-call | tf_op jit(solution)/shard_map/pallas_call | solution.py:244
  22.8 1.8 %collective-permute-start.9 = (bf16[832,128]{1,0:T(8,128)(2,1)S(1)}, bf16[832,128]{1,0:T(8,128)(2,1)S(1)}, u32[]{:S(2)}, u32[]{:S(2)}) collective-permute-start(bf16[832,128]{1,0:T(8,128)(2,1)S(1)} %get-tuple-element.44), channel_id=1, source_target_pairs={{0,4},{1,5},{2,6},{3,7},{4,0},{5,1},{6,2},{7,3},{8,12},{9,13},{10,... | collective-permute-start | bytes 638984 | tf_op jit(solution)/shard_map/ppermute | solution.py:529
  24.6 1.5 %collective-permute-start.11 = (bf16[832,128]{1,0:T(8,128)(2,1)S(1)}, bf16[832,128]{1,0:T(8,128)(2,1)S(1)}, u32[]{:S(2)}, u32[]{:S(2)}) collective-permute-start(bf16[832,128]{1,0:T(8,128)(2,1)S(1)} %get-tuple-element.47), channel_id=1, source_target_pairs={{0,2},{1,3},{2,0},{3,1},{4,6},{5,7},{6,4},{7,5},{8,10},{9,11},{10,... | collective-permute-start | bytes 638984 | tf_op jit(solution)/shard_map/ppermute | solution.py:529
  26.1 0.2 collective-permute-start.7
  26.4 0.7 %shard_map.88.refs_1_.placed_ref = bf16[128,512]{1,0:T(8,128)(2,1)S(1)} custom-call(s32[5,1,192]{2,1,0:T(1,128)S(1)} %get-tuple-element.45.early_ref, s32[3,1,192]{2,1,0:T(1,128)S(1)} %get-tuple-element.46.late_ref, bf16[528,128]{1,0:T(8,128)(2,1)S(1)} %copy-done.1, bf16[528,128]{1,0:T(8,128)(2,1)S(1)} %collective-permute-done.refs_1_, ...), custom_call_target="tpu_custom_call" | custom-call | tf_op jit(solution)/shard_map/pallas_call | solution.py:244
  27.1 3.1 %collective-permute-done.9.refs_0_ = bf16[832,128]{1,0:T(8,128)(2,1)S(1)} collective-permute-done((bf16[832,128]{1,0:T(8,128)(2,1)S(1)}, bf16[832,128]{1,0:T(8,128)(2,1)S(1)}, u32[]{:S(2)}, u32[]{:S(2)}) %collective-permute-start.9) | collective-permute-done | bytes 213024 | tf_op jit(solution)/shard_map/ppermute | solution.py:529
  30.2 2.6 %collective-permute-done.11.refs_4_.refs_3_ = bf16[832,128]{1,0:T(8,128)(2,1)S(1)} collective-permute-done((bf16[832,128]{1,0:T(8,128)(2,1)S(1)}, bf16[832,128]{1,0:T(8,128)(2,1)S(1)}, u32[]{:S(2)}, u32[]{:S(2)}) %collective-permute-start.11) | collective-permute-done | bytes 213024 | tf_op jit(solution)/shard_map/ppermute | solution.py:529
  32.8 3.2 %collective-permute-done.7.refs_0_.refs_1_ = bf16[832,128]{1,0:T(8,128)(2,1)S(1)} collective-permute-done((bf16[832,128]{1,0:T(8,128)(2,1)S(1)}, bf16[832,128]{1,0:T(8,128)(2,1)S(1)}, u32[]{:S(2)}, u32[]{:S(2)}) %collective-permute-start.7) | collective-permute-done | bytes 213024 | tf_op jit(solution)/shard_map/ppermute | solution.py:529
  36.0 0.8 %shard_map.91 = (bf16[128,384]{1,0:T(8,128)(2,1)S(1)}, bf16[128,384]{1,0:T(8,128)(2,1)S(1)}, bf16[128,384]{1,0:T(8,128)(2,1)S(1)}, bf16[128,384]{1,0:T(8,128)(2,1)S(1)}) custom-call(bf16[128,512]{1,0:T(8,128)(2,1)S(1)} %shard_map.88.refs_1_.placed_ref, bf16[832,128]{1,0:T(8,128)(2,1)S(1)} %get-tuple-element.48.refs_6_.refs_0_, ...), custom_call_target="tpu_custom_call" | custom-call | tf_op jit(solution)/shard_map/pallas_call | solution.py:244
  36.8 0.6 %collective-permute-done.8.refs_1_.piece_ref = bf16[832,128]{1,0:T(8,128)(2,1)S(1)} collective-permute-done((bf16[832,128]{1,0:T(8,128)(2,1)S(1)}, bf16[832,128]{1,0:T(8,128)(2,1)S(1)}, u32[]{:S(2)}, u32[]{:S(2)}) %collective-permute-start.8) | collective-permute-done | bytes 213024 | tf_op jit(solution)/shard_map/ppermute | solution.py:529
  37.5 0.5 shard_map.92
  37.9 2.8 %collective-permute-start.14 = (bf16[128,384]{1,0:T(8,128)(2,1)S(1)}, bf16[128,384]{1,0:T(8,128)(2,1)S(1)}, u32[]{:S(2)}, u32[]{:S(2)}) collective-permute-start(bf16[128,384]{1,0:T(8,128)(2,1)S(1)} %get-tuple-element.56), channel_id=1, source_target_pairs={{0,16},{8,24},{16,0},{24,8},{1,17},{9,25},{17,1},{25,9},{2,18},{10... | collective-permute-start | bytes 294920 | tf_op jit(solution)/shard_map/ppermute | solution.py:529
  40.7 1.6 %collective-permute-start.15 = (bf16[128,384]{1,0:T(8,128)(2,1)S(1)}, bf16[128,384]{1,0:T(8,128)(2,1)S(1)}, u32[]{:S(2)}, u32[]{:S(2)}) collective-permute-start(bf16[128,384]{1,0:T(8,128)(2,1)S(1)} %get-tuple-element.57), channel_id=1, source_target_pairs={{0,8},{8,0},{16,24},{24,16},{1,9},{9,1},{17,25},{25,17},{2,10},{10... | collective-permute-start | bytes 294920 | tf_op jit(solution)/shard_map/ppermute | solution.py:529
  42.3 0.1 collective-permute-start.16
  42.4 3.4 %shard_map.90 = (bf16[196,1024]{1,0:T(8,128)(2,1)}, bf16[64,512]{1,0:T(8,128)(2,1)}) custom-call(s32[1,196]{1,0:T(1,128)S(1)} %copy-done.3, s32[1,192]{1,0:T(1,128)S(1)} %copy-done.2, bf16[1024,1536]{1,0:T(8,128)(2,1)S(1)} %copy-done, bf16[832,128]{1,0:T(8,128)(2,1)S(1)} %collective-permute-done.7.refs_0_.refs_1_, ...), custom_call_target="tpu_custom_call" | custom-call | tf_op jit(solution)/shard_map/pallas_call | solution.py:244
  45.8 1.2 %collective-permute-done.14.refs_1_ = bf16[128,384]{1,0:T(8,128)(2,1)S(1)} collective-permute-done((bf16[128,384]{1,0:T(8,128)(2,1)S(1)}, bf16[128,384]{1,0:T(8,128)(2,1)S(1)}, u32[]{:S(2)}, u32[]{:S(2)}) %collective-permute-start.14) | collective-permute-done | bytes 98336 | tf_op jit(solution)/shard_map/ppermute | solution.py:529
  47.0 2.3 %collective-permute-done.16.refs_3_ = bf16[128,384]{1,0:T(8,128)(2,1)S(1)} collective-permute-done((bf16[128,384]{1,0:T(8,128)(2,1)S(1)}, bf16[128,384]{1,0:T(8,128)(2,1)S(1)}, u32[]{:S(2)}, u32[]{:S(2)}) %collective-permute-start.16) | collective-permute-done | bytes 98336 | tf_op jit(solution)/shard_map/ppermute | solution.py:529
  49.2 0.7 %shard_map.93 = f32[128,384]{1,0:T(8,128)} custom-call(bf16[128,384]{1,0:T(8,128)(2,1)S(1)} %get-tuple-element.55.refs_0_, bf16[128,384]{1,0:T(8,128)(2,1)S(1)} %collective-permute-done.14.refs_1_, bf16[128,384]{1,0:T(8,128)(2,1)S(1)} %collective-permute-done.15.refs_2_, bf16[128,384]{1,0:T(8,128)(2,1)S(1)} %collective-permute-done.16.refs_3_), custom_call_target="tpu_custom_call" | custom-call | tf_op jit(solution)/shard_map/pallas_call | solution.py:244
  (19 shorter events, 0.0 us)
Async XLA Ops:
  4.6 8.3 %collective-permute-start = (bf16[528,128]{1,0:T(8,128)(2,1)}, bf16[528,128]{1,0:T(8,128)(2,1)S(1)}, u32[]{:S(2)}, u32[]{:S(2)}) collective-permute-start(bf16[528,128]{1,0:T(8,128)(2,1)} %get-tuple-element.34), channel_id=1, source_target_pairs={{0,6},{1,7},{2,4},{3,5},{4,2},{5,3},{6,0},{7,1},{8,14},{9,15},{10,... | collective-permute-start | bytes 405512 | tf_op jit(solution)/shard_map/ppermute | solution.py:529
  8.5 7.2 %collective-permute-start.1 = (bf16[528,128]{1,0:T(8,128)(2,1)}, bf16[528,128]{1,0:T(8,128)(2,1)S(1)}, u32[]{:S(2)}, u32[]{:S(2)}) collective-permute-start(bf16[528,128]{1,0:T(8,128)(2,1)} %get-tuple-element.35), channel_id=1, source_target_pairs={{0,7},{1,6},{2,5},{3,4},{4,3},{5,2},{6,1},{7,0},{8,15},{9,14},{10,... | collective-permute-start | bytes 405512 | tf_op jit(solution)/shard_map/ppermute | solution.py:529
  8.5 9.6 %collective-permute-start.2 = (bf16[528,128]{1,0:T(8,128)(2,1)}, bf16[528,128]{1,0:T(8,128)(2,1)S(1)}, u32[]{:S(2)}, u32[]{:S(2)}) collective-permute-start(bf16[528,128]{1,0:T(8,128)(2,1)} %get-tuple-element.36), channel_id=1, source_target_pairs={{0,4},{1,5},{2,6},{3,7},{4,0},{5,1},{6,2},{7,3},{8,12},{9,13},{10,... | collective-permute-start | bytes 405512 | tf_op jit(solution)/shard_map/ppermute | solution.py:529
  9.7 9.6 %collective-permute-start.3 = (bf16[528,128]{1,0:T(8,128)(2,1)}, bf16[528,128]{1,0:T(8,128)(2,1)S(1)}, u32[]{:S(2)}, u32[]{:S(2)}) collective-permute-start(bf16[528,128]{1,0:T(8,128)(2,1)} %get-tuple-element.37), channel_id=1, source_target_pairs={{0,2},{1,3},{2,0},{3,1},{4,6},{5,7},{6,4},{7,5},{8,10},{9,11},{10,... | collective-permute-start | bytes 405512 | tf_op jit(solution)/shard_map/ppermute | solution.py:529
  11.2 9.8 %collective-permute-start.4 = (bf16[528,128]{1,0:T(8,128)(2,1)}, bf16[528,128]{1,0:T(8,128)(2,1)S(1)}, u32[]{:S(2)}, u32[]{:S(2)}) collective-permute-start(bf16[528,128]{1,0:T(8,128)(2,1)} %get-tuple-element.40), channel_id=1, source_target_pairs={{0,5},{1,4},{2,7},{3,6},{4,1},{5,0},{6,3},{7,2},{8,13},{9,12},{10,... | collective-permute-start | bytes 405512 | tf_op jit(solution)/shard_map/ppermute | solution.py:529
  12.9 8.1 %collective-permute-start.5 = (bf16[528,128]{1,0:T(8,128)(2,1)}, bf16[528,128]{1,0:T(8,128)(2,1)S(1)}, u32[]{:S(2)}, u32[]{:S(2)}) collective-permute-start(bf16[528,128]{1,0:T(8,128)(2,1)} %get-tuple-element.41), channel_id=1, source_target_pairs={{0,3},{1,2},{2,1},{3,0},{4,7},{5,6},{6,5},{7,4},{8,11},{9,10},{10,... | collective-permute-start | bytes 405512 | tf_op jit(solution)/shard_map/ppermute | solution.py:529
  15.8 5.2 %collective-permute-start.6 = (bf16[528,128]{1,0:T(8,128)(2,1)}, bf16[528,128]{1,0:T(8,128)(2,1)S(1)}, u32[]{:S(2)}, u32[]{:S(2)}) collective-permute-start(bf16[528,128]{1,0:T(8,128)(2,1)} %get-tuple-element.42), channel_id=1, source_target_pairs={{0,1},{1,0},{2,3},{3,2},{4,5},{5,4},{6,7},{7,6},{8,9},{9,8},{10,11... | collective-permute-start | bytes 405512 | tf_op jit(solution)/shard_map/ppermute | solution.py:529
  19.3 0.9 %copy-start.1 = (bf16[528,128]{1,0:T(8,128)(2,1)S(1)}, bf16[528,128]{1,0:T(8,128)(2,1)}, u32[]{:S(2)}) copy-start(bf16[528,128]{1,0:T(8,128)(2,1)} %get-tuple-element.33.refs_0_) | copy-start | bytes 405508
  20.7 21.6 %copy-start = (bf16[1024,1536]{1,0:T(8,128)(2,1)S(1)}, bf16[1024,1536]{1,0:T(8,128)(2,1)}, u32[]{:S(2)}) copy-start(bf16[1024,1536]{1,0:T(8,128)(2,1)} %w_hbm.1) | copy-start | bytes 9437188
  20.8 21.6 %copy-start.2 = (s32[1,192]{1,0:T(1,128)S(1)}, s32[1,192]{1,0:T(1,128)}, u32[]{:S(2)}) copy-start(s32[1,192]{1,0:T(1,128)} %get-tuple-element.32.target_ref) | copy-start | bytes 2308
  20.8 21.6 %copy-start.3 = (s32[1,196]{1,0:T(1,128)S(1)}, s32[1,196]{1,0:T(1,128)}, u32[]{:S(2)}) copy-start(s32[1,196]{1,0:T(1,128)} %get-tuple-element.31.segment_ref) | copy-start | bytes 2356
  22.8 7.4 %collective-permute-start.9 = (bf16[832,128]{1,0:T(8,128)(2,1)S(1)}, bf16[832,128]{1,0:T(8,128)(2,1)S(1)}, u32[]{:S(2)}, u32[]{:S(2)}) collective-permute-start(bf16[832,128]{1,0:T(8,128)(2,1)S(1)} %get-tuple-element.44), channel_id=1, source_target_pairs={{0,4},{1,5},{2,6},{3,7},{4,0},{5,1},{6,2},{7,3},{8,12},{9,13},{10,... | collective-permute-start | bytes 638984 | tf_op jit(solution)/shard_map/ppermute | solution.py:529
  24.6 8.1 %collective-permute-start.11 = (bf16[832,128]{1,0:T(8,128)(2,1)S(1)}, bf16[832,128]{1,0:T(8,128)(2,1)S(1)}, u32[]{:S(2)}, u32[]{:S(2)}) collective-permute-start(bf16[832,128]{1,0:T(8,128)(2,1)S(1)} %get-tuple-element.47), channel_id=1, source_target_pairs={{0,2},{1,3},{2,0},{3,1},{4,6},{5,7},{6,4},{7,5},{8,10},{9,11},{10,... | collective-permute-start | bytes 638984 | tf_op jit(solution)/shard_map/ppermute | solution.py:529
  26.1 9.9 %collective-permute-start.7 = (bf16[832,128]{1,0:T(8,128)(2,1)S(1)}, bf16[832,128]{1,0:T(8,128)(2,1)S(1)}, u32[]{:S(2)}, u32[]{:S(2)}) collective-permute-start(bf16[832,128]{1,0:T(8,128)(2,1)S(1)} %get-tuple-element.43), channel_id=1, source_target_pairs={{0,6},{1,7},{2,4},{3,5},{4,2},{5,3},{6,0},{7,1},{8,14},{9,15},{10,... | collective-permute-start | bytes 638984 | tf_op jit(solution)/shard_map/ppermute | solution.py:529
  26.4 9.6 %collective-permute-start.13 = (bf16[832,128]{1,0:T(8,128)(2,1)S(1)}, bf16[832,128]{1,0:T(8,128)(2,1)S(1)}, u32[]{:S(2)}, u32[]{:S(2)}) collective-permute-start(bf16[832,128]{1,0:T(8,128)(2,1)S(1)} %get-tuple-element.48.refs_6_.refs_0_), channel_id=1, source_target_pairs={{0,1},{1,0},{2,3},{3,2},{4,5},{5,4},{6,7},{7,6},{8,9},{9,8},{10,11... | collective-permute-start | bytes 638984 | tf_op jit(solution)/shard_map/ppermute | solution.py:529
  30.2 5.8 %collective-permute-start.10 = (bf16[832,128]{1,0:T(8,128)(2,1)S(1)}, bf16[832,128]{1,0:T(8,128)(2,1)S(1)}, u32[]{:S(2)}, u32[]{:S(2)}) collective-permute-start(bf16[832,128]{1,0:T(8,128)(2,1)S(1)} %shard_map.89.refs_2_), channel_id=1, source_target_pairs={{0,1},{1,0},{2,3},{3,2},{4,5},{5,4},{6,7},{7,6},{8,9},{9,8},{10,11... | collective-permute-start | bytes 638984 | tf_op jit(solution)/shard_map/ppermute | solution.py:529
  32.8 3.2 %collective-permute-start.12 = (bf16[832,128]{1,0:T(8,128)(2,1)S(1)}, bf16[832,128]{1,0:T(8,128)(2,1)S(1)}, u32[]{:S(2)}, u32[]{:S(2)}) collective-permute-start(bf16[832,128]{1,0:T(8,128)(2,1)S(1)} %collective-permute-done.11.refs_4_.refs_3_), channel_id=1, source_target_pairs={{0,1},{1,0},{2,3},{3,2},{4,5},{5,4},{6,7},{7,6},{8,9},{9,8},{10,11... | collective-permute-start | bytes 638984 | tf_op jit(solution)/shard_map/ppermute | solution.py:529
  36.0 1.5 %collective-permute-start.8 = (bf16[832,128]{1,0:T(8,128)(2,1)S(1)}, bf16[832,128]{1,0:T(8,128)(2,1)S(1)}, u32[]{:S(2)}, u32[]{:S(2)}) collective-permute-start(bf16[832,128]{1,0:T(8,128)(2,1)S(1)} %collective-permute-done.7.refs_0_.refs_1_), channel_id=1, source_target_pairs={{0,1},{1,0},{2,3},{3,2},{4,5},{5,4},{6,7},{7,6},{8,9},{9,8},{10,11... | collective-permute-start | bytes 638984 | tf_op jit(solution)/shard_map/ppermute | solution.py:529
  37.9 9.0 %collective-permute-start.14 = (bf16[128,384]{1,0:T(8,128)(2,1)S(1)}, bf16[128,384]{1,0:T(8,128)(2,1)S(1)}, u32[]{:S(2)}, u32[]{:S(2)}) collective-permute-start(bf16[128,384]{1,0:T(8,128)(2,1)S(1)} %get-tuple-element.56), channel_id=1, source_target_pairs={{0,16},{8,24},{16,0},{24,8},{1,17},{9,25},{17,1},{25,9},{2,18},{10... | collective-permute-start | bytes 294920 | tf_op jit(solution)/shard_map/ppermute | solution.py:529
  40.7 6.3 %collective-permute-start.15 = (bf16[128,384]{1,0:T(8,128)(2,1)S(1)}, bf16[128,384]{1,0:T(8,128)(2,1)S(1)}, u32[]{:S(2)}, u32[]{:S(2)}) collective-permute-start(bf16[128,384]{1,0:T(8,128)(2,1)S(1)} %get-tuple-element.57), channel_id=1, source_target_pairs={{0,8},{8,0},{16,24},{24,16},{1,9},{9,1},{17,25},{25,17},{2,10},{10... | collective-permute-start | bytes 294920 | tf_op jit(solution)/shard_map/ppermute | solution.py:529
  42.3 6.9 %collective-permute-start.16 = (bf16[128,384]{1,0:T(8,128)(2,1)S(1)}, bf16[128,384]{1,0:T(8,128)(2,1)S(1)}, u32[]{:S(2)}, u32[]{:S(2)}) collective-permute-start(bf16[128,384]{1,0:T(8,128)(2,1)S(1)} %get-tuple-element.58), channel_id=1, source_target_pairs={{0,24},{8,16},{16,8},{24,0},{1,25},{9,17},{17,9},{25,1},{2,26},{10... | collective-permute-start | bytes 294920 | tf_op jit(solution)/shard_map/ppermute | solution.py:529

commit v9 on v8

--- a/solution.py
+++ b/solution.py
@@ -468,7 +468,7 @@
 def weight_kernel(last, placed_ref, piece_ref, *refs):
     count = len(refs) // 2
     head = jnp.bitwise_xor(lax.axis_index("seq"), last)
-    columns = head_columns(placed_ref[...], [piece_ref])[0]
+    columns = head_columns(placed_ref[...], [piece_ref])[0].astype(jnp.bfloat16)
     width = refs[0].shape[1]
     groups = width // HEAD_DIM
     wide = [
@@ -478,12 +478,12 @@
     lane = lax.broadcasted_iota(jnp.int32, (1, width), 1)
     for flip in range(count):
         place = jnp.bitwise_xor(lax.axis_index("clip"), flip) * width + lane
-        others = refs[flip][...].astype(jnp.float32)
+        others = refs[flip][...]
         for part in range(3):
             first = (part * HEADS + head) * HEAD_DIM
             mine = (place >= first) & (place < first + HEAD_DIM)
             others = jnp.where(mine, wide[part], others)
-        refs[count + flip][...] = others.astype(jnp.bfloat16)
+        refs[count + flip][...] = others
 
 
 def patch_kernel(flips, segment_ref, target_ref, w_hbm, *refs):

time: 50.1 us -> 50 us (level)
  no operation moved by 1% of the time
where the time goes in v9:
time: 50 us; the launch traced here: 49.9 us
  waiting for transfers between devices  20.8 us (42%)
  starting transfers between devices  15.2 us (30%)
  Pallas kernels  12.3 us (25%)
  local copies, waits for them, and re-layouts  0.92 us (2%)
  between operations  0.73 us (1%)
    ppermute x17, waiting for transfers between devices, exchange(): lax.ppermute(rows, axis, [(index, index ^ flip) for index in range(count)])  20.8 us
    ppermute x17, starting transfers between devices, exchange(): lax.ppermute(rows, axis, [(index, index ^ flip) for index in range(count)])  15.2 us
    pallas_call x9, Pallas kernels, call(): pl.pallas_call(body, out_shape=outs, in_specs=[pl.BlockSpec(memory_space=...  12.3 us
  transfers between devices with their start and end apart: 17, of which 11 were waited for; matrix products, arithmetic and copies ran while one was open for 0% of the time, Pallas kernels for 11%

profile of v9, /device:TPU:0, one launch (start us, length us, event | category | flops | bytes accessed | tf_op | source)
XLA Modules:
  0.0 49.9 jit_solution(1388992111155469138)
XLA Ops:
  0.6 3.9 %shard_map.85 = (bf16[528,128]{1,0:T(8,128)(2,1)}, bf16[528,128]{1,0:T(8,128)(2,1)}, bf16[528,128]{1,0:T(8,128)(2,1)}, bf16[528,128]{1,0:T(8,128)(2,1)}, bf16[52...) custom-call(s32[1,196]{1,0:T(1,128)} %refs_0_.1, ...), custom_call_target="tpu_custom_call" | custom-call | tf_op jit(solution)/shard_map/pallas_call | solution.py:244
  4.6 4.0 %collective-permute-start = (bf16[528,128]{1,0:T(8,128)(2,1)}, bf16[528,128]{1,0:T(8,128)(2,1)S(1)}, u32[]{:S(2)}, u32[]{:S(2)}) collective-permute-start(bf16[528,128]{1,0:T(8,128)(2,1)} %get-tuple-element.34), channel_id=1, source_target_pairs={{0,6},{1,7},{2,4},{3,5},{4,2},{5,3},{6,0},{7,1},{8,14},{9,15},{10,... | collective-permute-start | bytes 405512 | tf_op jit(solution)/shard_map/ppermute | solution.py:529
  8.5 1.1 %collective-permute-start.2 = (bf16[528,128]{1,0:T(8,128)(2,1)}, bf16[528,128]{1,0:T(8,128)(2,1)S(1)}, u32[]{:S(2)}, u32[]{:S(2)}) collective-permute-start(bf16[528,128]{1,0:T(8,128)(2,1)} %get-tuple-element.36), channel_id=1, source_target_pairs={{0,4},{1,5},{2,6},{3,7},{4,0},{5,1},{6,2},{7,3},{8,12},{9,13},{10,... | collective-permute-start | bytes 405512 | tf_op jit(solution)/shard_map/ppermute | solution.py:529
  9.7 1.5 %collective-permute-start.3 = (bf16[528,128]{1,0:T(8,128)(2,1)}, bf16[528,128]{1,0:T(8,128)(2,1)S(1)}, u32[]{:S(2)}, u32[]{:S(2)}) collective-permute-start(bf16[528,128]{1,0:T(8,128)(2,1)} %get-tuple-element.37), channel_id=1, source_target_pairs={{0,2},{1,3},{2,0},{3,1},{4,6},{5,7},{6,4},{7,5},{8,10},{9,11},{10,... | collective-permute-start | bytes 405512 | tf_op jit(solution)/shard_map/ppermute | solution.py:529
  11.2 0.5 %collective-permute-start.4 = (bf16[528,128]{1,0:T(8,128)(2,1)}, bf16[528,128]{1,0:T(8,128)(2,1)S(1)}, u32[]{:S(2)}, u32[]{:S(2)}) collective-permute-start(bf16[528,128]{1,0:T(8,128)(2,1)} %get-tuple-element.40), channel_id=1, source_target_pairs={{0,5},{1,4},{2,7},{3,6},{4,1},{5,0},{6,3},{7,2},{8,13},{9,12},{10,... | collective-permute-start | bytes 405512 | tf_op jit(solution)/shard_map/ppermute | solution.py:529
  11.7 1.2 %collective-permute-done.refs_1_ = bf16[528,128]{1,0:T(8,128)(2,1)S(1)} collective-permute-done((bf16[528,128]{1,0:T(8,128)(2,1)}, bf16[528,128]{1,0:T(8,128)(2,1)S(1)}, u32[]{:S(2)}, u32[]{:S(2)}) %collective-permute-start) | collective-permute-done | bytes 135200 | tf_op jit(solution)/shard_map/ppermute | solution.py:529
  12.9 2.9 %collective-permute-done.1.refs_2_ = bf16[528,128]{1,0:T(8,128)(2,1)S(1)} collective-permute-done((bf16[528,128]{1,0:T(8,128)(2,1)}, bf16[528,128]{1,0:T(8,128)(2,1)S(1)}, u32[]{:S(2)}, u32[]{:S(2)}) %collective-permute-start.1) | collective-permute-done | bytes 135200 | tf_op jit(solution)/shard_map/ppermute | solution.py:529
  15.8 2.4 %collective-permute-done.2.refs_3_ = bf16[528,128]{1,0:T(8,128)(2,1)S(1)} collective-permute-done((bf16[528,128]{1,0:T(8,128)(2,1)}, bf16[528,128]{1,0:T(8,128)(2,1)S(1)}, u32[]{:S(2)}, u32[]{:S(2)}) %collective-permute-start.2) | collective-permute-done | bytes 135200 | tf_op jit(solution)/shard_map/ppermute | solution.py:529
  18.2 1.2 %collective-permute-done.3.refs_4_ = bf16[528,128]{1,0:T(8,128)(2,1)S(1)} collective-permute-done((bf16[528,128]{1,0:T(8,128)(2,1)}, bf16[528,128]{1,0:T(8,128)(2,1)S(1)}, u32[]{:S(2)}, u32[]{:S(2)}) %collective-permute-start.3) | collective-permute-done | bytes 135200 | tf_op jit(solution)/shard_map/ppermute | solution.py:529
  19.3 0.9 %copy-done.1 = bf16[528,128]{1,0:T(8,128)(2,1)S(1)} copy-done((bf16[528,128]{1,0:T(8,128)(2,1)S(1)}, bf16[528,128]{1,0:T(8,128)(2,1)}, u32[]{:S(2)}) %copy-start.1) | copy-done | bytes 135192
  20.2 0.5 %shard_map.86 = (bf16[512,192]{1,0:T(8,128)(2,1)S(1)}, s32[5,1,192]{2,1,0:T(1,128)S(1)}, bf16[5,64,64]{2,1,0:T(8,128)(2,1)S(1)}) custom-call(bf16[528,128]{1,0:T(8,128)(2,1)S(1)} %copy-done.1, bf16[528,128]{1,0:T(8,128)(2,1)S(1)} %collective-permute-done.refs_1_, bf16[528,128]{1,0:T(8,128)(2,1)S(1)} %collective-permute-done.1.refs_2_, ...), custom_call_target="tpu_custom_call" | custom-call | flops 1000000000 | tf_op jit(solution)/shard_map/pallas_call | solution.py:244
  20.7 0.0 copy-start
  20.8 0.0 copy-start.2
  20.8 0.2 collective-permute-done.4.refs_0_.refs_5_
  21.0 1.8 %shard_map.87 = (bf16[832,128]{1,0:T(8,128)(2,1)S(1)}, bf16[832,128]{1,0:T(8,128)(2,1)S(1)}, bf16[832,128]{1,0:T(8,128)(2,1)S(1)}, bf16[832,128]{1,0:T(8,128)(2,1)S(1)}, s32[3,1,192]{2,1,0:T(1,128)S(1)}) custom-call(bf16[512,192]{1,0:T(8,128)(2,1)S(1)} %get-tuple-element.38.early_ref, bf16[5,64,64]{2,1,0:T(8,128)(2,1)S(1)} %get-tuple-element.39.early_grad_ref, ...), custom_call_target="tpu_custom_call" | custom-call | tf_op jit(solution)/shard_map/pallas_call | solution.py:244
  22.8 1.8 %collective-permute-start.9 = (bf16[832,128]{1,0:T(8,128)(2,1)S(1)}, bf16[832,128]{1,0:T(8,128)(2,1)S(1)}, u32[]{:S(2)}, u32[]{:S(2)}) collective-permute-start(bf16[832,128]{1,0:T(8,128)(2,1)S(1)} %get-tuple-element.44), channel_id=1, source_target_pairs={{0,4},{1,5},{2,6},{3,7},{4,0},{5,1},{6,2},{7,3},{8,12},{9,13},{10,... | collective-permute-start | bytes 638984 | tf_op jit(solution)/shard_map/ppermute | solution.py:529
  24.6 1.5 %collective-permute-start.11 = (bf16[832,128]{1,0:T(8,128)(2,1)S(1)}, bf16[832,128]{1,0:T(8,128)(2,1)S(1)}, u32[]{:S(2)}, u32[]{:S(2)}) collective-permute-start(bf16[832,128]{1,0:T(8,128)(2,1)S(1)} %get-tuple-element.47), channel_id=1, source_target_pairs={{0,2},{1,3},{2,0},{3,1},{4,6},{5,7},{6,4},{7,5},{8,10},{9,11},{10,... | collective-permute-start | bytes 638984 | tf_op jit(solution)/shard_map/ppermute | solution.py:529
  26.1 0.2 collective-permute-start.7
  26.4 0.7 %shard_map.88.refs_1_.placed_ref = bf16[128,512]{1,0:T(8,128)(2,1)S(1)} custom-call(s32[5,1,192]{2,1,0:T(1,128)S(1)} %get-tuple-element.45.early_ref, s32[3,1,192]{2,1,0:T(1,128)S(1)} %get-tuple-element.46.late_ref, bf16[528,128]{1,0:T(8,128)(2,1)S(1)} %copy-done.1, bf16[528,128]{1,0:T(8,128)(2,1)S(1)} %collective-permute-done.refs_1_, ...), custom_call_target="tpu_custom_call" | custom-call | tf_op jit(solution)/shard_map/pallas_call | solution.py:244
  27.1 3.1 %collective-permute-done.9.refs_0_ = bf16[832,128]{1,0:T(8,128)(2,1)S(1)} collective-permute-done((bf16[832,128]{1,0:T(8,128)(2,1)S(1)}, bf16[832,128]{1,0:T(8,128)(2,1)S(1)}, u32[]{:S(2)}, u32[]{:S(2)}) %collective-permute-start.9) | collective-permute-done | bytes 213024 | tf_op jit(solution)/shard_map/ppermute | solution.py:529
  30.2 2.6 %collective-permute-done.11.refs_4_.refs_3_ = bf16[832,128]{1,0:T(8,128)(2,1)S(1)} collective-permute-done((bf16[832,128]{1,0:T(8,128)(2,1)S(1)}, bf16[832,128]{1,0:T(8,128)(2,1)S(1)}, u32[]{:S(2)}, u32[]{:S(2)}) %collective-permute-start.11) | collective-permute-done | bytes 213024 | tf_op jit(solution)/shard_map/ppermute | solution.py:529
  32.8 3.2 %collective-permute-done.7.refs_0_.refs_1_ = bf16[832,128]{1,0:T(8,128)(2,1)S(1)} collective-permute-done((bf16[832,128]{1,0:T(8,128)(2,1)S(1)}, bf16[832,128]{1,0:T(8,128)(2,1)S(1)}, u32[]{:S(2)}, u32[]{:S(2)}) %collective-permute-start.7) | collective-permute-done | bytes 213024 | tf_op jit(solution)/shard_map/ppermute | solution.py:529
  36.0 0.8 %shard_map.91 = (bf16[128,384]{1,0:T(8,128)(2,1)S(1)}, bf16[128,384]{1,0:T(8,128)(2,1)S(1)}, bf16[128,384]{1,0:T(8,128)(2,1)S(1)}, bf16[128,384]{1,0:T(8,128)(2,1)S(1)}) custom-call(bf16[128,512]{1,0:T(8,128)(2,1)S(1)} %shard_map.88.refs_1_.placed_ref, bf16[832,128]{1,0:T(8,128)(2,1)S(1)} %get-tuple-element.48.refs_6_.refs_0_, ...), custom_call_target="tpu_custom_call" | custom-call | tf_op jit(solution)/shard_map/pallas_call | solution.py:244
  36.8 0.6 %collective-permute-done.8.refs_1_.piece_ref = bf16[832,128]{1,0:T(8,128)(2,1)S(1)} collective-permute-done((bf16[832,128]{1,0:T(8,128)(2,1)S(1)}, bf16[832,128]{1,0:T(8,128)(2,1)S(1)}, u32[]{:S(2)}, u32[]{:S(2)}) %collective-permute-start.8) | collective-permute-done | bytes 213024 | tf_op jit(solution)/shard_map/ppermute | solution.py:529
  37.5 0.4 shard_map.92
  37.9 2.8 %collective-permute-start.14 = (bf16[128,384]{1,0:T(8,128)(2,1)S(1)}, bf16[128,384]{1,0:T(8,128)(2,1)S(1)}, u32[]{:S(2)}, u32[]{:S(2)}) collective-permute-start(bf16[128,384]{1,0:T(8,128)(2,1)S(1)} %get-tuple-element.56), channel_id=1, source_target_pairs={{0,16},{8,24},{16,0},{24,8},{1,17},{9,25},{17,1},{25,9},{2,18},{10... | collective-permute-start | bytes 294920 | tf_op jit(solution)/shard_map/ppermute | solution.py:529
  40.6 1.6 %collective-permute-start.15 = (bf16[128,384]{1,0:T(8,128)(2,1)S(1)}, bf16[128,384]{1,0:T(8,128)(2,1)S(1)}, u32[]{:S(2)}, u32[]{:S(2)}) collective-permute-start(bf16[128,384]{1,0:T(8,128)(2,1)S(1)} %get-tuple-element.57), channel_id=1, source_target_pairs={{0,8},{8,0},{16,24},{24,16},{1,9},{9,1},{17,25},{25,17},{2,10},{10... | collective-permute-start | bytes 294920 | tf_op jit(solution)/shard_map/ppermute | solution.py:529
  42.2 0.1 collective-permute-start.16
  42.3 3.4 %shard_map.90 = (bf16[196,1024]{1,0:T(8,128)(2,1)}, bf16[64,512]{1,0:T(8,128)(2,1)}) custom-call(s32[1,196]{1,0:T(1,128)S(1)} %copy-done.3, s32[1,192]{1,0:T(1,128)S(1)} %copy-done.2, bf16[1024,1536]{1,0:T(8,128)(2,1)S(1)} %copy-done, bf16[832,128]{1,0:T(8,128)(2,1)S(1)} %collective-permute-done.7.refs_0_.refs_1_, ...), custom_call_target="tpu_custom_call" | custom-call | tf_op jit(solution)/shard_map/pallas_call | solution.py:244
  45.7 1.2 %collective-permute-done.14.refs_1_ = bf16[128,384]{1,0:T(8,128)(2,1)S(1)} collective-permute-done((bf16[128,384]{1,0:T(8,128)(2,1)S(1)}, bf16[128,384]{1,0:T(8,128)(2,1)S(1)}, u32[]{:S(2)}, u32[]{:S(2)}) %collective-permute-start.14) | collective-permute-done | bytes 98336 | tf_op jit(solution)/shard_map/ppermute | solution.py:529
  46.9 2.3 %collective-permute-done.16.refs_3_ = bf16[128,384]{1,0:T(8,128)(2,1)S(1)} collective-permute-done((bf16[128,384]{1,0:T(8,128)(2,1)S(1)}, bf16[128,384]{1,0:T(8,128)(2,1)S(1)}, u32[]{:S(2)}, u32[]{:S(2)}) %collective-permute-start.16) | collective-permute-done | bytes 98336 | tf_op jit(solution)/shard_map/ppermute | solution.py:529
  49.1 0.7 %shard_map.93 = f32[128,384]{1,0:T(8,128)} custom-call(bf16[128,384]{1,0:T(8,128)(2,1)S(1)} %get-tuple-element.55.refs_0_, bf16[128,384]{1,0:T(8,128)(2,1)S(1)} %collective-permute-done.14.refs_1_, bf16[128,384]{1,0:T(8,128)(2,1)S(1)} %collective-permute-done.15.refs_2_, bf16[128,384]{1,0:T(8,128)(2,1)S(1)} %collective-permute-done.16.refs_3_), custom_call_target="tpu_custom_call" | custom-call | tf_op jit(solution)/shard_map/pallas_call | solution.py:244
  (19 shorter events, 0.0 us)
Async XLA Ops:
  4.6 8.3 %collective-permute-start = (bf16[528,128]{1,0:T(8,128)(2,1)}, bf16[528,128]{1,0:T(8,128)(2,1)S(1)}, u32[]{:S(2)}, u32[]{:S(2)}) collective-permute-start(bf16[528,128]{1,0:T(8,128)(2,1)} %get-tuple-element.34), channel_id=1, source_target_pairs={{0,6},{1,7},{2,4},{3,5},{4,2},{5,3},{6,0},{7,1},{8,14},{9,15},{10,... | collective-permute-start | bytes 405512 | tf_op jit(solution)/shard_map/ppermute | solution.py:529
  8.5 7.2 %collective-permute-start.1 = (bf16[528,128]{1,0:T(8,128)(2,1)}, bf16[528,128]{1,0:T(8,128)(2,1)S(1)}, u32[]{:S(2)}, u32[]{:S(2)}) collective-permute-start(bf16[528,128]{1,0:T(8,128)(2,1)} %get-tuple-element.35), channel_id=1, source_target_pairs={{0,7},{1,6},{2,5},{3,4},{4,3},{5,2},{6,1},{7,0},{8,15},{9,14},{10,... | collective-permute-start | bytes 405512 | tf_op jit(solution)/shard_map/ppermute | solution.py:529
  8.5 9.6 %collective-permute-start.2 = (bf16[528,128]{1,0:T(8,128)(2,1)}, bf16[528,128]{1,0:T(8,128)(2,1)S(1)}, u32[]{:S(2)}, u32[]{:S(2)}) collective-permute-start(bf16[528,128]{1,0:T(8,128)(2,1)} %get-tuple-element.36), channel_id=1, source_target_pairs={{0,4},{1,5},{2,6},{3,7},{4,0},{5,1},{6,2},{7,3},{8,12},{9,13},{10,... | collective-permute-start | bytes 405512 | tf_op jit(solution)/shard_map/ppermute | solution.py:529
  9.7 9.6 %collective-permute-start.3 = (bf16[528,128]{1,0:T(8,128)(2,1)}, bf16[528,128]{1,0:T(8,128)(2,1)S(1)}, u32[]{:S(2)}, u32[]{:S(2)}) collective-permute-start(bf16[528,128]{1,0:T(8,128)(2,1)} %get-tuple-element.37), channel_id=1, source_target_pairs={{0,2},{1,3},{2,0},{3,1},{4,6},{5,7},{6,4},{7,5},{8,10},{9,11},{10,... | collective-permute-start | bytes 405512 | tf_op jit(solution)/shard_map/ppermute | solution.py:529
  11.2 9.8 %collective-permute-start.4 = (bf16[528,128]{1,0:T(8,128)(2,1)}, bf16[528,128]{1,0:T(8,128)(2,1)S(1)}, u32[]{:S(2)}, u32[]{:S(2)}) collective-permute-start(bf16[528,128]{1,0:T(8,128)(2,1)} %get-tuple-element.40), channel_id=1, source_target_pairs={{0,5},{1,4},{2,7},{3,6},{4,1},{5,0},{6,3},{7,2},{8,13},{9,12},{10,... | collective-permute-start | bytes 405512 | tf_op jit(solution)/shard_map/ppermute | solution.py:529
  12.9 8.1 %collective-permute-start.5 = (bf16[528,128]{1,0:T(8,128)(2,1)}, bf16[528,128]{1,0:T(8,128)(2,1)S(1)}, u32[]{:S(2)}, u32[]{:S(2)}) collective-permute-start(bf16[528,128]{1,0:T(8,128)(2,1)} %get-tuple-element.41), channel_id=1, source_target_pairs={{0,3},{1,2},{2,1},{3,0},{4,7},{5,6},{6,5},{7,4},{8,11},{9,10},{10,... | collective-permute-start | bytes 405512 | tf_op jit(solution)/shard_map/ppermute | solution.py:529
  15.8 5.2 %collective-permute-start.6 = (bf16[528,128]{1,0:T(8,128)(2,1)}, bf16[528,128]{1,0:T(8,128)(2,1)S(1)}, u32[]{:S(2)}, u32[]{:S(2)}) collective-permute-start(bf16[528,128]{1,0:T(8,128)(2,1)} %get-tuple-element.42), channel_id=1, source_target_pairs={{0,1},{1,0},{2,3},{3,2},{4,5},{5,4},{6,7},{7,6},{8,9},{9,8},{10,11... | collective-permute-start | bytes 405512 | tf_op jit(solution)/shard_map/ppermute | solution.py:529
  19.3 0.9 %copy-start.1 = (bf16[528,128]{1,0:T(8,128)(2,1)S(1)}, bf16[528,128]{1,0:T(8,128)(2,1)}, u32[]{:S(2)}) copy-start(bf16[528,128]{1,0:T(8,128)(2,1)} %get-tuple-element.33.refs_0_) | copy-start | bytes 405508
  20.7 21.6 %copy-start = (bf16[1024,1536]{1,0:T(8,128)(2,1)S(1)}, bf16[1024,1536]{1,0:T(8,128)(2,1)}, u32[]{:S(2)}) copy-start(bf16[1024,1536]{1,0:T(8,128)(2,1)} %w_hbm.1) | copy-start | bytes 9437188
  20.8 21.6 %copy-start.2 = (s32[1,192]{1,0:T(1,128)S(1)}, s32[1,192]{1,0:T(1,128)}, u32[]{:S(2)}) copy-start(s32[1,192]{1,0:T(1,128)} %get-tuple-element.32.target_ref) | copy-start | bytes 2308
  20.8 21.5 %copy-start.3 = (s32[1,196]{1,0:T(1,128)S(1)}, s32[1,196]{1,0:T(1,128)}, u32[]{:S(2)}) copy-start(s32[1,196]{1,0:T(1,128)} %get-tuple-element.31.segment_ref) | copy-start | bytes 2356
  22.8 7.4 %collective-permute-start.9 = (bf16[832,128]{1,0:T(8,128)(2,1)S(1)}, bf16[832,128]{1,0:T(8,128)(2,1)S(1)}, u32[]{:S(2)}, u32[]{:S(2)}) collective-permute-start(bf16[832,128]{1,0:T(8,128)(2,1)S(1)} %get-tuple-element.44), channel_id=1, source_target_pairs={{0,4},{1,5},{2,6},{3,7},{4,0},{5,1},{6,2},{7,3},{8,12},{9,13},{10,... | collective-permute-start | bytes 638984 | tf_op jit(solution)/shard_map/ppermute | solution.py:529
  24.6 8.1 %collective-permute-start.11 = (bf16[832,128]{1,0:T(8,128)(2,1)S(1)}, bf16[832,128]{1,0:T(8,128)(2,1)S(1)}, u32[]{:S(2)}, u32[]{:S(2)}) collective-permute-start(bf16[832,128]{1,0:T(8,128)(2,1)S(1)} %get-tuple-element.47), channel_id=1, source_target_pairs={{0,2},{1,3},{2,0},{3,1},{4,6},{5,7},{6,4},{7,5},{8,10},{9,11},{10,... | collective-permute-start | bytes 638984 | tf_op jit(solution)/shard_map/ppermute | solution.py:529
  26.1 9.9 %collective-permute-start.7 = (bf16[832,128]{1,0:T(8,128)(2,1)S(1)}, bf16[832,128]{1,0:T(8,128)(2,1)S(1)}, u32[]{:S(2)}, u32[]{:S(2)}) collective-permute-start(bf16[832,128]{1,0:T(8,128)(2,1)S(1)} %get-tuple-element.43), channel_id=1, source_target_pairs={{0,6},{1,7},{2,4},{3,5},{4,2},{5,3},{6,0},{7,1},{8,14},{9,15},{10,... | collective-permute-start | bytes 638984 | tf_op jit(solution)/shard_map/ppermute | solution.py:529
  26.4 9.6 %collective-permute-start.13 = (bf16[832,128]{1,0:T(8,128)(2,1)S(1)}, bf16[832,128]{1,0:T(8,128)(2,1)S(1)}, u32[]{:S(2)}, u32[]{:S(2)}) collective-permute-start(bf16[832,128]{1,0:T(8,128)(2,1)S(1)} %get-tuple-element.48.refs_6_.refs_0_), channel_id=1, source_target_pairs={{0,1},{1,0},{2,3},{3,2},{4,5},{5,4},{6,7},{7,6},{8,9},{9,8},{10,11... | collective-permute-start | bytes 638984 | tf_op jit(solution)/shard_map/ppermute | solution.py:529
  30.2 5.8 %collective-permute-start.10 = (bf16[832,128]{1,0:T(8,128)(2,1)S(1)}, bf16[832,128]{1,0:T(8,128)(2,1)S(1)}, u32[]{:S(2)}, u32[]{:S(2)}) collective-permute-start(bf16[832,128]{1,0:T(8,128)(2,1)S(1)} %shard_map.89.refs_2_), channel_id=1, source_target_pairs={{0,1},{1,0},{2,3},{3,2},{4,5},{5,4},{6,7},{7,6},{8,9},{9,8},{10,11... | collective-permute-start | bytes 638984 | tf_op jit(solution)/shard_map/ppermute | solution.py:529
  32.8 3.2 %collective-permute-start.12 = (bf16[832,128]{1,0:T(8,128)(2,1)S(1)}, bf16[832,128]{1,0:T(8,128)(2,1)S(1)}, u32[]{:S(2)}, u32[]{:S(2)}) collective-permute-start(bf16[832,128]{1,0:T(8,128)(2,1)S(1)} %collective-permute-done.11.refs_4_.refs_3_), channel_id=1, source_target_pairs={{0,1},{1,0},{2,3},{3,2},{4,5},{5,4},{6,7},{7,6},{8,9},{9,8},{10,11... | collective-permute-start | bytes 638984 | tf_op jit(solution)/shard_map/ppermute | solution.py:529
  36.0 1.5 %collective-permute-start.8 = (bf16[832,128]{1,0:T(8,128)(2,1)S(1)}, bf16[832,128]{1,0:T(8,128)(2,1)S(1)}, u32[]{:S(2)}, u32[]{:S(2)}) collective-permute-start(bf16[832,128]{1,0:T(8,128)(2,1)S(1)} %collective-permute-done.7.refs_0_.refs_1_), channel_id=1, source_target_pairs={{0,1},{1,0},{2,3},{3,2},{4,5},{5,4},{6,7},{7,6},{8,9},{9,8},{10,11... | collective-permute-start | bytes 638984 | tf_op jit(solution)/shard_map/ppermute | solution.py:529
  37.9 9.0 %collective-permute-start.14 = (bf16[128,384]{1,0:T(8,128)(2,1)S(1)}, bf16[128,384]{1,0:T(8,128)(2,1)S(1)}, u32[]{:S(2)}, u32[]{:S(2)}) collective-permute-start(bf16[128,384]{1,0:T(8,128)(2,1)S(1)} %get-tuple-element.56), channel_id=1, source_target_pairs={{0,16},{8,24},{16,0},{24,8},{1,17},{9,25},{17,1},{25,9},{2,18},{10... | collective-permute-start | bytes 294920 | tf_op jit(solution)/shard_map/ppermute | solution.py:529
  40.6 6.3 %collective-permute-start.15 = (bf16[128,384]{1,0:T(8,128)(2,1)S(1)}, bf16[128,384]{1,0:T(8,128)(2,1)S(1)}, u32[]{:S(2)}, u32[]{:S(2)}) collective-permute-start(bf16[128,384]{1,0:T(8,128)(2,1)S(1)} %get-tuple-element.57), channel_id=1, source_target_pairs={{0,8},{8,0},{16,24},{24,16},{1,9},{9,1},{17,25},{25,17},{2,10},{10... | collective-permute-start | bytes 294920 | tf_op jit(solution)/shard_map/ppermute | solution.py:529
  42.2 6.9 %collective-permute-start.16 = (bf16[128,384]{1,0:T(8,128)(2,1)S(1)}, bf16[128,384]{1,0:T(8,128)(2,1)S(1)}, u32[]{:S(2)}, u32[]{:S(2)}) collective-permute-start(bf16[128,384]{1,0:T(8,128)(2,1)S(1)} %get-tuple-element.58), channel_id=1, source_target_pairs={{0,24},{8,16},{16,8},{24,0},{1,25},{9,17},{17,9},{25,1},{2,26},{10... | collective-permute-start | bytes 294920 | tf_op jit(solution)/shard_map/ppermute | solution.py:529

commit v10 on v9

--- a/solution.py
+++ b/solution.py
@@ -300,7 +300,7 @@
     counts = jnp.sum(jnp.where(member, 1.0, 0.0), axis=1, keepdims=True)
     copies[1].wait()
     token_sums = dot(one_hot(member), patch_ref[...])
-    tokens = (token_sums / jnp.maximum(counts, 1.0)).astype(jnp.bfloat16)
+    tokens = (token_sums * (1.0 / jnp.maximum(counts, 1.0))).astype(jnp.bfloat16)
     for copy in copies[2:5]:
         copy.wait()
     shard, slot = shard_ref[...], slot_ref[...]

time: 50 us -> 50 us (level)
  no operation moved by 1% of the time
where the time goes in v10:
time: 50 us; the launch traced here: 49.9 us
  waiting for transfers between devices  20.8 us (42%)
  starting transfers between devices  15.2 us (30%)
  Pallas kernels  12.3 us (25%)
  local copies, waits for them, and re-layouts  0.92 us (2%)
  between operations  0.73 us (1%)
    ppermute x17, waiting for transfers between devices, exchange(): lax.ppermute(rows, axis, [(index, index ^ flip) for index in range(count)])  20.8 us
    ppermute x17, starting transfers between devices, exchange(): lax.ppermute(rows, axis, [(index, index ^ flip) for index in range(count)])  15.2 us
    pallas_call x9, Pallas kernels, call(): pl.pallas_call(body, out_shape=outs, in_specs=[pl.BlockSpec(memory_space=...  12.3 us
  transfers between devices with their start and end apart: 17, of which 11 were waited for; matrix products, arithmetic and copies ran while one was open for 0% of the time, Pallas kernels for 11%

profile of v10, /device:TPU:0, one launch (start us, length us, event | category | flops | bytes accessed | tf_op | source)
XLA Modules:
  0.0 49.9 jit_solution(1388992111155469138)
XLA Ops:
  0.6 3.9 %shard_map.85 = (bf16[528,128]{1,0:T(8,128)(2,1)}, bf16[528,128]{1,0:T(8,128)(2,1)}, bf16[528,128]{1,0:T(8,128)(2,1)}, bf16[528,128]{1,0:T(8,128)(2,1)}, bf16[52...) custom-call(s32[1,196]{1,0:T(1,128)} %refs_0_.1, ...), custom_call_target="tpu_custom_call" | custom-call | tf_op jit(solution)/shard_map/pallas_call | solution.py:244
  4.6 4.0 %collective-permute-start = (bf16[528,128]{1,0:T(8,128)(2,1)}, bf16[528,128]{1,0:T(8,128)(2,1)S(1)}, u32[]{:S(2)}, u32[]{:S(2)}) collective-permute-start(bf16[528,128]{1,0:T(8,128)(2,1)} %get-tuple-element.34), channel_id=1, source_target_pairs={{0,6},{1,7},{2,4},{3,5},{4,2},{5,3},{6,0},{7,1},{8,14},{9,15},{10,... | collective-permute-start | bytes 405512 | tf_op jit(solution)/shard_map/ppermute | solution.py:529
  8.5 1.1 %collective-permute-start.2 = (bf16[528,128]{1,0:T(8,128)(2,1)}, bf16[528,128]{1,0:T(8,128)(2,1)S(1)}, u32[]{:S(2)}, u32[]{:S(2)}) collective-permute-start(bf16[528,128]{1,0:T(8,128)(2,1)} %get-tuple-element.36), channel_id=1, source_target_pairs={{0,4},{1,5},{2,6},{3,7},{4,0},{5,1},{6,2},{7,3},{8,12},{9,13},{10,... | collective-permute-start | bytes 405512 | tf_op jit(solution)/shard_map/ppermute | solution.py:529
  9.7 1.5 %collective-permute-start.3 = (bf16[528,128]{1,0:T(8,128)(2,1)}, bf16[528,128]{1,0:T(8,128)(2,1)S(1)}, u32[]{:S(2)}, u32[]{:S(2)}) collective-permute-start(bf16[528,128]{1,0:T(8,128)(2,1)} %get-tuple-element.37), channel_id=1, source_target_pairs={{0,2},{1,3},{2,0},{3,1},{4,6},{5,7},{6,4},{7,5},{8,10},{9,11},{10,... | collective-permute-start | bytes 405512 | tf_op jit(solution)/shard_map/ppermute | solution.py:529
  11.2 0.5 %collective-permute-start.4 = (bf16[528,128]{1,0:T(8,128)(2,1)}, bf16[528,128]{1,0:T(8,128)(2,1)S(1)}, u32[]{:S(2)}, u32[]{:S(2)}) collective-permute-start(bf16[528,128]{1,0:T(8,128)(2,1)} %get-tuple-element.40), channel_id=1, source_target_pairs={{0,5},{1,4},{2,7},{3,6},{4,1},{5,0},{6,3},{7,2},{8,13},{9,12},{10,... | collective-permute-start | bytes 405512 | tf_op jit(solution)/shard_map/ppermute | solution.py:529
  11.7 1.2 %collective-permute-done.refs_1_ = bf16[528,128]{1,0:T(8,128)(2,1)S(1)} collective-permute-done((bf16[528,128]{1,0:T(8,128)(2,1)}, bf16[528,128]{1,0:T(8,128)(2,1)S(1)}, u32[]{:S(2)}, u32[]{:S(2)}) %collective-permute-start) | collective-permute-done | bytes 135200 | tf_op jit(solution)/shard_map/ppermute | solution.py:529
  12.9 2.9 %collective-permute-done.1.refs_2_ = bf16[528,128]{1,0:T(8,128)(2,1)S(1)} collective-permute-done((bf16[528,128]{1,0:T(8,128)(2,1)}, bf16[528,128]{1,0:T(8,128)(2,1)S(1)}, u32[]{:S(2)}, u32[]{:S(2)}) %collective-permute-start.1) | collective-permute-done | bytes 135200 | tf_op jit(solution)/shard_map/ppermute | solution.py:529
  15.8 2.4 %collective-permute-done.2.refs_3_ = bf16[528,128]{1,0:T(8,128)(2,1)S(1)} collective-permute-done((bf16[528,128]{1,0:T(8,128)(2,1)}, bf16[528,128]{1,0:T(8,128)(2,1)S(1)}, u32[]{:S(2)}, u32[]{:S(2)}) %collective-permute-start.2) | collective-permute-done | bytes 135200 | tf_op jit(solution)/shard_map/ppermute | solution.py:529
  18.2 1.2 %collective-permute-done.3.refs_4_ = bf16[528,128]{1,0:T(8,128)(2,1)S(1)} collective-permute-done((bf16[528,128]{1,0:T(8,128)(2,1)}, bf16[528,128]{1,0:T(8,128)(2,1)S(1)}, u32[]{:S(2)}, u32[]{:S(2)}) %collective-permute-start.3) | collective-permute-done | bytes 135200 | tf_op jit(solution)/shard_map/ppermute | solution.py:529
  19.3 0.9 %copy-done.1 = bf16[528,128]{1,0:T(8,128)(2,1)S(1)} copy-done((bf16[528,128]{1,0:T(8,128)(2,1)S(1)}, bf16[528,128]{1,0:T(8,128)(2,1)}, u32[]{:S(2)}) %copy-start.1) | copy-done | bytes 135192
  20.2 0.5 %shard_map.86 = (bf16[512,192]{1,0:T(8,128)(2,1)S(1)}, s32[5,1,192]{2,1,0:T(1,128)S(1)}, bf16[5,64,64]{2,1,0:T(8,128)(2,1)S(1)}) custom-call(bf16[528,128]{1,0:T(8,128)(2,1)S(1)} %copy-done.1, bf16[528,128]{1,0:T(8,128)(2,1)S(1)} %collective-permute-done.refs_1_, bf16[528,128]{1,0:T(8,128)(2,1)S(1)} %collective-permute-done.1.refs_2_, ...), custom_call_target="tpu_custom_call" | custom-call | flops 1000000000 | tf_op jit(solution)/shard_map/pallas_call | solution.py:244
  20.7 0.0 copy-start
  20.8 0.0 copy-start.2
  20.8 0.2 collective-permute-done.4.refs_0_.refs_5_
  21.0 1.8 %shard_map.87 = (bf16[832,128]{1,0:T(8,128)(2,1)S(1)}, bf16[832,128]{1,0:T(8,128)(2,1)S(1)}, bf16[832,128]{1,0:T(8,128)(2,1)S(1)}, bf16[832,128]{1,0:T(8,128)(2,1)S(1)}, s32[3,1,192]{2,1,0:T(1,128)S(1)}) custom-call(bf16[512,192]{1,0:T(8,128)(2,1)S(1)} %get-tuple-element.38.early_ref, bf16[5,64,64]{2,1,0:T(8,128)(2,1)S(1)} %get-tuple-element.39.early_grad_ref, ...), custom_call_target="tpu_custom_call" | custom-call | tf_op jit(solution)/shard_map/pallas_call | solution.py:244
  22.8 1.8 %collective-permute-start.9 = (bf16[832,128]{1,0:T(8,128)(2,1)S(1)}, bf16[832,128]{1,0:T(8,128)(2,1)S(1)}, u32[]{:S(2)}, u32[]{:S(2)}) collective-permute-start(bf16[832,128]{1,0:T(8,128)(2,1)S(1)} %get-tuple-element.44), channel_id=1, source_target_pairs={{0,4},{1,5},{2,6},{3,7},{4,0},{5,1},{6,2},{7,3},{8,12},{9,13},{10,... | collective-permute-start | bytes 638984 | tf_op jit(solution)/shard_map/ppermute | solution.py:529
  24.6 1.5 %collective-permute-start.11 = (bf16[832,128]{1,0:T(8,128)(2,1)S(1)}, bf16[832,128]{1,0:T(8,128)(2,1)S(1)}, u32[]{:S(2)}, u32[]{:S(2)}) collective-permute-start(bf16[832,128]{1,0:T(8,128)(2,1)S(1)} %get-tuple-element.47), channel_id=1, source_target_pairs={{0,2},{1,3},{2,0},{3,1},{4,6},{5,7},{6,4},{7,5},{8,10},{9,11},{10,... | collective-permute-start | bytes 638984 | tf_op jit(solution)/shard_map/ppermute | solution.py:529
  26.1 0.2 collective-permute-start.7
  26.4 0.7 %shard_map.88.refs_1_.placed_ref = bf16[128,512]{1,0:T(8,128)(2,1)S(1)} custom-call(s32[5,1,192]{2,1,0:T(1,128)S(1)} %get-tuple-element.45.early_ref, s32[3,1,192]{2,1,0:T(1,128)S(1)} %get-tuple-element.46.late_ref, bf16[528,128]{1,0:T(8,128)(2,1)S(1)} %copy-done.1, bf16[528,128]{1,0:T(8,128)(2,1)S(1)} %collective-permute-done.refs_1_, ...), custom_call_target="tpu_custom_call" | custom-call | tf_op jit(solution)/shard_map/pallas_call | solution.py:244
  27.1 3.1 %collective-permute-done.9.refs_0_ = bf16[832,128]{1,0:T(8,128)(2,1)S(1)} collective-permute-done((bf16[832,128]{1,0:T(8,128)(2,1)S(1)}, bf16[832,128]{1,0:T(8,128)(2,1)S(1)}, u32[]{:S(2)}, u32[]{:S(2)}) %collective-permute-start.9) | collective-permute-done | bytes 213024 | tf_op jit(solution)/shard_map/ppermute | solution.py:529
  30.2 2.6 %collective-permute-done.11.refs_4_.refs_3_ = bf16[832,128]{1,0:T(8,128)(2,1)S(1)} collective-permute-done((bf16[832,128]{1,0:T(8,128)(2,1)S(1)}, bf16[832,128]{1,0:T(8,128)(2,1)S(1)}, u32[]{:S(2)}, u32[]{:S(2)}) %collective-permute-start.11) | collective-permute-done | bytes 213024 | tf_op jit(solution)/shard_map/ppermute | solution.py:529
  32.8 3.2 %collective-permute-done.7.refs_0_.refs_1_ = bf16[832,128]{1,0:T(8,128)(2,1)S(1)} collective-permute-done((bf16[832,128]{1,0:T(8,128)(2,1)S(1)}, bf16[832,128]{1,0:T(8,128)(2,1)S(1)}, u32[]{:S(2)}, u32[]{:S(2)}) %collective-permute-start.7) | collective-permute-done | bytes 213024 | tf_op jit(solution)/shard_map/ppermute | solution.py:529
  36.0 0.8 %shard_map.91 = (bf16[128,384]{1,0:T(8,128)(2,1)S(1)}, bf16[128,384]{1,0:T(8,128)(2,1)S(1)}, bf16[128,384]{1,0:T(8,128)(2,1)S(1)}, bf16[128,384]{1,0:T(8,128)(2,1)S(1)}) custom-call(bf16[128,512]{1,0:T(8,128)(2,1)S(1)} %shard_map.88.refs_1_.placed_ref, bf16[832,128]{1,0:T(8,128)(2,1)S(1)} %get-tuple-element.48.refs_6_.refs_0_, ...), custom_call_target="tpu_custom_call" | custom-call | tf_op jit(solution)/shard_map/pallas_call | solution.py:244
  36.8 0.6 %collective-permute-done.8.refs_1_.piece_ref = bf16[832,128]{1,0:T(8,128)(2,1)S(1)} collective-permute-done((bf16[832,128]{1,0:T(8,128)(2,1)S(1)}, bf16[832,128]{1,0:T(8,128)(2,1)S(1)}, u32[]{:S(2)}, u32[]{:S(2)}) %collective-permute-start.8) | collective-permute-done | bytes 213024 | tf_op jit(solution)/shard_map/ppermute | solution.py:529
  37.5 0.4 shard_map.92
  37.9 2.8 %collective-permute-start.14 = (bf16[128,384]{1,0:T(8,128)(2,1)S(1)}, bf16[128,384]{1,0:T(8,128)(2,1)S(1)}, u32[]{:S(2)}, u32[]{:S(2)}) collective-permute-start(bf16[128,384]{1,0:T(8,128)(2,1)S(1)} %get-tuple-element.56), channel_id=1, source_target_pairs={{0,16},{8,24},{16,0},{24,8},{1,17},{9,25},{17,1},{25,9},{2,18},{10... | collective-permute-start | bytes 294920 | tf_op jit(solution)/shard_map/ppermute | solution.py:529
  40.6 1.6 %collective-permute-start.15 = (bf16[128,384]{1,0:T(8,128)(2,1)S(1)}, bf16[128,384]{1,0:T(8,128)(2,1)S(1)}, u32[]{:S(2)}, u32[]{:S(2)}) collective-permute-start(bf16[128,384]{1,0:T(8,128)(2,1)S(1)} %get-tuple-element.57), channel_id=1, source_target_pairs={{0,8},{8,0},{16,24},{24,16},{1,9},{9,1},{17,25},{25,17},{2,10},{10... | collective-permute-start | bytes 294920 | tf_op jit(solution)/shard_map/ppermute | solution.py:529
  42.2 0.1 collective-permute-start.16
  42.3 3.4 %shard_map.90 = (bf16[196,1024]{1,0:T(8,128)(2,1)}, bf16[64,512]{1,0:T(8,128)(2,1)}) custom-call(s32[1,196]{1,0:T(1,128)S(1)} %copy-done.3, s32[1,192]{1,0:T(1,128)S(1)} %copy-done.2, bf16[1024,1536]{1,0:T(8,128)(2,1)S(1)} %copy-done, bf16[832,128]{1,0:T(8,128)(2,1)S(1)} %collective-permute-done.7.refs_0_.refs_1_, ...), custom_call_target="tpu_custom_call" | custom-call | tf_op jit(solution)/shard_map/pallas_call | solution.py:244
  45.7 1.2 %collective-permute-done.14.refs_1_ = bf16[128,384]{1,0:T(8,128)(2,1)S(1)} collective-permute-done((bf16[128,384]{1,0:T(8,128)(2,1)S(1)}, bf16[128,384]{1,0:T(8,128)(2,1)S(1)}, u32[]{:S(2)}, u32[]{:S(2)}) %collective-permute-start.14) | collective-permute-done | bytes 98336 | tf_op jit(solution)/shard_map/ppermute | solution.py:529
  46.9 2.3 %collective-permute-done.16.refs_3_ = bf16[128,384]{1,0:T(8,128)(2,1)S(1)} collective-permute-done((bf16[128,384]{1,0:T(8,128)(2,1)S(1)}, bf16[128,384]{1,0:T(8,128)(2,1)S(1)}, u32[]{:S(2)}, u32[]{:S(2)}) %collective-permute-start.16) | collective-permute-done | bytes 98336 | tf_op jit(solution)/shard_map/ppermute | solution.py:529
  49.1 0.7 %shard_map.93 = f32[128,384]{1,0:T(8,128)} custom-call(bf16[128,384]{1,0:T(8,128)(2,1)S(1)} %get-tuple-element.55.refs_0_, bf16[128,384]{1,0:T(8,128)(2,1)S(1)} %collective-permute-done.14.refs_1_, bf16[128,384]{1,0:T(8,128)(2,1)S(1)} %collective-permute-done.15.refs_2_, bf16[128,384]{1,0:T(8,128)(2,1)S(1)} %collective-permute-done.16.refs_3_), custom_call_target="tpu_custom_call" | custom-call | tf_op jit(solution)/shard_map/pallas_call | solution.py:244
  (19 shorter events, 0.0 us)
Async XLA Ops:
  4.6 8.3 %collective-permute-start = (bf16[528,128]{1,0:T(8,128)(2,1)}, bf16[528,128]{1,0:T(8,128)(2,1)S(1)}, u32[]{:S(2)}, u32[]{:S(2)}) collective-permute-start(bf16[528,128]{1,0:T(8,128)(2,1)} %get-tuple-element.34), channel_id=1, source_target_pairs={{0,6},{1,7},{2,4},{3,5},{4,2},{5,3},{6,0},{7,1},{8,14},{9,15},{10,... | collective-permute-start | bytes 405512 | tf_op jit(solution)/shard_map/ppermute | solution.py:529
  8.5 7.2 %collective-permute-start.1 = (bf16[528,128]{1,0:T(8,128)(2,1)}, bf16[528,128]{1,0:T(8,128)(2,1)S(1)}, u32[]{:S(2)}, u32[]{:S(2)}) collective-permute-start(bf16[528,128]{1,0:T(8,128)(2,1)} %get-tuple-element.35), channel_id=1, source_target_pairs={{0,7},{1,6},{2,5},{3,4},{4,3},{5,2},{6,1},{7,0},{8,15},{9,14},{10,... | collective-permute-start | bytes 405512 | tf_op jit(solution)/shard_map/ppermute | solution.py:529
  8.5 9.6 %collective-permute-start.2 = (bf16[528,128]{1,0:T(8,128)(2,1)}, bf16[528,128]{1,0:T(8,128)(2,1)S(1)}, u32[]{:S(2)}, u32[]{:S(2)}) collective-permute-start(bf16[528,128]{1,0:T(8,128)(2,1)} %get-tuple-element.36), channel_id=1, source_target_pairs={{0,4},{1,5},{2,6},{3,7},{4,0},{5,1},{6,2},{7,3},{8,12},{9,13},{10,... | collective-permute-start | bytes 405512 | tf_op jit(solution)/shard_map/ppermute | solution.py:529
  9.7 9.6 %collective-permute-start.3 = (bf16[528,128]{1,0:T(8,128)(2,1)}, bf16[528,128]{1,0:T(8,128)(2,1)S(1)}, u32[]{:S(2)}, u32[]{:S(2)}) collective-permute-start(bf16[528,128]{1,0:T(8,128)(2,1)} %get-tuple-element.37), channel_id=1, source_target_pairs={{0,2},{1,3},{2,0},{3,1},{4,6},{5,7},{6,4},{7,5},{8,10},{9,11},{10,... | collective-permute-start | bytes 405512 | tf_op jit(solution)/shard_map/ppermute | solution.py:529
  11.2 9.8 %collective-permute-start.4 = (bf16[528,128]{1,0:T(8,128)(2,1)}, bf16[528,128]{1,0:T(8,128)(2,1)S(1)}, u32[]{:S(2)}, u32[]{:S(2)}) collective-permute-start(bf16[528,128]{1,0:T(8,128)(2,1)} %get-tuple-element.40), channel_id=1, source_target_pairs={{0,5},{1,4},{2,7},{3,6},{4,1},{5,0},{6,3},{7,2},{8,13},{9,12},{10,... | collective-permute-start | bytes 405512 | tf_op jit(solution)/shard_map/ppermute | solution.py:529
  12.9 8.1 %collective-permute-start.5 = (bf16[528,128]{1,0:T(8,128)(2,1)}, bf16[528,128]{1,0:T(8,128)(2,1)S(1)}, u32[]{:S(2)}, u32[]{:S(2)}) collective-permute-start(bf16[528,128]{1,0:T(8,128)(2,1)} %get-tuple-element.41), channel_id=1, source_target_pairs={{0,3},{1,2},{2,1},{3,0},{4,7},{5,6},{6,5},{7,4},{8,11},{9,10},{10,... | collective-permute-start | bytes 405512 | tf_op jit(solution)/shard_map/ppermute | solution.py:529
  15.8 5.2 %collective-permute-start.6 = (bf16[528,128]{1,0:T(8,128)(2,1)}, bf16[528,128]{1,0:T(8,128)(2,1)S(1)}, u32[]{:S(2)}, u32[]{:S(2)}) collective-permute-start(bf16[528,128]{1,0:T(8,128)(2,1)} %get-tuple-element.42), channel_id=1, source_target_pairs={{0,1},{1,0},{2,3},{3,2},{4,5},{5,4},{6,7},{7,6},{8,9},{9,8},{10,11... | collective-permute-start | bytes 405512 | tf_op jit(solution)/shard_map/ppermute | solution.py:529
  19.3 0.9 %copy-start.1 = (bf16[528,128]{1,0:T(8,128)(2,1)S(1)}, bf16[528,128]{1,0:T(8,128)(2,1)}, u32[]{:S(2)}) copy-start(bf16[528,128]{1,0:T(8,128)(2,1)} %get-tuple-element.33.refs_0_) | copy-start | bytes 405508
  20.7 21.6 %copy-start = (bf16[1024,1536]{1,0:T(8,128)(2,1)S(1)}, bf16[1024,1536]{1,0:T(8,128)(2,1)}, u32[]{:S(2)}) copy-start(bf16[1024,1536]{1,0:T(8,128)(2,1)} %w_hbm.1) | copy-start | bytes 9437188
  20.8 21.6 %copy-start.2 = (s32[1,192]{1,0:T(1,128)S(1)}, s32[1,192]{1,0:T(1,128)}, u32[]{:S(2)}) copy-start(s32[1,192]{1,0:T(1,128)} %get-tuple-element.32.target_ref) | copy-start | bytes 2308
  20.8 21.5 %copy-start.3 = (s32[1,196]{1,0:T(1,128)S(1)}, s32[1,196]{1,0:T(1,128)}, u32[]{:S(2)}) copy-start(s32[1,196]{1,0:T(1,128)} %get-tuple-element.31.segment_ref) | copy-start | bytes 2356
  22.8 7.4 %collective-permute-start.9 = (bf16[832,128]{1,0:T(8,128)(2,1)S(1)}, bf16[832,128]{1,0:T(8,128)(2,1)S(1)}, u32[]{:S(2)}, u32[]{:S(2)}) collective-permute-start(bf16[832,128]{1,0:T(8,128)(2,1)S(1)} %get-tuple-element.44), channel_id=1, source_target_pairs={{0,4},{1,5},{2,6},{3,7},{4,0},{5,1},{6,2},{7,3},{8,12},{9,13},{10,... | collective-permute-start | bytes 638984 | tf_op jit(solution)/shard_map/ppermute | solution.py:529
  24.6 8.1 %collective-permute-start.11 = (bf16[832,128]{1,0:T(8,128)(2,1)S(1)}, bf16[832,128]{1,0:T(8,128)(2,1)S(1)}, u32[]{:S(2)}, u32[]{:S(2)}) collective-permute-start(bf16[832,128]{1,0:T(8,128)(2,1)S(1)} %get-tuple-element.47), channel_id=1, source_target_pairs={{0,2},{1,3},{2,0},{3,1},{4,6},{5,7},{6,4},{7,5},{8,10},{9,11},{10,... | collective-permute-start | bytes 638984 | tf_op jit(solution)/shard_map/ppermute | solution.py:529
  26.1 9.9 %collective-permute-start.7 = (bf16[832,128]{1,0:T(8,128)(2,1)S(1)}, bf16[832,128]{1,0:T(8,128)(2,1)S(1)}, u32[]{:S(2)}, u32[]{:S(2)}) collective-permute-start(bf16[832,128]{1,0:T(8,128)(2,1)S(1)} %get-tuple-element.43), channel_id=1, source_target_pairs={{0,6},{1,7},{2,4},{3,5},{4,2},{5,3},{6,0},{7,1},{8,14},{9,15},{10,... | collective-permute-start | bytes 638984 | tf_op jit(solution)/shard_map/ppermute | solution.py:529
  26.4 9.6 %collective-permute-start.13 = (bf16[832,128]{1,0:T(8,128)(2,1)S(1)}, bf16[832,128]{1,0:T(8,128)(2,1)S(1)}, u32[]{:S(2)}, u32[]{:S(2)}) collective-permute-start(bf16[832,128]{1,0:T(8,128)(2,1)S(1)} %get-tuple-element.48.refs_6_.refs_0_), channel_id=1, source_target_pairs={{0,1},{1,0},{2,3},{3,2},{4,5},{5,4},{6,7},{7,6},{8,9},{9,8},{10,11... | collective-permute-start | bytes 638984 | tf_op jit(solution)/shard_map/ppermute | solution.py:529
  30.2 5.8 %collective-permute-start.10 = (bf16[832,128]{1,0:T(8,128)(2,1)S(1)}, bf16[832,128]{1,0:T(8,128)(2,1)S(1)}, u32[]{:S(2)}, u32[]{:S(2)}) collective-permute-start(bf16[832,128]{1,0:T(8,128)(2,1)S(1)} %shard_map.89.refs_2_), channel_id=1, source_target_pairs={{0,1},{1,0},{2,3},{3,2},{4,5},{5,4},{6,7},{7,6},{8,9},{9,8},{10,11... | collective-permute-start | bytes 638984 | tf_op jit(solution)/shard_map/ppermute | solution.py:529
  32.8 3.2 %collective-permute-start.12 = (bf16[832,128]{1,0:T(8,128)(2,1)S(1)}, bf16[832,128]{1,0:T(8,128)(2,1)S(1)}, u32[]{:S(2)}, u32[]{:S(2)}) collective-permute-start(bf16[832,128]{1,0:T(8,128)(2,1)S(1)} %collective-permute-done.11.refs_4_.refs_3_), channel_id=1, source_target_pairs={{0,1},{1,0},{2,3},{3,2},{4,5},{5,4},{6,7},{7,6},{8,9},{9,8},{10,11... | collective-permute-start | bytes 638984 | tf_op jit(solution)/shard_map/ppermute | solution.py:529
  36.0 1.5 %collective-permute-start.8 = (bf16[832,128]{1,0:T(8,128)(2,1)S(1)}, bf16[832,128]{1,0:T(8,128)(2,1)S(1)}, u32[]{:S(2)}, u32[]{:S(2)}) collective-permute-start(bf16[832,128]{1,0:T(8,128)(2,1)S(1)} %collective-permute-done.7.refs_0_.refs_1_), channel_id=1, source_target_pairs={{0,1},{1,0},{2,3},{3,2},{4,5},{5,4},{6,7},{7,6},{8,9},{9,8},{10,11... | collective-permute-start | bytes 638984 | tf_op jit(solution)/shard_map/ppermute | solution.py:529
  37.9 9.0 %collective-permute-start.14 = (bf16[128,384]{1,0:T(8,128)(2,1)S(1)}, bf16[128,384]{1,0:T(8,128)(2,1)S(1)}, u32[]{:S(2)}, u32[]{:S(2)}) collective-permute-start(bf16[128,384]{1,0:T(8,128)(2,1)S(1)} %get-tuple-element.56), channel_id=1, source_target_pairs={{0,16},{8,24},{16,0},{24,8},{1,17},{9,25},{17,1},{25,9},{2,18},{10... | collective-permute-start | bytes 294920 | tf_op jit(solution)/shard_map/ppermute | solution.py:529
  40.6 6.3 %collective-permute-start.15 = (bf16[128,384]{1,0:T(8,128)(2,1)S(1)}, bf16[128,384]{1,0:T(8,128)(2,1)S(1)}, u32[]{:S(2)}, u32[]{:S(2)}) collective-permute-start(bf16[128,384]{1,0:T(8,128)(2,1)S(1)} %get-tuple-element.57), channel_id=1, source_target_pairs={{0,8},{8,0},{16,24},{24,16},{1,9},{9,1},{17,25},{25,17},{2,10},{10... | collective-permute-start | bytes 294920 | tf_op jit(solution)/shard_map/ppermute | solution.py:529
  42.2 6.9 %collective-permute-start.16 = (bf16[128,384]{1,0:T(8,128)(2,1)S(1)}, bf16[128,384]{1,0:T(8,128)(2,1)S(1)}, u32[]{:S(2)}, u32[]{:S(2)}) collective-permute-start(bf16[128,384]{1,0:T(8,128)(2,1)S(1)} %get-tuple-element.58), channel_id=1, source_target_pairs={{0,24},{8,16},{16,8},{24,0},{1,25},{9,17},{17,9},{25,1},{2,26},{10... | collective-permute-start | bytes 294920 | tf_op jit(solution)/shard_map/ppermute | solution.py:529
